TPU v7x, 32 devices: a whole 2x2x4 slice. The times are simulated.
32 devices in a mesh: row: 8 (over y, x, core), col: 4 (over z).
Axes of the slice: x: 2, y: 2, z: 4, core: 2. Of those that a mesh axis runs over, the one named last changes fastest.
Arguments:
- latent: bfloat16 [672, 672, 256], P('row', 'col'), may hold values from -6 to 6
- cotangent: bfloat16 [672, 672, 256], P('row', 'col'), may hold values from -6 to 6
- factor_one: bfloat16 [672, 672], P('row'), as said below
- factor_two: bfloat16 [672, 672], P('col'), as said below
Outputs:
- grad_latent: bfloat16 [672, 672, 256], P('row', 'col')
- grad_factor_one: float32 [672, 672], P('row', 'col')
- grad_factor_two: float32 [672, 672], P('row', 'col')
Inputs may be any that keep to these rules, and one draw needn't show every extreme that they name: `factor_one`: lower triangular, with diagonal entries between 0.5 and 1.5. `factor_two`: lower triangular, with diagonal entries between 0.5 and 1.5.
All inputs are finite; a program needn't handle non-finite values.
Results may differ from a plain program's by a relative error of at most 0.0049.
Values may be sent and summed in bfloat16 or wider, within the bound.
No kernel may reach another device: no remote copies, remote signals or barrier semaphores. Data moves between devices by JAX's collectives and lax.ppermute only.
A program may use at most 128 MiB of HBM per device.

v0:
```python
import jax
import jax.numpy as jnp
from jax import lax
from jax.sharding import PartitionSpec as P


def contract_first(left, right):
    return lax.dot_general(
        left, right, (((0,), (0,)), ((), ())), preferred_element_type=jnp.float32
    )


def contract_last(left, right):
    return lax.dot_general(
        left, right, (((1,), (1,)), ((), ())), preferred_element_type=jnp.float32
    )


def reduce_grad(partial_value, depth):
    portion = lax.psum_scatter(partial_value, "row", scatter_dimension=0, tiled=True)
    portion = lax.psum_scatter(portion, "col", scatter_dimension=1, tiled=True)
    span_rows, span_cols = portion.shape
    row_ids = lax.axis_index("row") * span_rows + lax.broadcasted_iota(
        jnp.int32, (span_rows, span_cols), 0
    )
    col_ids = lax.axis_index("col") * span_cols + lax.broadcasted_iota(
        jnp.int32, (span_rows, span_cols), 1
    )
    return jnp.where(row_ids >= col_ids, portion / depth, 0.0)


def on_device(latent, cotangent, factor_one, factor_two):
    rows_one, rows_two, depth = latent.shape
    latent_flat = jnp.transpose(latent, (1, 0, 2)).reshape(rows_two, rows_one * depth)
    latent_two = lax.all_to_all(latent_flat, "col", split_axis=1, concat_axis=0, tiled=True)
    cotan_flat = cotangent.reshape(rows_one, rows_two * depth)
    cotan_one = lax.all_to_all(cotan_flat, "row", split_axis=1, concat_axis=0, tiled=True)
    full_one = lax.all_gather(factor_one, "row", axis=0, tiled=True)
    full_two = lax.all_gather(factor_two, "col", axis=0, tiled=True)
    mixed_two = jnp.dot(full_two, latent_two, preferred_element_type=jnp.float32)
    pulled_one = contract_first(full_one, cotan_one)
    mixed_two = mixed_two.astype(jnp.bfloat16)
    pulled_one = pulled_one.astype(jnp.bfloat16)
    mixed_back = lax.all_to_all(mixed_two, "col", split_axis=0, concat_axis=1, tiled=True)
    mixed_block = (
        mixed_back.reshape(rows_two, rows_one, depth)
        .transpose(1, 0, 2)
        .reshape(rows_one, rows_two * depth)
    )
    mixed_one = lax.all_to_all(mixed_block, "row", split_axis=1, concat_axis=0, tiled=True)
    pulled_back = lax.all_to_all(pulled_one, "row", split_axis=0, concat_axis=1, tiled=True)
    pulled_block = (
        pulled_back.reshape(rows_one, rows_two, depth)
        .transpose(1, 0, 2)
        .reshape(rows_two, rows_one * depth)
    )
    pulled_two = lax.all_to_all(pulled_block, "col", split_axis=1, concat_axis=0, tiled=True)
    grad_factor_one = reduce_grad(contract_last(cotan_one, mixed_one), depth)
    grad_factor_two = reduce_grad(contract_last(pulled_two, latent_two), depth)
    result_two = contract_first(full_two, pulled_two)
    result_two = result_two.astype(jnp.bfloat16)
    result_back = lax.all_to_all(result_two, "col", split_axis=0, concat_axis=1, tiled=True)
    grad_latent = result_back.reshape(rows_two, rows_one, depth).transpose(1, 0, 2)
    return (grad_latent, grad_factor_one, grad_factor_two)


def solution(mesh):
    placed = (P("row", "col", None), P("row", "col", None), P("row", None), P("col", None))
    return jax.shard_map(
        on_device,
        mesh=mesh,
        in_specs=placed,
        out_specs=(P("row", "col", None), P("row", "col"), P("row", "col")),
        check_vma=False,
    )
```

profile of v0, /device:TPU:0, one launch (start us, length us, event | category | flops | bytes accessed | tf_op | source)
XLA Modules:
  0.0 993.6 jit_solution(9086830693234594142)
XLA Ops:
  7.2 13.3 %all_to_all.92 = bf16[84,8,5376]{2,1,0:T(8,128)(2,1)} reshape(bf16[84,168,256]{2,1,0:T(8,128)(2,1)} %param.5) | data formatting | bytes 14450688 | tf_op jit(solution)/shard_map/all_to_all | solution.py:37
  20.5 7.4 copy.20
  27.9 5.2 all-to-all-start
  33.0 7.6 copy.25
  40.6 12.1 %all_to_all.106 = bf16[168,4,5376]{2,1,0:T(4,128)(2,1)} reshape(bf16[168,84,256]{2,1,0:T(8,128)(2,1)} %copy.25) | data formatting | bytes 14450688 | tf_op jit(solution)/shard_map/all_to_all | solution.py:35
  52.7 6.7 copy.26
  59.4 0.0 copy-start.1
  59.4 59.3 %all-to-all-done = bf16[84,8,5376]{2,0,1:T(8,128)(2,1)} async-done(((bf16[84,8,5376]{2,0,1:T(8,128)(2,1)}), bf16[84,8,5376]{2,0,1:T(8,128)(2,1)}, u32[]{:S(2)}, u32[]{:S(2)}) %all-to-all-start) | async-done | bytes 7225376 | tf_op jit(solution)/shard_map/all_to_all | solution.py:37
  118.7 5.7 all-to-all-start.4
  124.4 0.0 copy-done.1
  124.4 10.3 %all-gather = bf16[8,84,672]{2,1,0:T(8,128)(2,1)S(1)} all-gather(bf16[1,84,672]{2,1,0:T(8,128)(2,1)S(1)} %bitcast.44), channel_id=1, replica_groups=mesh['row'=8,'col'=4] {'row'}, dimensions={0}, use_global_device_ids=true | all-gather | bytes 1016064 | tf_op jit(solution)/shard_map/all_gather | solution.py:38
  134.7 0.4 reshape.51
  135.1 7.0 all_to_all.95
  142.1 11.6 %convolution_convert_fusion.2 = bf16[672,5376]{1,0:T(8,128)(2,1)} fusion(bf16[672,672]{1,0:T(8,128)(2,1)S(1)} %reshape.51, bf16[672,5376]{1,0:T(8,128)(2,1)} %all_to_all.95), kind=kOutput, calls=%fused_computation.2 | convolution fusion | flops 4859043840 | bytes 15353856 | tf_op jit(solution)/shard_map/dot_general | solution.py:8
  153.7 7.0 all_to_all.96
  160.7 0.0 copy-start
  160.7 119.6 %all-to-all-done.4 = bf16[168,4,5376]{2,0,1:T(8,128)(2,1)} async-done(((bf16[168,4,5376]{2,0,1:T(8,128)(2,1)}), bf16[168,4,5376]{2,0,1:T(8,128)(2,1)}, u32[]{:S(2)}, u32[]{:S(2)}) %all-to-all-start.4) | async-done | bytes 7225376 | tf_op jit(solution)/shard_map/all_to_all | solution.py:35
  280.3 5.0 all-to-all-start.1
  285.3 0.0 copy-done
  285.3 21.9 %all_gather.7 = bf16[672,672]{1,0:T(8,128)(2,1)S(1)} all-gather(bf16[168,672]{1,0:T(8,128)(2,1)S(1)} %copy-done), channel_id=1, replica_groups=mesh['row'=8,'col'=4] {'col'}, dimensions={0}, use_global_device_ids=true | all-gather | bytes 1128960 | tf_op jit(solution)/shard_map/all_gather | solution.py:39
  307.2 10.8 %convolution_convert_fusion = bf16[672,5376]{1,0:T(8,128)(2,1)} fusion(bf16[672,672]{1,0:T(8,128)(2,1)S(1)} %all_gather.7, bf16[672,5376]{1,0:T(8,128)(2,1)} %bitcast.12), kind=kOutput, calls=%fused_computation | convolution fusion | flops 4859043840 | bytes 15353856 | tf_op jit(solution)/shard_map/dot_general | solution.py:40
  318.0 52.6 %all-to-all-done.1 = bf16[8,84,5376]{2,1,0:T(8,128)(2,1)} async-done(((bf16[8,84,5376]{2,1,0:T(8,128)(2,1)}), bf16[8,84,5376]{2,1,0:T(8,128)(2,1)}, u32[]{:S(2)}, u32[]{:S(2)}) %all-to-all-start.1) | async-done | bytes 7225376 | tf_op jit(solution)/shard_map/all_to_all | solution.py:51
  370.7 5.4 all-to-all-start.5
  376.1 7.3 copy.21
  383.4 13.5 %reshape.47 = bf16[84,168,256]{2,1,0:T(8,128)(2,1)} reshape(bf16[84,8,5376]{2,1,0:T(8,128)(2,1)} %copy.21) | data formatting | bytes 14450688 | tf_op jit(solution)/shard_map/reshape | solution.py:53
  397.0 7.5 copy.22
  404.5 12.2 %all_to_all.99 = bf16[168,4,5376]{2,1,0:T(4,128)(2,1)} reshape(bf16[168,84,256]{2,1,0:T(8,128)(2,1)} %copy.22) | data formatting | bytes 14450688 | tf_op jit(solution)/shard_map/all_to_all | solution.py:57
  416.7 6.7 copy.23
  423.4 108.2 %all-to-all-done.5 = bf16[4,168,5376]{2,1,0:T(8,128)(2,1)} async-done(((bf16[4,168,5376]{2,1,0:T(8,128)(2,1)}), bf16[4,168,5376]{2,1,0:T(8,128)(2,1)}, u32[]{:S(2)}, u32[]{:S(2)}) %all-to-all-start.5) | async-done | bytes 7225376 | tf_op jit(solution)/shard_map/all_to_all | solution.py:44
  531.7 5.6 all-to-all-start.2
  537.3 8.8 copy.27
  546.1 12.4 %reshape.49 = bf16[168,84,256]{2,1,0:T(8,128)(2,1)} reshape(bf16[168,4,5376]{2,1,0:T(4,128)(2,1)} %copy.27) | data formatting | bytes 14450688 | tf_op jit(solution)/shard_map/reshape | solution.py:46
  558.5 7.6 copy.28
  566.0 13.3 %all_to_all.113 = bf16[84,8,5376]{2,1,0:T(8,128)(2,1)} reshape(bf16[84,168,256]{2,1,0:T(8,128)(2,1)} %copy.28) | data formatting | bytes 14450688 | tf_op jit(solution)/shard_map/all_to_all | solution.py:50
  579.3 7.4 copy.29
  586.7 108.2 %all-to-all-done.2 = bf16[168,4,5376]{2,0,1:T(8,128)(2,1)} async-done(((bf16[168,4,5376]{2,0,1:T(8,128)(2,1)}), bf16[168,4,5376]{2,0,1:T(8,128)(2,1)}, u32[]{:S(2)}, u32[]{:S(2)}) %all-to-all-start.2) | async-done | bytes 7225376 | tf_op jit(solution)/shard_map/all_to_all | solution.py:57
  694.9 5.0 all-to-all-start.6
  699.9 11.6 %convolution_convert_fusion.1 = bf16[5376,672]{0,1:T(8,128)(2,1)} fusion(bf16[672,5376]{1,0:T(8,128)(2,1)} %bitcast.5, bf16[672,672]{1,0:T(8,128)(2,1)S(1)} %all_gather.7), kind=kOutput, calls=%fused_computation.1 | convolution fusion | flops 4859043840 | bytes 15353856 | tf_op jit(solution)/shard_map/dot_general | solution.py:8
  711.5 73.8 %all-to-all-done.6 = bf16[84,8,5376]{2,0,1:T(8,128)(2,1)} async-done(((bf16[84,8,5376]{2,0,1:T(8,128)(2,1)}), bf16[84,8,5376]{2,0,1:T(8,128)(2,1)}, u32[]{:S(2)}, u32[]{:S(2)}) %all-to-all-start.6) | async-done | bytes 7225376 | tf_op jit(solution)/shard_map/all_to_all | solution.py:50
  785.3 5.5 all-to-all-start.3
  790.8 0.3 all-reduce.7.cloned.1.call-start
  791.1 11.2 %fusion = f32[672,672]{0,1:T(8,128)} fusion(bf16[672,5376]{1,0:T(8,128)(2,1)} %bitcast.5, bf16[672,5376]{1,0:T(8,128)(2,1)} %bitcast.12), kind=kOutput, calls=%fused_computation.10 | convolution fusion | flops 4855431168 | bytes 16257024 | tf_op jit(solution)/shard_map/dot_general | solution.py:14
  802.3 7.0 all_to_all.116
  809.3 0.0 copy-start.2
  809.3 11.2 %convolution_bitcast_fusion = f32[672,672]{0,1:T(8,128)} fusion(bf16[672,5376]{1,0:T(8,128)(2,1)} %all_to_all.116, bf16[672,5376]{1,0:T(8,128)(2,1)} %all_to_all.95), kind=kOutput, calls=%fused_computation.3 | convolution fusion | flops 4855431168 | bytes 16257024 | tf_op jit(solution)/shard_map/dot_general | solution.py:14
  820.5 0.0 all-reduce.7.cloned.1.call-update
  820.5 0.0 reduce-scatter.11.cloned.1.call-start
  820.5 0.0 copy-done.2
  820.5 0.6 dynamic-slice
  821.8 79.3 %all-reduce.7.cloned.1.call-done = (f32[672,672]{0,1:T(8,128)}, f32[672,672]{0,1:T(8,128)}) async-done(((f32[672,672]{0,1:T(8,128)}, f32[672,672]{0,1:T(8,128)}), (f32[672,672]{0,1:T(8,128)}, f32[672,672]{0,1:T(8,128)})) %all-reduce.7.cloned.1.call-update) | async-done | bytes 3612688
  901.1 2.0 constant_dynamic-slice_fusion
  903.1 0.0 reduce-scatter.11.cloned.1.call-update
  903.1 0.0 reduce-scatter.9.cloned.1.call-start
  903.2 2.0 constant_dynamic-slice_fusion.1
  905.2 0.0 reduce-scatter.9.cloned.1.call-update
  905.2 19.4 %reduce-scatter.11.cloned.1.call-done = f32[84,168]{0,1:T(8,128)} async-done(((f32[84,672]{0,1:T(8,128)}), f32[84,168]{0,1:T(8,128)}) %reduce-scatter.11.cloned.1.call-update) | async-done | bytes 56464
  924.6 21.4 %reduce-scatter.9.cloned.1.call-done = f32[84,168]{0,1:T(8,128)} async-done(((f32[84,672]{0,1:T(8,128)}), f32[84,168]{0,1:T(8,128)}) %reduce-scatter.9.cloned.1.call-update) | async-done | bytes 56464
  946.0 1.7 compare_select_fusion
  947.7 10.0 %all-to-all-done.3 = bf16[4,168,5376]{2,1,0:T(8,128)(2,1)} async-done(((bf16[4,168,5376]{2,1,0:T(8,128)(2,1)}), bf16[4,168,5376]{2,1,0:T(8,128)(2,1)}, u32[]{:S(2)}, u32[]{:S(2)}) %all-to-all-start.3) | async-done | bytes 7225376 | tf_op jit(solution)/shard_map/all_to_all | solution.py:62
  957.8 8.8 copy.24
  966.6 12.4 %reshape.48 = bf16[168,84,256]{2,1,0:T(8,128)(2,1)} reshape(bf16[168,4,5376]{2,1,0:T(4,128)(2,1)} %copy.24) | data formatting | bytes 14450688 | tf_op jit(solution)/shard_map/reshape | solution.py:63
  979.0 7.7 copy.31
  (2 shorter events, 0.0 us)
Async XLA Ops:
  27.9 90.8 %all-to-all-start = ((bf16[84,8,5376]{2,0,1:T(8,128)(2,1)}), bf16[84,8,5376]{2,0,1:T(8,128)(2,1)}, u32[]{:S(2)}, u32[]{:S(2)}) async-start(bf16[84,8,5376]{2,0,1:T(8,128)(2,1)} %copy.20), calls=%async_computation | async-start | bytes 15138816 | tf_op jit(solution)/shard_map/all_to_all | solution.py:37
  59.4 65.0 %copy-start.1 = (bf16[84,672]{1,0:T(8,128)(2,1)S(1)}, bf16[84,672]{1,0:T(8,128)(2,1)}, u32[]{:S(2)}) copy-start(bf16[84,672]{1,0:T(8,128)(2,1)} %param.6) | copy-start | bytes 338692
  118.7 161.6 %all-to-all-start.4 = ((bf16[168,4,5376]{2,0,1:T(8,128)(2,1)}), bf16[168,4,5376]{2,0,1:T(8,128)(2,1)}, u32[]{:S(2)}, u32[]{:S(2)}) async-start(bf16[168,4,5376]{2,0,1:T(8,128)(2,1)} %copy.26), calls=%async_computation.4 | async-start | bytes 14450688 | tf_op jit(solution)/shard_map/all_to_all | solution.py:35
  160.7 124.6 %copy-start = (bf16[168,672]{1,0:T(8,128)(2,1)S(1)}, bf16[168,672]{1,0:T(8,128)(2,1)}, u32[]{:S(2)}) copy-start(bf16[168,672]{1,0:T(8,128)(2,1)} %param.7) | copy-start | bytes 677380
  280.3 90.4 %all-to-all-start.1 = ((bf16[8,84,5376]{2,1,0:T(8,128)(2,1)}), bf16[8,84,5376]{2,1,0:T(8,128)(2,1)}, u32[]{:S(2)}, u32[]{:S(2)}) async-start(bf16[8,84,5376]{2,1,0:T(8,128)(2,1)} %all_to_all.96), calls=%async_computation.1 | async-start | bytes 15138816 | tf_op jit(solution)/shard_map/all_to_all | solution.py:51
  370.7 161.0 %all-to-all-start.5 = ((bf16[4,168,5376]{2,1,0:T(8,128)(2,1)}), bf16[4,168,5376]{2,1,0:T(8,128)(2,1)}, u32[]{:S(2)}, u32[]{:S(2)}) async-start(bf16[4,168,5376]{2,1,0:T(8,128)(2,1)} %bitcast.43), calls=%async_computation.5 | async-start | bytes 14450688 | tf_op jit(solution)/shard_map/all_to_all | solution.py:44
  531.7 163.3 %all-to-all-start.2 = ((bf16[168,4,5376]{2,0,1:T(8,128)(2,1)}), bf16[168,4,5376]{2,0,1:T(8,128)(2,1)}, u32[]{:S(2)}, u32[]{:S(2)}) async-start(bf16[168,4,5376]{2,0,1:T(8,128)(2,1)} %copy.23), calls=%async_computation.2 | async-start | bytes 14450688 | tf_op jit(solution)/shard_map/all_to_all | solution.py:57
  694.9 90.4 %all-to-all-start.6 = ((bf16[84,8,5376]{2,0,1:T(8,128)(2,1)}), bf16[84,8,5376]{2,0,1:T(8,128)(2,1)}, u32[]{:S(2)}, u32[]{:S(2)}) async-start(bf16[84,8,5376]{2,0,1:T(8,128)(2,1)} %copy.29), calls=%async_computation.6 | async-start | bytes 15138816 | tf_op jit(solution)/shard_map/all_to_all | solution.py:50
  785.3 172.4 %all-to-all-start.3 = ((bf16[4,168,5376]{2,1,0:T(8,128)(2,1)}), bf16[4,168,5376]{2,1,0:T(8,128)(2,1)}, u32[]{:S(2)}, u32[]{:S(2)}) async-start(bf16[4,168,5376]{2,1,0:T(8,128)(2,1)} %bitcast.42), calls=%async_computation.3 | async-start | bytes 14450688 | tf_op jit(solution)/shard_map/all_to_all | solution.py:62
  790.8 110.3 %all-reduce.7.cloned.1.call-start = ((), (), s32[]{:S(2)}) async-start(), calls=%async_computation.11 | async-start | bytes 8257536
  809.3 11.3 %copy-start.2 = (u32[32]{0:T(128)S(1)}, u32[32]{0:T(128)}, u32[]{:S(2)}) copy-start(u32[32]{0:T(128)} %constant.24) | copy-start | bytes 388
  820.5 104.1 %reduce-scatter.11.cloned.1.call-start = ((), (), s32[]{:S(2)}) async-start(), calls=%async_computation.10 | async-start | bytes 430080
  903.1 42.9 %reduce-scatter.9.cloned.1.call-start = ((), (), s32[]{:S(2)}) async-start(), calls=%async_computation.9 | async-start | bytes 430080
Sparse Core Ops, SparseCore 0:
  820.6 80.4 all-reduce.6
  904.0 20.6 reduce-scatter.10
  926.9 19.1 reduce-scatter.8
where the time goes:
time: 1000 us; the launch traced here: 994 us
  waiting for transfers between devices  652 us (65%)
  local copies, waits for them, and re-layouts  199 us (20%)
  matrix products  56.4 us (6%)
  starting transfers between devices  37.8 us (4%)
  blocking collectives  32.3 us (3%)
  between operations  14.9 us (1%)
    unnamed x6, waiting for transfers between devices  120 us
    all_to_all x1, waiting for transfers between devices, on_device(): lax.all_to_all(latent_flat, 'col', split_axis=1, concat_axis=0, tiled=True)  120 us
    all_to_all x1, waiting for transfers between devices, on_device(): lax.all_to_all(mixed_two, 'col', split_axis=0, concat_axis=1, tiled=True)  108 us
    all_to_all x1, waiting for transfers between devices, on_device(): lax.all_to_all(pulled_block, 'col', split_axis=1, concat_axis=0, tiled=True)  108 us
    all_to_all x1, waiting for transfers between devices, on_device(): lax.all_to_all(mixed_block, 'row', split_axis=1, concat_axis=0, tiled=True)  73.8 us
    all_to_all x1, waiting for transfers between devices, on_device(): lax.all_to_all(cotan_flat, 'row', split_axis=1, concat_axis=0, tiled=True)  59.3 us
    all_to_all x1, waiting for transfers between devices, on_device(): lax.all_to_all(pulled_one, 'row', split_axis=0, concat_axis=1, tiled=True)  52.6 us
    all_to_all x3, local copies, waits for them, and re-layouts, on_device(): lax.all_to_all(mixed_block, 'row', split_axis=1, concat_axis=0, tiled=True)  27.7 us
  transfers between devices with their start and end apart: 10, of which 10 were waited for; matrix products, arithmetic and copies ran while one was open for 15% of the time, Pallas kernels for 0%

commit v1 on v0

v1 whole, which is shorter than its diff:
```python
import functools

import jax
import jax.numpy as jnp
from jax import lax
from jax.experimental import pallas as pl
from jax.experimental.pallas import tpu as pltpu
from jax.sharding import PartitionSpec as P

LANES = 128
F32, BF16 = jnp.float32, jnp.bfloat16


def contract_first(left, right):
    return lax.dot_general(
        left, right, (((0,), (0,)), ((), ())), preferred_element_type=F32
    )


def contract_last(left, right):
    return lax.dot_general(
        left, right, (((1,), (1,)), ((), ())), preferred_element_type=F32
    )


def keep_lower(portion, depth):
    span_rows, span_cols = portion.shape
    row_ids = lax.axis_index("row") * span_rows + lax.broadcasted_iota(
        jnp.int32, (span_rows, span_cols), 0
    )
    col_ids = lax.axis_index("col") * span_cols + lax.broadcasted_iota(
        jnp.int32, (span_rows, span_cols), 1
    )
    return jnp.where(row_ids >= col_ids, portion / depth, 0.0)


def reduce_grad(partial_value, depth):
    portion = lax.psum_scatter(partial_value, "row", scatter_dimension=0, tiled=True)
    portion = lax.psum_scatter(portion, "col", scatter_dimension=1, tiled=True)
    return keep_lower(portion, depth)


def by_lines(latent, cotangent, factor_one, factor_two):
    rows_one, rows_two, depth = latent.shape
    latent_flat = jnp.transpose(latent, (1, 0, 2)).reshape(rows_two, rows_one * depth)
    latent_two = lax.all_to_all(latent_flat, "col", split_axis=1, concat_axis=0, tiled=True)
    cotan_flat = cotangent.reshape(rows_one, rows_two * depth)
    cotan_one = lax.all_to_all(cotan_flat, "row", split_axis=1, concat_axis=0, tiled=True)
    full_one = lax.all_gather(factor_one, "row", axis=0, tiled=True)
    full_two = lax.all_gather(factor_two, "col", axis=0, tiled=True)
    mixed_two = jnp.dot(full_two, latent_two, preferred_element_type=F32)
    pulled_one = contract_first(full_one, cotan_one)
    mixed_two = mixed_two.astype(BF16)
    pulled_one = pulled_one.astype(BF16)
    mixed_back = lax.all_to_all(mixed_two, "col", split_axis=0, concat_axis=1, tiled=True)
    mixed_block = (
        mixed_back.reshape(rows_two, rows_one, depth)
        .transpose(1, 0, 2)
        .reshape(rows_one, rows_two * depth)
    )
    mixed_one = lax.all_to_all(mixed_block, "row", split_axis=1, concat_axis=0, tiled=True)
    pulled_back = lax.all_to_all(pulled_one, "row", split_axis=0, concat_axis=1, tiled=True)
    pulled_block = (
        pulled_back.reshape(rows_one, rows_two, depth)
        .transpose(1, 0, 2)
        .reshape(rows_two, rows_one * depth)
    )
    pulled_two = lax.all_to_all(pulled_block, "col", split_axis=1, concat_axis=0, tiled=True)
    grad_factor_one = reduce_grad(contract_last(cotan_one, mixed_one), depth)
    grad_factor_two = reduce_grad(contract_last(pulled_two, latent_two), depth)
    result_two = contract_first(full_two, pulled_two)
    result_two = result_two.astype(BF16)
    result_back = lax.all_to_all(result_two, "col", split_axis=0, concat_axis=1, tiled=True)
    grad_latent = result_back.reshape(rows_two, rows_one, depth).transpose(1, 0, 2)
    return (grad_latent, grad_factor_one, grad_factor_two)


def dot(left, right):
    return jnp.dot(left, right, preferred_element_type=F32)


def dot_nt(left, right):
    return lax.dot_general(
        left, right, (((1,), (1,)), ((), ())), preferred_element_type=F32
    )


def whole(shape):
    return pl.BlockSpec(shape, lambda *_: (0,) * len(shape))


def params():
    return pltpu.CompilerParams(vmem_limit_bytes=48 * 1024 * 1024)


def cost(flops, arrays):
    return pl.CostEstimate(flops=1, bytes_accessed=1, transcendentals=0)


def swap_matrix(fold):
    size = fold * LANES
    part = LANES // fold
    rows = lax.broadcasted_iota(jnp.int32, (size, size), 0)
    cols = lax.broadcasted_iota(jnp.int32, (size, size), 1)
    major, minor, lane = rows // LANES, (rows % LANES) // part, rows % part
    return (cols == minor * LANES + major * part + lane).astype(BF16)


def lanes_of(pieces):
    return jnp.concatenate(pieces, axis=-1)


def group(value, index):
    return value[:, index * LANES : (index + 1) * LANES]


HELD = pl.BlockSpec(memory_space=pl.ANY)


def pack(block, swap, tiles, span, rows):
    depth = block.shape[2]
    fold = swap.shape[0] // LANES
    first, count = tiles[0], tiles[1] - tiles[0]
    lo, hi = span
    wide_rows = hi - lo if lo % (hi - lo) == 0 else lo
    per = 3 if first % 3 == 0 and count % 3 == 0 else 1

    def kernel(x_ref, p_ref, o_ref):
        for t in range(per):
            for half in range(depth // LANES):
                at = half * LANES
                x = lanes_of([x_ref[t * fold + n, : hi - lo, at : at + LANES] for n in range(fold)])
                y = dot(x, p_ref[...]).astype(BF16)
                for n in range(fold):
                    o_ref[half * fold + n, t] = group(y, n)

    out = jax.ShapeDtypeStruct((rows, count, hi - lo, LANES), BF16)
    return pl.pallas_call(
        kernel,
        grid=(count // per,),
        in_specs=[
            pl.BlockSpec(
                (per * fold, wide_rows, depth), lambda t: (first // per + t, lo // wide_rows, 0)
            ),
            whole(swap.shape),
        ],
        out_specs=pl.BlockSpec((rows, per, hi - lo, LANES), lambda t: (0, t, 0, 0)),
        out_shape=out,
        compiler_params=params(),
        cost_estimate=cost(2 * out.size * swap.shape[0], (out, out)),
        name="pack",
    )(block, swap)


def unpack(part, swap, shape, where, before):
    rows, tiles, span, _ = part.shape
    fold = swap.shape[0] // LANES
    depth = shape[2]
    lo, hi, unit = where
    index = lo // unit
    extra = [] if before is None else [before]
    per = 3 if tiles % 3 == 0 else 1

    def kernel(x_ref, p_ref, *rest):
        o_ref = rest[-1]
        for t in range(per):
            for half in range(depth // LANES):
                x = lanes_of([x_ref[half * fold + n, t] for n in range(fold)])
                y = dot(x, p_ref[...]).astype(BF16)
                for n in range(fold):
                    at = half * LANES
                    o_ref[t * fold + n, :span, at : at + LANES] = group(y, n)

    return pl.pallas_call(
        kernel,
        grid=(tiles // per,),
        in_specs=[
            pl.BlockSpec((rows, per, span, LANES), lambda t: (0, t, 0, 0)),
            whole(swap.shape),
        ]
        + [HELD] * len(extra),
        out_specs=pl.BlockSpec((per * fold, unit, depth), lambda t: (t, index, 0)),
        out_shape=jax.ShapeDtypeStruct(shape, BF16),
        input_output_aliases={2: 0} if extra else {},
        compiler_params=params(),
        cost_estimate=cost(2 * part.size * swap.shape[0], (part, part)),
        name="unpack",
    )(part, swap, *extra)


def swapped(pieces):
    fold = len(pieces)
    width = LANES // fold
    return [
        lanes_of([x[:, n * width : (n + 1) * width] for x in pieces]) for n in range(fold)
    ]


def to_y(refs, base, fold):
    turned = [swapped([r[base + n].astype(F32) for n in range(fold)]) for r in refs]
    return jnp.concatenate([y[n] for n in range(fold) for y in turned], axis=0).astype(BF16)


def from_y(value, refs, base, fold):
    spans = [r.shape[1] for r in refs]
    total = sum(spans)
    start = 0
    for r, span in zip(refs, spans):
        y = swapped([value[n * total + start : n * total + start + span] for n in range(fold)])
        for n in range(fold):
            r[base + n] = y[n].astype(BF16)
        start += span


def raise_field(field, left, fold, spans):
    span_two = field.shape[0]
    order = left.shape[0]
    step = 2 * fold
    count = span_two // step

    def kernel(x_ref, l_ref, y_ref, *outs):
        y = lanes_of([to_y([x_ref], u * fold, fold) for u in range(2)])
        y_ref[0] = y
        v = dot(l_ref[...], y)
        for u in range(2):
            from_y(group(v, u), outs, u * fold, fold)

    shapes = [jax.ShapeDtypeStruct((span_two, span, LANES), BF16) for span in spans]
    y_shape = jax.ShapeDtypeStruct((count, order, 2 * LANES), BF16)
    return pl.pallas_call(
        kernel,
        grid=(count,),
        in_specs=[pl.BlockSpec((step,) + field.shape[1:], lambda t: (t, 0, 0)), whole(left.shape)],
        out_specs=[pl.BlockSpec((1, order, 2 * LANES), lambda t: (t, 0, 0))]
        + [pl.BlockSpec((step, span, LANES), lambda t: (t, 0, 0)) for span in spans],
        out_shape=[y_shape] + shapes,
        compiler_params=params(),
        cost_estimate=cost(2 * y_shape.size * order, (y_shape,) * 3),
        name="raise_field",
    )(field, left)


def finish(parts, left_t, fold):
    span_two = parts[0].shape[0]
    order = left_t.shape[0]
    step = 2 * fold
    count = span_two // step
    n = len(parts)

    def kernel(*refs):
        ins, l_ref, out_ref, y_ref = refs[:n], refs[n], refs[n + 1], refs[n + 2]
        w = lanes_of([to_y(ins, u * fold, fold) for u in range(2)])
        y_ref[0] = w
        v = dot(l_ref[...], w)
        for u in range(2):
            from_y(group(v, u), [out_ref], u * fold, fold)

    out = jax.ShapeDtypeStruct((span_two, order // fold, LANES), BF16)
    y_shape = jax.ShapeDtypeStruct((count, order, 2 * LANES), BF16)
    return pl.pallas_call(
        kernel,
        grid=(count,),
        in_specs=[pl.BlockSpec((step,) + p.shape[1:], lambda t: (t, 0, 0)) for p in parts]
        + [whole(left_t.shape)],
        out_specs=[
            pl.BlockSpec((step,) + out.shape[1:], lambda t: (t, 0, 0)),
            pl.BlockSpec((1, order, 2 * LANES), lambda t: (t, 0, 0)),
        ],
        out_shape=[out, y_shape],
        compiler_params=params(),
        cost_estimate=cost(2 * out.size * order, (out,) * 3),
        name="finish",
    )(*parts, left_t)


def match(w, z, first, before):
    count, order, width = w.shape
    extra = [] if before is None else [before]

    def kernel(w_ref, z_ref, *rest):
        g_ref = rest[-1]

        @pl.when(pl.program_id(0) == 0)
        def _():
            g_ref[...] = jnp.zeros_like(g_ref) if before is None else rest[0][...]

        g_ref[...] += dot_nt(w_ref[0], z_ref[0])

    g_shape = jax.ShapeDtypeStruct((order, order), F32)
    return pl.pallas_call(
        kernel,
        grid=(count,),
        in_specs=[
            pl.BlockSpec((1, order, width), lambda t: (t, 0, 0)),
            pl.BlockSpec((1, order, width), lambda t: (first + t, 0, 0)),
        ]
        + [whole(b.shape) for b in extra],
        out_specs=whole(g_shape.shape),
        out_shape=g_shape,
        compiler_params=params(),
        cost_estimate=cost(2 * w.size * order, (w, w)),
        name="match",
    )(w, z, *extra)


def wide(ref):
    return lanes_of([ref[t] for t in range(ref.shape[0])])


def tall(refs):
    return jnp.concatenate([wide(r) for r in refs], axis=0)


def gathered(slots, fields, mix, cuts, per):
    tiles, span_two, _ = slots[0].shape
    n, m = len(slots), len(fields)

    def kernel(*refs):
        ins, vs, m_ref = refs[:n], refs[n : n + m], refs[n + m]
        outs, g_ref = refs[n + m + 1 : -1], refs[-1]

        @pl.when(pl.program_id(0) == 0)
        def _():
            g_ref[...] = jnp.zeros_like(g_ref)

        v = tall(vs)
        total = None
        for d in range(n):
            c = wide(ins[d])
            g_ref[d] += dot_nt(c, v)
            term = dot(m_ref[d], c)
            total = term if total is None else total + term
        total = total.astype(BF16)
        for (lo, hi), out in zip(cuts, outs):
            for t in range(per):
                out[t] = group(total[lo:hi], t)

    def spec(span):
        return pl.BlockSpec((per, span, LANES), lambda t: (t, 0, 0))

    g_shape = jax.ShapeDtypeStruct((n, span_two, span_two), F32)
    return pl.pallas_call(
        kernel,
        grid=(tiles // per,),
        in_specs=[spec(span_two)] * n + [spec(f.shape[1]) for f in fields] + [whole(mix.shape)],
        out_specs=[spec(hi - lo) for lo, hi in cuts] + [whole(g_shape.shape)],
        out_shape=[jax.ShapeDtypeStruct((tiles, hi - lo, LANES), BF16) for lo, hi in cuts]
        + [g_shape],
        compiler_params=params(),
        cost_estimate=cost(4 * slots[0].size * n * span_two, tuple(slots) + tuple(slots[:2])),
        name="gathered",
    )(*slots, *fields, mix)


def pairs(field, others, per):
    tiles, span_two, _ = field.shape
    n = len(others)

    def kernel(*refs):
        c_ref, ins, g_ref = refs[0], refs[1 : n + 1], refs[-1]

        @pl.when(pl.program_id(0) == 0)
        def _():
            g_ref[...] = jnp.zeros_like(g_ref)

        g_ref[...] += dot_nt(wide(c_ref), tall(ins))

    def spec(span):
        return pl.BlockSpec((per, span, LANES), lambda t: (t, 0, 0))

    g_shape = jax.ShapeDtypeStruct((span_two, span_two), F32)
    return pl.pallas_call(
        kernel,
        grid=(tiles // per,),
        in_specs=[spec(span_two)] + [spec(o.shape[1]) for o in others],
        out_specs=whole(g_shape.shape),
        out_shape=g_shape,
        compiler_params=params(),
        cost_estimate=cost(2 * field.size * span_two, (field, field)),
        name="pairs",
    )(field, *others)


def shares(field, mix, cuts, per):
    tiles, span_two, _ = field.shape
    n = mix.shape[0]

    def kernel(c_ref, m_ref, *rest):
        outs = iter(rest)
        c = wide(c_ref)
        for d in range(n):
            total = dot(m_ref[d], c)
            for lo, hi in cuts:
                out = next(outs)
                for t in range(per):
                    out[t] = group(total[lo:hi], t).astype(out.dtype)

    def spec(span):
        return pl.BlockSpec((per, span, LANES), lambda t: (t, 0, 0))

    outs = [
        jax.ShapeDtypeStruct((tiles, hi - lo, LANES), BF16 if d else F32)
        for d in range(n)
        for lo, hi in cuts
    ]
    found = pl.pallas_call(
        kernel,
        grid=(tiles // per,),
        in_specs=[spec(span_two), whole(mix.shape)],
        out_specs=[spec(o.shape[1]) for o in outs],
        out_shape=outs,
        compiler_params=params(),
        cost_estimate=cost(2 * field.size * n * span_two, outs),
        name="shares",
    )(field, mix)
    return [found[d * len(cuts) : (d + 1) * len(cuts)] for d in range(n)]


def add(left, right):
    return (left.astype(F32) + right.astype(F32)).astype(BF16)


def after(value, *others):
    return lax.optimization_barrier((value,) + others)[0]


def by_tiles(rows, cols, latent, cotangent, factor_one, factor_two):
    span_one, span_two, depth = latent.shape
    order_one, order_two = factor_one.shape[1], factor_two.shape[1]
    fold = LANES * rows // depth
    tiles = span_one // fold
    near = 4 * tiles // 7
    part = near // 2
    groups = [(0, part), (part, near), (near, tiles)]
    unit = -(-span_two // 32) * 16
    cuts = [(0, unit), (unit, span_two)]
    half = unit // 2
    per = rows
    place = lax.axis_index("col")
    swap = swap_matrix(fold)
    last = cols - 1

    def exchange(value):
        return lax.all_to_all(value, "row", split_axis=0, concat_axis=0, tiled=True)

    def flat(value):
        return value.reshape((-1,) + value.shape[2:])

    def turn(value):
        return jnp.transpose(value, (1, 0, 2))

    def move(value, pairs_of):
        return lax.ppermute(value, "col", pairs_of)

    def down(value, step):
        return move(value, [(c, c - 1) for c in range(1, cols + 1 - step)])

    def up(value, step):
        return move(value, [(c, c + 1) for c in range(step - 1, cols - 1)])

    padded = jnp.pad(factor_two, ((0, 0), (last * span_two, 0)))
    beside = lax.dynamic_slice(padded, (0, place * span_two), (span_two, cols * span_two))
    mix_far = beside.T.reshape(cols, span_two, span_two)[::-1]
    mix_near = jnp.stack(
        [mix_far[0]]
        + [move(mix_far[d], [(c, c - d) for c in range(d, cols)]) for d in range(1, cols)]
    )

    every = (0, span_two)
    first = flat(exchange(pack(cotangent, swap, groups[0], every, rows)))
    firsts = [first, down(first, 1)]
    far_part = pack(cotangent, swap, groups[2], every, rows)
    far_part = flat(exchange(after(far_part, first, mix_near)))
    for step in range(2, cols):
        firsts.append(down(firsts[-1], step))
    own = shares(far_part, mix_far, cuts, per)
    sums = []
    for q in range(len(cuts)):
        held = after(own[last][q], *sums)
        sums.append(move(held, [(c, c - 1) for c in range(last, cols)]))
    z_first = pack(latent, swap, (0, tiles), cuts[0], rows)
    block = cuts[0][1] * LANES
    extra = -(-factor_one.size // block)
    full_one = jnp.pad(factor_one.reshape(-1), (0, extra * block - factor_one.size))
    full_one = full_one.reshape(1, extra, cuts[0][1], LANES)
    full_one = jnp.broadcast_to(full_one, (rows,) + full_one.shape[1:])
    z_first = jnp.concatenate([z_first, full_one], axis=1)
    z_first = exchange(after(z_first, far_part, firsts[1]))
    full_one = z_first[:, tiles:].reshape(rows, -1)[:, : factor_one.size]
    z_first = z_first[:, :tiles]
    second = pack(cotangent, swap, groups[1], every, rows)
    second = flat(exchange(after(second, z_first, firsts[min(2, last)], sums[0])))

    full_one = full_one.reshape(order_one, order_one)
    spot = lax.broadcasted_iota(jnp.int32, (order_one, order_one), 0)
    target = lax.broadcasted_iota(jnp.int32, spot.shape, 1)
    unit_of, tile = spot // (rows * tiles), spot % (rows * tiles)
    pick_latent = (target == tile * fold + unit_of).astype(BF16)
    index = 0
    for lo, hi in groups:
        inside = (tile >= rows * lo) & (tile < rows * hi)
        here = tile - rows * lo
        here = here // (hi - lo) * span_one + (lo + here % (hi - lo)) * fold + unit_of
        index = jnp.where(inside, here, index)
    pick_cotan = (target == index).astype(BF16)
    left = dot_nt(dot(pick_cotan, full_one).astype(BF16), pick_latent).astype(BF16)
    left_t = left.T

    counts = [rows * (hi - lo) for lo, hi in groups]
    y_first, *v_first = raise_field(turn(flat(z_first)), left, fold, counts)
    v_first = [turn(v) for v in v_first]
    ups_first = [v_first[-1]]
    for step in range(1, cols):
        ups_first.append(up(ups_first[-1], step))
    seconds = [second, down(after(second, v_first[-1]), 1)]
    z_last = pack(latent, swap, (0, tiles), cuts[1], rows)

    def hop(q, back):
        value = sums[q] if back == last else add(sums[q], own[back][q])
        return move(value, [(c, c - 1) for c in range(back, cols)])

    later = max(last - 1, 0)
    if later:
        sums[0] = hop(0, later)
    z_last = exchange(after(z_last, second, firsts[last], sums[0]))
    z_last = after(z_last, seconds[1], sums[1])
    y_last, *v_last = raise_field(turn(flat(z_last)), left, fold, counts)
    v_last = [turn(v) for v in v_last]
    ups_last = [v_last[-1]]
    for step in range(1, cols):
        ups_last.append(up(ups_last[-1], step))
    for back in range(later - 1, 0, -1):
        sums[0] = hop(0, back)
    if later:
        sums[1] = hop(1, later)
    early = sums[1]
    for back in range(later - 1, 0, -1):
        sums[1] = hop(1, back)
    for step in range(2, cols):
        held = seconds[-1]
        if step == last:
            held = after(held, v_last[-1], ups_first[last], sums[0])
        seconds.append(down(held, step))
    bits = [(0, 0, half), (0, half, unit), (1, unit, span_two)]
    ends = [sums[q][:, lo - cuts[q][0] : hi - cuts[q][0]] for q, lo, hi in bits]

    w_near, grad_near = [], 0.0
    for g, chunk in enumerate((firsts, seconds)):
        held = [chunk[0]] + chunk[1:]
        if g:
            held[0] = after(held[0], early, ups_last[min(2, last)])
        else:
            held[0] = after(held[0], ups_last[1])
        *w, grad = gathered(held, [v_first[g], v_last[g]], mix_near, cuts, per)
        w_near.append(w)
        grad_near = grad_near + grad

    two, met, sent = [], [], []
    for d in range(cols):
        grad = pairs(far_part, [ups_first[d], ups_last[d]], per)
        met.append(grad)
        if d:
            grad = move(grad, [(c, c - d) for c in range(d, cols)])
            sent.append(grad)
        two.append(grad_near[d] + grad)
    two = jnp.concatenate(two, axis=0)
    two = jnp.pad(two, ((order_two - span_two, 0), (0, 0)))
    two = lax.dynamic_slice(
        two, (order_two - span_two - place * span_two, 0), (order_two, span_two)
    )
    two = two.reshape(rows, order_two // rows, span_two)

    grad_latent, one, moved, written = None, None, [], []
    for n, (q, lo, hi) in enumerate(bits):
        own_here = own[0][q][:, lo - cuts[q][0] : hi - cuts[q][0]]
        share = turn(add(ends[n], own_here))
        if n == 1:
            share = after(share, *met, sums[1], one)
        elif n == 2:
            share = after(share, *sent, one)
        parts = [turn(w[q][:, lo - cuts[q][0] : hi - cuts[q][0]]) for w in w_near] + [share]
        grad, w_y = finish(parts, left_t, fold)
        one = match(w_y, y_last if q else y_first, (lo - cuts[q][0]) // (2 * fold), one)
        grad = turn(grad).reshape(rows, tiles, hi - lo, LANES)
        moved = [exchange(after(grad, *moved, *written[:-1]))]
        where = (lo, hi, half if q == 0 else unit)
        grad_latent = unpack(moved[0], swap, latent.shape, where, grad_latent)
        written.append(grad_latent)

    one = dot(one.astype(BF16), pick_latent).astype(BF16)
    one = jnp.transpose(one.reshape(order_one, cols, order_one // cols), (1, 0, 2))
    total = lax.dynamic_index_in_dim(one, place, 0, keepdims=False).astype(F32)
    for d in range(1, cols):
        ring = [(c, (c + d) % cols) for c in range(cols)]
        mine = lax.dynamic_index_in_dim(one, (place + d) % cols, 0, keepdims=False)
        total = total + move(mine, ring).astype(F32)
    total = total.reshape(fold, rows * tiles, order_one // cols)
    total = jnp.concatenate(
        [
            total[:, rows * lo : rows * hi].reshape(fold, rows, hi - lo, order_one // cols)
            for lo, hi in groups
        ],
        axis=2,
    )
    total = jnp.transpose(total, (1, 2, 0, 3)).reshape(rows, span_one, order_one // cols)
    total = jnp.concatenate([total, two], axis=2)
    total = exchange(after(total, *moved, written[-2])).sum(0)
    grad_one = keep_lower(total[:, : order_one // cols], depth)
    grad_two = keep_lower(total[:, order_one // cols :], depth)
    return (grad_latent, grad_one, grad_two)


def tiles_fit(rows, cols, span_one, span_two, depth):
    if depth % LANES or depth % rows or LANES * rows % depth:
        return False
    fold = LANES * rows // depth
    if fold > LANES or LANES % fold or depth // LANES * fold != rows:
        return False
    return (
        cols > 1
        and rows % 8 == 0
        and span_one % fold == 0
        and span_one // fold >= 4
        and span_two % (2 * fold) == 0
        and span_two % 8 == 0
        and span_two >= 64
        and 16 % (2 * fold) == 0
    )


def solution(mesh):
    rows, cols = mesh.shape["row"], mesh.shape["col"]

    def on_device(latent, cotangent, factor_one, factor_two):
        if tiles_fit(rows, cols, *latent.shape):
            return by_tiles(rows, cols, latent, cotangent, factor_one, factor_two)
        return by_lines(latent, cotangent, factor_one, factor_two)

    placed = (P("row", "col", None), P("row", "col", None), P("row", None), P("col", None))
    return jax.shard_map(
        on_device,
        mesh=mesh,
        in_specs=placed,
        out_specs=(P("row", "col", None), P("row", "col"), P("row", "col")),
        check_vma=False,
    )
```

time: 1000 us -> 623 us (0.62)
  waiting for transfers between devices: 652 us -> 260 us
  Pallas kernels: 0 us -> 163 us
  local copies, waits for them, and re-layouts: 199 us -> 58.3 us
  starting transfers between devices: 37.8 us -> 93.6 us
  matrix products: 56.4 us -> 7.21 us
  blocking collectives: 32.3 us -> 0 us
  other arithmetic: 1.7 us -> 27.1 us
  between operations: 14.9 us -> 2.29 us
    all_to_all x7 -> x9, waiting for transfers between devices: 532 us -> 55.2 us  [exchange(): return lax.all_to_all(value, 'row', split_axis=0, concat_axis=0, tiled=True)]
    ppermute x0 -> x27, waiting for transfers between devices: none -> 204 us  [move(): return lax.ppermute(value, 'col', pairs_of)]
    pallas_call x0 -> x23, Pallas kernels: none -> 163 us  [the longest x4 26.9 us: pairs(): pl.pallas_call(kernel, grid=(tiles // per,), in_specs=[spec(span_two)] +...]
    all_to_all x14 -> x0, local copies, waits for them, and re-layouts: 125 us -> none  [the longest x3 27.7 us: on_device(): lax.all_to_all(mixed_block, 'row', split_axis=1, concat_axis=0, tiled=True)]
    unnamed x6 -> x0, waiting for transfers between devices: 120 us -> none
    ppermute x0 -> x27, starting transfers between devices: none -> 52.7 us  [move(): return lax.ppermute(value, 'col', pairs_of)]
    dot_general x5 -> x3, matrix products: 56.4 us -> 7.21 us  [the longest x2 5.3 us: dot(): return jnp.dot(left, right, preferred_element_type=F32)]
    all_gather x2 -> x0, blocking collectives: 32.3 us -> none  [the longest x1 21.9 us: on_device(): full_two = lax.all_gather(factor_two, 'col', axis=0, tiled=True)]
  transfers between devices with their start and end apart: 10 -> 36, of which waited for: 10 -> 14; matrix products, arithmetic and copies ran while one was open for 15% -> 12% of each run, Pallas kernels for 0% -> 24%
where the time goes in v1:
time: 623 us; the launch traced here: 612 us
  waiting for transfers between devices  260 us (42%)
  Pallas kernels  163 us (26%)
  starting transfers between devices  93.6 us (15%)
  local copies, waits for them, and re-layouts  58.3 us (9%)
  other arithmetic  27.1 us (4%)
  matrix products  7.21 us (1%)
    ppermute x27, waiting for transfers between devices, move(): return lax.ppermute(value, 'col', pairs_of)  204 us
    all_to_all x9, waiting for transfers between devices, exchange(): return lax.all_to_all(value, 'row', split_axis=0, concat_axis=0, tiled=True)  55.2 us
    ppermute x27, starting transfers between devices, move(): return lax.ppermute(value, 'col', pairs_of)  52.7 us
    all_to_all x9, starting transfers between devices, exchange(): return lax.all_to_all(value, 'row', split_axis=0, concat_axis=0, tiled=True)  40.8 us
    pallas_call x4, Pallas kernels, pairs(): pl.pallas_call(kernel, grid=(tiles // per,), in_specs=[spec(span_two)] +...  26.9 us
    pallas_call x5, Pallas kernels, pack(): pl.pallas_call(kernel, grid=(count // per,), in_specs=[pl.BlockSpec((per...  25.3 us
    pallas_call x2, Pallas kernels, raise_field(): pl.pallas_call(kernel, grid=(count,), in_specs=[pl.BlockSpec((step,) + fi...  23.6 us
    pallas_call x3, Pallas kernels, unpack(): pl.pallas_call(kernel, grid=(tiles // per,), in_specs=[pl.BlockSpec((rows...  23.2 us
  transfers between devices with their start and end apart: 36, of which 14 were waited for; matrix products, arithmetic and copies ran while one was open for 12% of the time, Pallas kernels for 24%

profile of v1, /device:TPU:0, one launch (start us, length us, event | category | flops | bytes accessed | tf_op | source)
XLA Modules:
  0.0 611.5 jit_solution(6322337585083685035)
XLA Ops:
  1.7 3.7 pack.5
  5.4 5.3 all-to-all-start
  15.1 4.1 pack.9
  20.9 2.7 collective-permute-done.1
  23.6 13.3 %all-to-all-done = bf16[8,6,168,128]{3,2,1,0:T(8,128)(2,1)S(1)} async-done(((bf16[8,6,168,128]{3,2,1,0:T(8,128)(2,1)}), bf16[8,6,168,128]{3,2,1,0:T(8,128)(2,1)S(1)}, u32[]{:S(2)}, u32[]{:S(2)}) %all-to-all-start) | async-done | bytes 2064416 | tf_op jit(solution)/shard_map/all_to_all | solution.py:444
  37.0 4.5 all-to-all-start.1
  42.9 7.0 %pack.8 = bf16[8,21,96,128]{3,2,1,0:T(8,128)(2,1)S(1)} custom-call(bf16[84,168,256]{2,1,0:T(8,128)(2,1)} %x_ref.8, bf16[512,512]{1,0:T(8,128)(2,1)S(1)} %fusion.63.p_ref), custom_call_target="tpu_custom_call" | custom-call | flops 1 | bytes 1 | tf_op jit(solution)/shard_map/pack/pallas_call | solution.py:138
  49.9 2.0 copy-done
  52.3 4.9 pad_maximum_fusion
  57.3 33.5 %collective-permute-done.3.refs_1_ = bf16[48,168,128]{2,1,0:T(8,128)(2,1)} collective-permute-done((bf16[48,168,128]{2,1,0:T(8,128)(2,1)S(1)}, bf16[48,168,128]{2,1,0:T(8,128)(2,1)}, u32[]{:S(2)}, u32[]{:S(2)}) %collective-permute-start.3) | collective-permute-done | bytes 2064416 | tf_op jit(solution)/shard_map/ppermute | solution.py:453
  90.8 4.8 all-to-all-start.2
  97.2 9.2 %shares.1 = (f32[72,96,128]{2,1,0:T(8,128)}, f32[72,72,128]{2,1,0:T(8,128)}, bf16[72,96,128]{2,1,0:T(8,128)(2,1)S(1)}, bf16[72,72,128]{2,1,0:T(8,128)(2,1)S(1)},...) custom-call(bf16[72,168,128]{2,1,0:T(8,128)(2,1)} %bitcast.7.c_ref.r, ...), custom_call_target="tpu_custom_call" | custom-call | flops 1 | bytes 1 | tf_op jit(solution)/shard_map/shares/pallas_call | solution.py:406
  108.8 4.4 copy.112
  115.0 3.7 pack.7
  118.7 26.2 %collective-permute-done.4.refs_2_ = bf16[48,168,128]{2,1,0:T(8,128)(2,1)} collective-permute-done((bf16[48,168,128]{2,1,0:T(8,128)(2,1)}, bf16[48,168,128]{2,1,0:T(8,128)(2,1)}, u32[]{:S(2)}, u32[]{:S(2)}) %collective-permute-start.4) | collective-permute-done | bytes 2064416 | tf_op jit(solution)/shard_map/ppermute | solution.py:453
  146.3 8.3 %all-to-all-done.2 = bf16[8,26,96,128]{3,2,1,0:T(8,128)(2,1)} async-done(((bf16[8,26,96,128]{3,2,1,0:T(8,128)(2,1)}), bf16[8,26,96,128]{3,2,1,0:T(8,128)(2,1)}, u32[]{:S(2)}, u32[]{:S(2)}) %all-to-all-start.2) | async-done | bytes 5111840 | tf_op jit(solution)/shard_map/all_to_all | solution.py:444
  157.6 4.9 slice.111
  162.5 4.5 all-to-all-start.3
  167.1 3.7 fusion.52.clone.5
  173.5 5.8 copy.178
  179.3 13.2 %raise_field.2 = (bf16[12,672,256]{2,1,0:T(8,128)(2,1)}, bf16[96,48,128]{2,1,0:T(8,128)(2,1)S(1)}, bf16[96,48,128]{2,1,0:T(8,128)(2,1)S(1)}, bf16[96,72,128]{2,1,0:T(8,128)(2,1)S(1)}) custom-call(bf16[96,168,128]{2,1,0:T(8,128)(2,1)} %bitcast.124, bf16[672,672]{1,0:T(8,128)(2,1)S(1)} %copy.116.l_ref), custom_call_target="tpu_custom_call" | custom-call | flops 1 | bytes 1 | tf_op jit(solution)/shard_map/raise_field/pallas_call | solution.py:230
  194.1 4.8 collective-permute-start.14
  198.9 3.4 add_convert_fusion.1
  205.6 30.9 %collective-permute-done.14.refs_1_ = bf16[72,96,128]{2,1,0:T(8,128)(2,1)} collective-permute-done((bf16[72,96,128]{2,1,0:T(8,128)(2,1)}, bf16[72,96,128]{2,1,0:T(8,128)(2,1)}, u32[]{:S(2)}, u32[]{:S(2)}) %collective-permute-start.14) | collective-permute-done | bytes 1769504 | tf_op jit(solution)/shard_map/ppermute | solution.py:453
  238.3 6.9 %pack.6 = bf16[8,21,72,128]{3,2,1,0:T(8,128)(2,1)S(1)} custom-call(bf16[84,168,256]{2,1,0:T(8,128)(2,1)} %x_ref.8, bf16[512,512]{1,0:T(8,128)(2,1)S(1)} %fusion.63.p_ref), custom_call_target="tpu_custom_call" | custom-call | flops 1 | bytes 1 | tf_op jit(solution)/shard_map/pack/pallas_call | solution.py:138
  246.8 4.5 all-to-all-start.4
  256.0 3.6 add_convert_fusion
  262.7 25.9 %all-to-all-done.4 = bf16[8,21,72,128]{3,2,1,0:T(8,128)(2,1)} async-done(((bf16[8,21,72,128]{3,2,1,0:T(8,128)(2,1)}), bf16[8,21,72,128]{3,2,1,0:T(8,128)(2,1)}, u32[]{:S(2)}, u32[]{:S(2)}) %all-to-all-start.4) | async-done | bytes 3096608 | tf_op jit(solution)/shard_map/all_to_all | solution.py:444
  288.7 3.9 copy.179
  292.6 10.3 %raise_field.3 = (bf16[9,672,256]{2,1,0:T(8,128)(2,1)}, bf16[72,48,128]{2,1,0:T(8,128)(2,1)S(1)}, bf16[72,48,128]{2,1,0:T(8,128)(2,1)S(1)}, bf16[72,72,128]{2,1,0:T(8,128)(2,1)S(1)}) custom-call(bf16[72,168,128]{2,1,0:T(8,128)(2,1)} %bitcast.127, bf16[672,672]{1,0:T(8,128)(2,1)S(1)} %copy.116.l_ref), custom_call_target="tpu_custom_call" | custom-call | flops 1 | bytes 1 | tf_op jit(solution)/shard_map/raise_field/pallas_call | solution.py:230
  303.1 12.8 %collective-permute-start.10 = (bf16[72,72,128]{2,1,0:T(8,128)(2,1)S(1)}, bf16[72,72,128]{2,1,0:T(8,128)(2,1)S(1)}, u32[]{:S(2)}, u32[]{:S(2)}) collective-permute-start(bf16[72,72,128]{2,1,0:T(8,128)(2,1)S(1)} %bitcast.114), channel_id=1, source_target_pairs={{0,1},{1,2},{2,3},{4,5},{5,6},{6,7},{8,9},{9,10},{10,11},{12,13},{... | collective-permute-start | bytes 3981320 | tf_op jit(solution)/shard_map/ppermute | solution.py:453
  315.9 58.5 %collective-permute-done.17 = bf16[72,96,128]{2,0,1:T(8,128)(2,1)} collective-permute-done((bf16[72,96,128]{2,0,1:T(8,128)(2,1)}, bf16[72,96,128]{2,0,1:T(8,128)(2,1)}, u32[]{:S(2)}, u32[]{:S(2)}) %collective-permute-start.17) | collective-permute-done | bytes 1769504 | tf_op jit(solution)/shard_map/ppermute | solution.py:453
  375.7 2.7 add_convert_fusion.3
  381.0 2.1 copy.134
  384.7 2.7 fusion.104
  387.9 7.8 %gathered.2 = (bf16[48,96,128]{2,1,0:T(8,128)(2,1)S(1)}, bf16[48,72,128]{2,1,0:T(8,128)(2,1)S(1)}, f32[4,168,168]{2,1,0:T(8,128)S(1)}) custom-call(bf16[48,168,128]{2,1,0:T(8,128)(2,1)} %bitcast.131, bf16[48,168,128]{2,1,0:T(8,128)(2,1)} %collective-permute-done.3.refs_1_, bf16[48,168,128]{2,1,0:T(8,128)(2,1)} %collective-permute-done.4.refs_2_, ...), custom_call_target="tpu_custom_call" | custom-call | flops 1 | bytes 1 | tf_op jit(solution)/shard_map/gathered/pallas_call | solution.py:342
  397.1 25.0 %collective-permute-done.18.refs_3_ = bf16[48,168,128]{2,1,0:T(8,128)(2,1)} collective-permute-done((bf16[48,168,128]{2,1,0:T(8,128)(2,1)}, bf16[48,168,128]{2,1,0:T(8,128)(2,1)}, u32[]{:S(2)}, u32[]{:S(2)}) %collective-permute-start.18) | collective-permute-done | bytes 2064416 | tf_op jit(solution)/shard_map/ppermute | solution.py:453
  422.1 7.8 %gathered.3 = (bf16[48,96,128]{2,1,0:T(8,128)(2,1)S(1)}, bf16[48,72,128]{2,1,0:T(8,128)(2,1)S(1)}, f32[4,168,168]{2,1,0:T(8,128)S(1)}) custom-call(bf16[48,168,128]{2,1,0:T(8,128)(2,1)} %bitcast.9.refs_0_, bf16[48,168,128]{2,1,0:T(8,128)(2,1)} %collective-permute-done.8.refs_1_, bf16[48,168,128]{2,1,0:T(8,128)(2,1)} %collective-permute-done.13.refs_2_, ...), custom_call_target="tpu_custom_call" | custom-call | flops 1 | bytes 1 | tf_op jit(solution)/shard_map/gathered/pallas_call | solution.py:342
  431.8 6.2 %finish.3 = (bf16[48,168,128]{2,1,0:T(8,128)(2,1)S(1)}, bf16[6,672,256]{2,1,0:T(8,128)(2,1)}) custom-call(bf16[48,48,128]{2,1,0:T(8,128)(2,1)S(1)} %get-tuple-element.96.refs_0_, bf16[48,48,128]{2,1,0:T(8,128)(2,1)S(1)} %get-tuple-element.94.refs_1_, bf16[48,72,128]{2,1,0:T(8,128)(2,1)S(1)} %get-tuple-element.92.refs_2_, bf16[672,672]{1,0:T(8,128)(2,1)S(1)} %bitcast.111), custom_call_target="tpu_custom_call" | custom-call | flops 1 | bytes 1 | tf_op jit(solution)/shard_map/finish/pallas_call | solution.py:260
  439.6 4.4 all-to-all-start.5
  444.7 2.0 add_convert_fusion.2
  448.2 6.6 %pairs.7 = f32[168,168]{1,0:T(8,128)S(1)} custom-call(bf16[72,168,128]{2,1,0:T(8,128)(2,1)} %bitcast.7.c_ref.refs_0_, bf16[72,96,128]{2,1,0:T(8,128)(2,1)} %bitcast.102.refs_1_, bf16[72,72,128]{2,1,0:T(8,128)(2,1)S(1)} %bitcast.115), custom_call_target="tpu_custom_call" | custom-call | flops 1 | bytes 1 | tf_op jit(solution)/shard_map/pairs/pallas_call | solution.py:372
  455.5 6.7 %pairs.4 = f32[168,168]{1,0:T(8,128)S(1)} custom-call(bf16[72,168,128]{2,1,0:T(8,128)(2,1)} %bitcast.7.c_ref.refs_0_, bf16[72,96,128]{2,1,0:T(8,128)(2,1)} %collective-permute-done.14.refs_1_, bf16[72,72,128]{2,1,0:T(8,128)(2,1)S(1)} %copy-done.18), custom_call_target="tpu_custom_call" | custom-call | flops 1 | bytes 1 | tf_op jit(solution)/shard_map/pairs/pallas_call | solution.py:372
  462.3 6.8 %pairs.5 = f32[168,168]{1,0:T(8,128)S(1)} custom-call(bf16[72,168,128]{2,1,0:T(8,128)(2,1)} %bitcast.7.c_ref.refs_0_, bf16[72,96,128]{2,1,0:T(8,128)(2,1)} %collective-permute-done.15.refs_1_, bf16[72,72,128]{2,1,0:T(8,128)(2,1)S(1)} %copy-done.20), custom_call_target="tpu_custom_call" | custom-call | flops 1 | bytes 1 | tf_op jit(solution)/shard_map/pairs/pallas_call | solution.py:372
  469.1 5.1 match.3.rest_0_
  475.6 6.7 %pairs.6 = f32[168,168]{1,0:T(8,128)S(1)} custom-call(bf16[72,168,128]{2,1,0:T(8,128)(2,1)} %bitcast.7.c_ref.refs_0_, bf16[72,96,128]{2,1,0:T(8,128)(2,1)} %collective-permute-done.16.refs_1_, bf16[72,72,128]{2,1,0:T(8,128)(2,1)S(1)} %collective-permute-done.22.refs_2_), custom_call_target="tpu_custom_call" | custom-call | flops 1 | bytes 1 | tf_op jit(solution)/shard_map/pairs/pallas_call | solution.py:372
  482.4 6.2 %finish.4 = (bf16[48,168,128]{2,1,0:T(8,128)(2,1)S(1)}, bf16[6,672,256]{2,1,0:T(8,128)(2,1)}) custom-call(bf16[48,48,128]{2,1,0:T(8,128)(2,1)S(1)} %copy-done.8, bf16[48,48,128]{2,1,0:T(8,128)(2,1)S(1)} %get-tuple-element.95.refs_1_, bf16[48,72,128]{2,1,0:T(8,128)(2,1)S(1)} %copy-done.7, bf16[672,672]{1,0:T(8,128)(2,1)S(1)} %bitcast.112), custom_call_target="tpu_custom_call" | custom-call | flops 1 | bytes 1 | tf_op jit(solution)/shard_map/finish/pallas_call | solution.py:260
  490.2 4.5 all-to-all-start.6
  498.9 2.5 fusion.53.refs_2_
  503.0 5.0 match.4.rest_0_
  508.1 8.3 %collective-permute-done.21 = f32[168,168]{1,0:T(8,128)S(1)} collective-permute-done((f32[168,168]{1,0:T(8,128)S(1)}, f32[168,168]{1,0:T(8,128)S(1)}, u32[]{:S(2)}, u32[]{:S(2)}) %collective-permute-start.21) | collective-permute-done | bytes 112928 | tf_op jit(solution)/shard_map/ppermute | solution.py:453
  516.4 9.1 %finish.5 = (bf16[72,168,128]{2,1,0:T(8,128)(2,1)}, bf16[9,672,256]{2,1,0:T(8,128)(2,1)}) custom-call(bf16[72,48,128]{2,1,0:T(8,128)(2,1)S(1)} %bitcast.119, bf16[72,48,128]{2,1,0:T(8,128)(2,1)S(1)} %bitcast.120, bf16[72,72,128]{2,1,0:T(8,128)(2,1)S(1)} %fusion.53.refs_2_, bf16[672,672]{1,0:T(8,128)(2,1)S(1)} %bitcast.113), custom_call_target="tpu_custom_call" | custom-call | flops 1 | bytes 1 | tf_op jit(solution)/shard_map/finish/pallas_call | solution.py:260
  525.5 3.9 copy.138
  529.4 7.6 %unpack.3.rest_0_ = bf16[84,168,256]{2,1,0:T(8,128)(2,1)} custom-call(bf16[8,21,48,128]{3,2,1,0:T(8,128)(2,1)} %all-to-all-done.5.x_ref, bf16[512,512]{1,0:T(8,128)(2,1)S(1)} %fusion.63.p_ref), custom_call_target="tpu_custom_call" | custom-call | flops 1 | bytes 1 | tf_op jit(solution)/shard_map/unpack/pallas_call | solution.py:174
  536.9 4.6 all-to-all-start.7
  543.4 8.0 %match.5 = f32[672,672]{1,0:T(8,128)S(1)} custom-call(bf16[9,672,256]{2,1,0:T(8,128)(2,1)} %get-tuple-element.84.w_ref, bf16[9,672,256]{2,1,0:T(8,128)(2,1)} %get-tuple-element.85.z_ref, f32[672,672]{1,0:T(8,128)S(1)} %copy-done.4), custom_call_target="tpu_custom_call" | custom-call | flops 1 | bytes 1 | tf_op jit(solution)/shard_map/match/pallas_call | solution.py:290
  553.1 3.8 collective-permute-start.26
  558.3 5.7 collective-permute-done.24
  564.0 5.8 collective-permute-done.26
  569.9 7.8 %collective-permute-done.25 = bf16[672,168]{0,1:T(8,128)(2,1)} collective-permute-done((bf16[672,168]{0,1:T(8,128)(2,1)S(1)}, bf16[672,168]{0,1:T(8,128)(2,1)}, u32[]{:S(2)}, u32[]{:S(2)}) %collective-permute-start.25) | collective-permute-done | bytes 225824 | tf_op jit(solution)/shard_map/ppermute | solution.py:453
  581.1 7.6 %unpack.4.rest_0_ = bf16[84,168,256]{2,1,0:T(8,128)(2,1)} custom-call(bf16[8,21,48,128]{3,2,1,0:T(8,128)(2,1)} %all-to-all-done.6.x_ref, bf16[512,512]{1,0:T(8,128)(2,1)S(1)} %fusion.63.p_ref, bf16[84,168,256]{2,1,0:T(8,128)(2,1)} %unpack.3.rest_0_), custom_call_target="tpu_custom_call", output_to_operand_aliasing={{}: (2, {})} | custom-call | flops 1 | bytes 1 | tf_op jit(solution)/shard_map/unpack/pallas_call | solution.py:174
  589.8 3.8 all-to-all-start.8
  593.7 8.0 %unpack.5 = bf16[84,168,256]{2,1,0:T(8,128)(2,1)} custom-call(bf16[8,21,72,128]{3,2,1,0:T(8,128)(2,1)} %all-to-all-done.7.x_ref, bf16[512,512]{1,0:T(8,128)(2,1)S(1)} %fusion.63.p_ref, bf16[84,168,256]{2,1,0:T(8,128)(2,1)} %unpack.4.rest_0_), custom_call_target="tpu_custom_call", output_to_operand_aliasing={{}: (2, {})} | custom-call | flops 1 | bytes 1 | tf_op jit(solution)/shard_map/unpack/pallas_call | solution.py:174
  601.7 7.7 %all-to-all-done.8 = f32[8,84,336]{2,1,0:T(8,128)S(1)} async-done(((f32[8,84,336]{2,1,0:T(8,128)}), f32[8,84,336]{2,1,0:T(8,128)S(1)}, u32[]{:S(2)}, u32[]{:S(2)}) %all-to-all-start.8) | async-done | bytes 903200 | tf_op jit(solution)/shard_map/all_to_all | solution.py:444
  (216 shorter events, 71.6 us)
Async XLA Ops:
  5.4 31.6 %all-to-all-start = ((bf16[8,6,168,128]{3,2,1,0:T(8,128)(2,1)}), bf16[8,6,168,128]{3,2,1,0:T(8,128)(2,1)S(1)}, u32[]{:S(2)}, u32[]{:S(2)}) async-start(bf16[8,6,168,128]{3,2,1,0:T(8,128)(2,1)} %pack.5), calls=%async_computation | async-start | bytes 4128768 | tf_op jit(solution)/shard_map/all_to_all | solution.py:444
  10.8 8.3 %copy-start.40 = (bf16[168,672]{0,1:T(8,128)(2,1)}, bf16[168,672]{0,1:T(8,128)(2,1)S(1)}, u32[]{:S(2)}) copy-start(bf16[168,672]{0,1:T(8,128)(2,1)S(1)} %copy.111) | copy-start | bytes 677380
  11.2 9.7 %collective-permute-start.2 = (bf16[168,168]{1,0:T(8,128)(2,1)S(1)}, bf16[168,168]{1,0:T(8,128)(2,1)S(1)}, u32[]{:S(2)}, u32[]{:S(2)}) collective-permute-start(bf16[168,168]{1,0:T(8,128)(2,1)S(1)} %get-tuple-element.108), channel_id=1, source_target_pairs={{3,0},{7,4},{11,8},{15,12},{19,16},{23,20},{27,24},{31,28}} | collective-permute-start | bytes 169352 | tf_op jit(solution)/shard_map/ppermute | solution.py:453
  12.5 11.1 %collective-permute-start.1 = (bf16[168,168]{1,0:T(8,128)(2,1)S(1)}, bf16[168,168]{1,0:T(8,128)(2,1)S(1)}, u32[]{:S(2)}, u32[]{:S(2)}) collective-permute-start(bf16[168,168]{1,0:T(8,128)(2,1)S(1)} %get-tuple-element.109), channel_id=1, source_target_pairs={{2,0},{3,1},{6,4},{7,5},{10,8},{11,9},{14,12},{15,13},{18,16},{19,... | collective-permute-start | bytes 169352 | tf_op jit(solution)/shard_map/ppermute | solution.py:453
  13.8 9.8 %collective-permute-start = (bf16[168,168]{1,0:T(8,128)(2,1)S(1)}, bf16[168,168]{1,0:T(8,128)(2,1)S(1)}, u32[]{:S(2)}, u32[]{:S(2)}) collective-permute-start(bf16[168,168]{1,0:T(8,128)(2,1)S(1)} %get-tuple-element.110), channel_id=1, source_target_pairs={{1,0},{2,1},{3,2},{5,4},{6,5},{7,6},{9,8},{10,9},{11,10},{13,12},{... | collective-permute-start | bytes 169352 | tf_op jit(solution)/shard_map/ppermute | solution.py:453
  37.0 53.8 %all-to-all-start.1 = ((bf16[8,9,168,128]{3,2,1,0:T(8,128)(2,1)}), bf16[8,9,168,128]{3,2,1,0:T(8,128)(2,1)}, u32[]{:S(2)}, u32[]{:S(2)}) async-start(bf16[8,9,168,128]{3,2,1,0:T(8,128)(2,1)} %copy-done.1), calls=%async_computation.1 | async-start | bytes 6193152 | tf_op jit(solution)/shard_map/all_to_all | solution.py:444
  41.4 10.5 %copy-start.53 = (bf16[84,672]{1,0:T(8,128)(2,1)S(1)}, bf16[84,672]{1,0:T(8,128)(2,1)}, u32[]{:S(2)}) copy-start(bf16[84,672]{1,0:T(8,128)(2,1)} %param.6) | copy-start | bytes 338692
  41.5 49.3 %collective-permute-start.3 = (bf16[48,168,128]{2,1,0:T(8,128)(2,1)S(1)}, bf16[48,168,128]{2,1,0:T(8,128)(2,1)}, u32[]{:S(2)}, u32[]{:S(2)}) collective-permute-start(bf16[48,168,128]{2,1,0:T(8,128)(2,1)S(1)} %bitcast.130), channel_id=1, source_target_pairs={{1,0},{2,1},{3,2},{5,4},{6,5},{7,6},{9,8},{10,9},{11,10},{13,12},{... | collective-permute-start | bytes 6193160 | tf_op jit(solution)/shard_map/ppermute | solution.py:453
  90.8 6.1 copy-start.41
  90.8 63.7 %all-to-all-start.2 = ((bf16[8,26,96,128]{3,2,1,0:T(8,128)(2,1)}), bf16[8,26,96,128]{3,2,1,0:T(8,128)(2,1)}, u32[]{:S(2)}, u32[]{:S(2)}) async-start(bf16[8,26,96,128]{3,2,1,0:T(8,128)(2,1)} %pad_maximum_fusion), calls=%async_computation.2 | async-start | bytes 10223616 | tf_op jit(solution)/shard_map/all_to_all | solution.py:444
  95.6 49.4 %collective-permute-start.4 = (bf16[48,168,128]{2,1,0:T(8,128)(2,1)}, bf16[48,168,128]{2,1,0:T(8,128)(2,1)}, u32[]{:S(2)}, u32[]{:S(2)}) collective-permute-start(bf16[48,168,128]{2,1,0:T(8,128)(2,1)} %collective-permute-done.3.refs_1_), channel_id=1, source_target_pairs={{1,0},{2,1},{5,4},{6,5},{9,8},{10,9},{13,12},{14,13},{17,16},{18,1... | collective-permute-start | bytes 6193160 | tf_op jit(solution)/shard_map/ppermute | solution.py:453
  108.7 9.9 %copy-start.13 = (bf16[72,72,128]{2,1,0:T(8,128)(2,1)}, bf16[72,72,128]{2,1,0:T(8,128)(2,1)S(1)}, u32[]{:S(2)}) copy-start(bf16[72,72,128]{2,1,0:T(8,128)(2,1)S(1)} %get-tuple-element.55) | copy-start | bytes 3981316
  108.8 9.9 %copy-start.15 = (bf16[72,72,128]{2,1,0:T(8,128)(2,1)}, bf16[72,72,128]{2,1,0:T(8,128)(2,1)S(1)}, u32[]{:S(2)}) copy-start(bf16[72,72,128]{2,1,0:T(8,128)(2,1)S(1)} %get-tuple-element.62) | copy-start | bytes 3981316
  113.1 49.4 %collective-permute-start.5 = (bf16[72,96,128]{2,0,1:T(8,128)(2,1)}, bf16[72,96,128]{2,0,1:T(8,128)(2,1)}, u32[]{:S(2)}, u32[]{:S(2)}) collective-permute-start(bf16[72,96,128]{2,0,1:T(8,128)(2,1)} %copy.112), channel_id=1, source_target_pairs={{3,2},{7,6},{11,10},{15,14},{19,18},{23,22},{27,26},{31,30}} | collective-permute-start | bytes 5308424 | tf_op jit(solution)/shard_map/ppermute | solution.py:453
  145.0 101.9 %collective-permute-start.6 = (bf16[48,168,128]{2,1,0:T(8,128)(2,1)}, bf16[48,168,128]{2,1,0:T(8,128)(2,1)}, u32[]{:S(2)}, u32[]{:S(2)}) collective-permute-start(bf16[48,168,128]{2,1,0:T(8,128)(2,1)} %collective-permute-done.4.refs_2_), channel_id=1, source_target_pairs={{1,0},{5,4},{9,8},{13,12},{17,16},{21,20},{25,24},{29,28}} | collective-permute-start | bytes 6193160 | tf_op jit(solution)/shard_map/ppermute | solution.py:453
  162.5 41.8 %all-to-all-start.3 = ((bf16[8,6,168,128]{3,2,1,0:T(8,128)(2,1)}), bf16[8,6,168,128]{3,2,1,0:T(8,128)(2,1)}, u32[]{:S(2)}, u32[]{:S(2)}) async-start(bf16[8,6,168,128]{3,2,1,0:T(8,128)(2,1)} %pack.7), calls=%async_computation.3 | async-start | bytes 4128768 | tf_op jit(solution)/shard_map/all_to_all | solution.py:444
  192.5 9.8 %copy-start.21 = (bf16[96,48,128]{2,1,0:T(8,128)(2,1)}, bf16[96,48,128]{2,1,0:T(8,128)(2,1)S(1)}, u32[]{:S(2)}) copy-start(bf16[96,48,128]{2,1,0:T(8,128)(2,1)S(1)} %get-tuple-element.66) | copy-start | bytes 3538948
  192.5 9.8 %copy-start.23 = (bf16[96,48,128]{2,1,0:T(8,128)(2,1)}, bf16[96,48,128]{2,1,0:T(8,128)(2,1)S(1)}, u32[]{:S(2)}) copy-start(bf16[96,48,128]{2,1,0:T(8,128)(2,1)S(1)} %get-tuple-element.59) | copy-start | bytes 3538948
  192.5 6.4 %copy-start.42 = (bf16[72,96,128]{2,1,0:T(8,128)(2,1)S(1)}, bf16[72,96,128]{2,1,0:T(8,128)(2,1)}, u32[]{:S(2)}) copy-start(bf16[72,96,128]{2,1,0:T(8,128)(2,1)} %get-tuple-element.50) | copy-start | bytes 5308420
  194.1 42.4 %collective-permute-start.14 = (bf16[72,96,128]{2,1,0:T(8,128)(2,1)}, bf16[72,96,128]{2,1,0:T(8,128)(2,1)}, u32[]{:S(2)}, u32[]{:S(2)}) collective-permute-start(bf16[72,96,128]{2,1,0:T(8,128)(2,1)} %bitcast.102.refs_1_), channel_id=1, source_target_pairs={{0,1},{1,2},{2,3},{4,5},{5,6},{6,7},{8,9},{9,10},{10,11},{12,13},{... | collective-permute-start | bytes 5308424 | tf_op jit(solution)/shard_map/ppermute | solution.py:453
  202.3 44.5 %collective-permute-start.7 = (bf16[72,96,128]{2,0,1:T(8,128)(2,1)}, bf16[72,96,128]{2,0,1:T(8,128)(2,1)}, u32[]{:S(2)}, u32[]{:S(2)}) collective-permute-start(bf16[72,96,128]{2,0,1:T(8,128)(2,1)} %add_convert_fusion.1), channel_id=1, source_target_pairs={{2,1},{3,2},{6,5},{7,6},{10,9},{11,10},{14,13},{15,14},{18,17},{19... | collective-permute-start | bytes 5308424 | tf_op jit(solution)/shard_map/ppermute | solution.py:453
  204.3 50.4 %collective-permute-start.8 = (bf16[48,168,128]{2,1,0:T(8,128)(2,1)}, bf16[48,168,128]{2,1,0:T(8,128)(2,1)}, u32[]{:S(2)}, u32[]{:S(2)}) collective-permute-start(bf16[48,168,128]{2,1,0:T(8,128)(2,1)} %bitcast.9.refs_0_), channel_id=1, source_target_pairs={{1,0},{2,1},{3,2},{5,4},{6,5},{7,6},{9,8},{10,9},{11,10},{13,12},{... | collective-permute-start | bytes 6193160 | tf_op jit(solution)/shard_map/ppermute | solution.py:453
  236.5 24.4 %collective-permute-start.15 = (bf16[72,96,128]{2,1,0:T(8,128)(2,1)}, bf16[72,96,128]{2,1,0:T(8,128)(2,1)}, u32[]{:S(2)}, u32[]{:S(2)}) collective-permute-start(bf16[72,96,128]{2,1,0:T(8,128)(2,1)} %collective-permute-done.14.refs_1_), channel_id=1, source_target_pairs={{1,2},{2,3},{5,6},{6,7},{9,10},{10,11},{13,14},{14,15},{17,18},{18... | collective-permute-start | bytes 5308424 | tf_op jit(solution)/shard_map/ppermute | solution.py:453
  246.8 41.8 %all-to-all-start.4 = ((bf16[8,21,72,128]{3,2,1,0:T(8,128)(2,1)}), bf16[8,21,72,128]{3,2,1,0:T(8,128)(2,1)}, u32[]{:S(2)}, u32[]{:S(2)}) async-start(bf16[8,21,72,128]{3,2,1,0:T(8,128)(2,1)} %copy-done.2), calls=%async_computation.4 | async-start | bytes 6193152 | tf_op jit(solution)/shard_map/all_to_all | solution.py:444
  252.9 9.8 %collective-permute-start.9 = (bf16[72,72,128]{2,0,1:T(8,128)(2,1)S(1)}, bf16[72,72,128]{2,0,1:T(8,128)(2,1)}, u32[]{:S(2)}, u32[]{:S(2)}) collective-permute-start(bf16[72,72,128]{2,0,1:T(8,128)(2,1)S(1)} %copy.118), channel_id=1, source_target_pairs={{3,2},{7,6},{11,10},{15,14},{19,18},{23,22},{27,26},{31,30}} | collective-permute-start | bytes 3981320 | tf_op jit(solution)/shard_map/ppermute | solution.py:453
  254.7 119.7 %collective-permute-start.13 = (bf16[48,168,128]{2,1,0:T(8,128)(2,1)}, bf16[48,168,128]{2,1,0:T(8,128)(2,1)}, u32[]{:S(2)}, u32[]{:S(2)}) collective-permute-start(bf16[48,168,128]{2,1,0:T(8,128)(2,1)} %collective-permute-done.8.refs_1_), channel_id=1, source_target_pairs={{1,0},{2,1},{5,4},{6,5},{9,8},{10,9},{13,12},{14,13},{17,16},{18,1... | collective-permute-start | bytes 6193160 | tf_op jit(solution)/shard_map/ppermute | solution.py:453
  259.6 114.8 %collective-permute-start.17 = (bf16[72,96,128]{2,0,1:T(8,128)(2,1)}, bf16[72,96,128]{2,0,1:T(8,128)(2,1)}, u32[]{:S(2)}, u32[]{:S(2)}) collective-permute-start(bf16[72,96,128]{2,0,1:T(8,128)(2,1)} %add_convert_fusion), channel_id=1, source_target_pairs={{1,0},{2,1},{3,2},{5,4},{6,5},{7,6},{9,8},{10,9},{11,10},{13,12},{... | collective-permute-start | bytes 5308424 | tf_op jit(solution)/shard_map/ppermute | solution.py:453
  260.9 113.5 %collective-permute-start.16 = (bf16[72,96,128]{2,1,0:T(8,128)(2,1)}, bf16[72,96,128]{2,1,0:T(8,128)(2,1)}, u32[]{:S(2)}, u32[]{:S(2)}) collective-permute-start(bf16[72,96,128]{2,1,0:T(8,128)(2,1)} %collective-permute-done.15.refs_1_), channel_id=1, source_target_pairs={{2,3},{6,7},{10,11},{14,15},{18,19},{22,23},{26,27},{30,31}} | collective-permute-start | bytes 5308424 | tf_op jit(solution)/shard_map/ppermute | solution.py:453
  302.9 72.8 %copy-start.16 = (bf16[72,72,128]{2,1,0:T(8,128)(2,1)S(1)}, bf16[72,72,128]{2,1,0:T(8,128)(2,1)}, u32[]{:S(2)}) copy-start(bf16[72,72,128]{2,1,0:T(8,128)(2,1)} %copy-done.15) | copy-start | bytes 3981316
  303.1 78.0 %copy-start.39 = (f32[72,96,128]{2,1,0:T(8,128)S(1)}, f32[72,96,128]{2,1,0:T(8,128)}, u32[]{:S(2)}) copy-start(f32[72,96,128]{2,1,0:T(8,128)} %get-tuple-element.73) | copy-start | bytes 10616836
  303.1 77.0 %collective-permute-start.10 = (bf16[72,72,128]{2,1,0:T(8,128)(2,1)S(1)}, bf16[72,72,128]{2,1,0:T(8,128)(2,1)S(1)}, u32[]{:S(2)}, u32[]{:S(2)}) collective-permute-start(bf16[72,72,128]{2,1,0:T(8,128)(2,1)S(1)} %bitcast.114), channel_id=1, source_target_pairs={{0,1},{1,2},{2,3},{4,5},{5,6},{6,7},{8,9},{9,10},{10,11},{12,13},{... | collective-permute-start | bytes 3981320 | tf_op jit(solution)/shard_map/ppermute | solution.py:453
  374.4 47.7 %collective-permute-start.18 = (bf16[48,168,128]{2,1,0:T(8,128)(2,1)}, bf16[48,168,128]{2,1,0:T(8,128)(2,1)}, u32[]{:S(2)}, u32[]{:S(2)}) collective-permute-start(bf16[48,168,128]{2,1,0:T(8,128)(2,1)} %collective-permute-done.13.refs_2_), channel_id=1, source_target_pairs={{1,0},{5,4},{9,8},{13,12},{17,16},{21,20},{25,24},{29,28}} | collective-permute-start | bytes 6193160 | tf_op jit(solution)/shard_map/ppermute | solution.py:453
  378.4 18.7 %collective-permute-start.11 = (bf16[72,72,128]{2,0,1:T(8,128)(2,1)}, bf16[72,72,128]{2,0,1:T(8,128)(2,1)}, u32[]{:S(2)}, u32[]{:S(2)}) collective-permute-start(bf16[72,72,128]{2,0,1:T(8,128)(2,1)} %add_convert_fusion.3), channel_id=1, source_target_pairs={{2,1},{3,2},{6,5},{7,6},{10,9},{11,10},{14,13},{15,14},{18,17},{19... | collective-permute-start | bytes 3981320 | tf_op jit(solution)/shard_map/ppermute | solution.py:453
  380.1 17.0 %collective-permute-start.12 = (bf16[72,72,128]{2,1,0:T(8,128)(2,1)S(1)}, bf16[72,72,128]{2,1,0:T(8,128)(2,1)S(1)}, u32[]{:S(2)}, u32[]{:S(2)}) collective-permute-start(bf16[72,72,128]{2,1,0:T(8,128)(2,1)S(1)} %collective-permute-done.10.refs_2_), channel_id=1, source_target_pairs={{1,2},{2,3},{5,6},{6,7},{9,10},{10,11},{13,14},{14,15},{17,18},{18... | collective-permute-start | bytes 3981320 | tf_op jit(solution)/shard_map/ppermute | solution.py:453
  397.1 32.8 %copy-start.19 = (bf16[72,72,128]{2,1,0:T(8,128)(2,1)}, bf16[72,72,128]{2,1,0:T(8,128)(2,1)S(1)}, u32[]{:S(2)}) copy-start(bf16[72,72,128]{2,1,0:T(8,128)(2,1)S(1)} %collective-permute-done.12.refs_2_) | copy-start | bytes 3981316
  439.6 50.6 %all-to-all-start.5 = ((bf16[8,21,48,128]{3,2,1,0:T(8,128)(2,1)}), bf16[8,21,48,128]{3,2,1,0:T(8,128)(2,1)}, u32[]{:S(2)}, u32[]{:S(2)}) async-start(bf16[8,21,48,128]{3,2,1,0:T(8,128)(2,1)} %bitcast.129), calls=%async_computation.5 | async-start | bytes 4128768 | tf_op jit(solution)/shard_map/all_to_all | solution.py:444
  444.0 31.6 %collective-permute-start.22 = (bf16[72,72,128]{2,1,0:T(8,128)(2,1)}, bf16[72,72,128]{2,1,0:T(8,128)(2,1)S(1)}, u32[]{:S(2)}, u32[]{:S(2)}) collective-permute-start(bf16[72,72,128]{2,1,0:T(8,128)(2,1)} %copy-done.19), channel_id=1, source_target_pairs={{2,3},{6,7},{10,11},{14,15},{18,19},{22,23},{26,27},{30,31}} | collective-permute-start | bytes 3981320 | tf_op jit(solution)/shard_map/ppermute | solution.py:453
  446.7 8.8 %copy-start.18 = (bf16[72,72,128]{2,1,0:T(8,128)(2,1)S(1)}, bf16[72,72,128]{2,1,0:T(8,128)(2,1)}, u32[]{:S(2)}) copy-start(bf16[72,72,128]{2,1,0:T(8,128)(2,1)} %copy-done.17) | copy-start | bytes 3981316
  446.7 35.6 %collective-permute-start.19 = (bf16[72,72,128]{2,0,1:T(8,128)(2,1)S(1)}, bf16[72,72,128]{2,0,1:T(8,128)(2,1)S(1)}, u32[]{:S(2)}, u32[]{:S(2)}) collective-permute-start(bf16[72,72,128]{2,0,1:T(8,128)(2,1)S(1)} %add_convert_fusion.2), channel_id=1, source_target_pairs={{1,0},{2,1},{3,2},{5,4},{6,5},{7,6},{9,8},{10,9},{11,10},{13,12},{... | collective-permute-start | bytes 3981320 | tf_op jit(solution)/shard_map/ppermute | solution.py:453
  455.5 6.7 %copy-start.20 = (bf16[72,72,128]{2,1,0:T(8,128)(2,1)S(1)}, bf16[72,72,128]{2,1,0:T(8,128)(2,1)}, u32[]{:S(2)}) copy-start(bf16[72,72,128]{2,1,0:T(8,128)(2,1)} %copy-done.19) | copy-start | bytes 3981316
  462.2 6.8 %copy-start.36 = (f32[168,168]{1,0:T(8,128)}, f32[168,168]{1,0:T(8,128)S(1)}, u32[]{:S(2)}) copy-start(f32[168,168]{1,0:T(8,128)S(1)} %pairs.4) | copy-start | bytes 338692
  462.3 6.8 %copy-start.10 = (bf16[6,672,256]{2,1,0:T(8,128)(2,1)S(1)}, bf16[6,672,256]{2,1,0:T(8,128)(2,1)}, u32[]{:S(2)}) copy-start(bf16[6,672,256]{2,1,0:T(8,128)(2,1)} %get-tuple-element.74.w_ref) | copy-start | bytes 6193156
  475.6 6.8 %copy-start.7 = (bf16[48,72,128]{2,1,0:T(8,128)(2,1)S(1)}, bf16[48,72,128]{2,1,0:T(8,128)(2,1)}, u32[]{:S(2)}) copy-start(bf16[48,72,128]{2,1,0:T(8,128)(2,1)} %get-tuple-element.76.refs_2_) | copy-start | bytes 2654212
  475.6 6.8 %copy-start.8 = (bf16[48,48,128]{2,1,0:T(8,128)(2,1)S(1)}, bf16[48,48,128]{2,1,0:T(8,128)(2,1)}, u32[]{:S(2)}) copy-start(bf16[48,48,128]{2,1,0:T(8,128)(2,1)} %get-tuple-element.97.refs_0_) | copy-start | bytes 1769476
  482.3 6.2 %copy-start.43 = (bf16[72,72,128]{2,0,1:T(8,128)(2,1)}, bf16[72,72,128]{2,0,1:T(8,128)(2,1)S(1)}, u32[]{:S(2)}) copy-start(bf16[72,72,128]{2,0,1:T(8,128)(2,1)S(1)} %collective-permute-done.19) | copy-start | bytes 3981316
  490.2 5.8 copy-start.35
  490.2 8.7 %copy-start.44 = (bf16[72,72,128]{2,0,1:T(8,128)(2,1)S(1)}, bf16[72,72,128]{2,0,1:T(8,128)(2,1)}, u32[]{:S(2)}) copy-start(bf16[72,72,128]{2,0,1:T(8,128)(2,1)} %copy-done.43) | copy-start | bytes 3981316
  490.2 46.8 %all-to-all-start.6 = ((bf16[8,21,48,128]{3,2,1,0:T(8,128)(2,1)}), bf16[8,21,48,128]{3,2,1,0:T(8,128)(2,1)}, u32[]{:S(2)}, u32[]{:S(2)}) async-start(bf16[8,21,48,128]{3,2,1,0:T(8,128)(2,1)} %bitcast.128), calls=%async_computation.6 | async-start | bytes 4128768 | tf_op jit(solution)/shard_map/all_to_all | solution.py:444
  494.7 13.4 %collective-permute-start.20 = (f32[168,168]{1,0:T(8,128)S(1)}, f32[168,168]{1,0:T(8,128)S(1)}, u32[]{:S(2)}, u32[]{:S(2)}) collective-permute-start(f32[168,168]{1,0:T(8,128)S(1)} %copy-done.37), channel_id=1, source_target_pairs={{1,0},{2,1},{3,2},{5,4},{6,5},{7,6},{9,8},{10,9},{11,10},{13,12},{... | collective-permute-start | bytes 338696 | tf_op jit(solution)/shard_map/ppermute | solution.py:453
  496.0 20.4 %collective-permute-start.21 = (f32[168,168]{1,0:T(8,128)S(1)}, f32[168,168]{1,0:T(8,128)S(1)}, u32[]{:S(2)}, u32[]{:S(2)}) collective-permute-start(f32[168,168]{1,0:T(8,128)S(1)} %copy-done.35), channel_id=1, source_target_pairs={{2,0},{3,1},{6,4},{7,5},{10,8},{11,9},{14,12},{15,13},{18,16},{19,... | collective-permute-start | bytes 338696 | tf_op jit(solution)/shard_map/ppermute | solution.py:453
  497.3 19.1 %collective-permute-start.23 = (f32[168,168]{1,0:T(8,128)S(1)}, f32[168,168]{1,0:T(8,128)S(1)}, u32[]{:S(2)}, u32[]{:S(2)}) collective-permute-start(f32[168,168]{1,0:T(8,128)S(1)} %pairs.6), channel_id=1, source_target_pairs={{3,0},{7,4},{11,8},{15,12},{19,16},{23,20},{27,24},{31,28}} | collective-permute-start | bytes 338696 | tf_op jit(solution)/shard_map/ppermute | solution.py:453
  508.1 17.4 %copy-start.3 = (f32[672,672]{1,0:T(8,128)}, f32[672,672]{1,0:T(8,128)S(1)}, u32[]{:S(2)}) copy-start(f32[672,672]{1,0:T(8,128)S(1)} %match.4.rest_0_) | copy-start | bytes 5419012
  508.1 17.4 %copy-start.47 = (f32[168,168]{1,0:T(8,128)}, f32[168,168]{1,0:T(8,128)S(1)}, u32[]{:S(2)}) copy-start(f32[168,168]{1,0:T(8,128)S(1)} %collective-permute-done.20) | copy-start | bytes 338692
  516.4 9.1 %copy-start.49 = (f32[168,168]{1,0:T(8,128)}, f32[168,168]{1,0:T(8,128)S(1)}, u32[]{:S(2)}) copy-start(f32[168,168]{1,0:T(8,128)S(1)} %collective-permute-done.21) | copy-start | bytes 338692
  516.4 9.1 %copy-start.51 = (f32[168,168]{1,0:T(8,128)}, f32[168,168]{1,0:T(8,128)S(1)}, u32[]{:S(2)}) copy-start(f32[168,168]{1,0:T(8,128)S(1)} %collective-permute-done.23) | copy-start | bytes 338692
  536.9 51.7 %all-to-all-start.7 = ((bf16[8,21,72,128]{3,2,1,0:T(8,128)(2,1)}), bf16[8,21,72,128]{3,2,1,0:T(8,128)(2,1)}, u32[]{:S(2)}, u32[]{:S(2)}) async-start(bf16[8,21,72,128]{3,2,1,0:T(8,128)(2,1)} %bitcast.126), calls=%async_computation.7 | async-start | bytes 6193152 | tf_op jit(solution)/shard_map/all_to_all | solution.py:444
  551.4 5.6 copy-start.30
  551.4 5.6 copy-start.48
  551.4 5.6 copy-start.50
  551.4 5.6 copy-start.52
  553.1 11.0 %collective-permute-start.24 = (bf16[672,168]{0,1:T(8,128)(2,1)S(1)}, bf16[672,168]{0,1:T(8,128)(2,1)S(1)}, u32[]{:S(2)}, u32[]{:S(2)}) collective-permute-start(bf16[672,168]{0,1:T(8,128)(2,1)S(1)} %get-tuple-element.98), channel_id=1, source_target_pairs={{0,1},{1,2},{2,3},{3,0},{4,5},{5,6},{6,7},{7,4},{8,9},{9,10},{10,1... | collective-permute-start | bytes 677384 | tf_op jit(solution)/shard_map/ppermute | solution.py:453
  553.1 16.7 %collective-permute-start.26 = (bf16[672,168]{0,1:T(8,128)(2,1)S(1)}, bf16[672,168]{0,1:T(8,128)(2,1)S(1)}, u32[]{:S(2)}, u32[]{:S(2)}) collective-permute-start(bf16[672,168]{0,1:T(8,128)(2,1)S(1)} %get-tuple-element.99), channel_id=1, source_target_pairs={{0,3},{1,0},{2,1},{3,2},{4,7},{5,4},{6,5},{7,6},{8,11},{9,8},{10,9... | collective-permute-start | bytes 677384 | tf_op jit(solution)/shard_map/ppermute | solution.py:453
  557.0 20.7 %collective-permute-start.25 = (bf16[672,168]{0,1:T(8,128)(2,1)S(1)}, bf16[672,168]{0,1:T(8,128)(2,1)}, u32[]{:S(2)}, u32[]{:S(2)}) collective-permute-start(bf16[672,168]{0,1:T(8,128)(2,1)S(1)} %get-tuple-element.100), channel_id=1, source_target_pairs={{0,2},{1,3},{2,0},{3,1},{4,6},{5,7},{6,4},{7,5},{8,10},{9,11},{10,... | collective-permute-start | bytes 677384 | tf_op jit(solution)/shard_map/ppermute | solution.py:453
  589.8 19.6 %all-to-all-start.8 = ((f32[8,84,336]{2,1,0:T(8,128)}), f32[8,84,336]{2,1,0:T(8,128)S(1)}, u32[]{:S(2)}, u32[]{:S(2)}) async-start(f32[8,84,336]{2,1,0:T(8,128)} %copy.147), calls=%async_computation.8 | async-start | bytes 2162688 | tf_op jit(solution)/shard_map/all_to_all | solution.py:444
  (26 other events, 65.1 us)

commit v2 on v1

--- a/solution.py
+++ b/solution.py
@@ -529,84 +529,94 @@
     ups_last = [v_last[-1]]
     for step in range(1, cols):
         ups_last.append(up(ups_last[-1], step))
-    for back in range(later - 1, 0, -1):
+    for back in range(later - 1, 1, -1):
         sums[0] = hop(0, back)
     if later:
         sums[1] = hop(1, later)
     early = sums[1]
-    for back in range(later - 1, 0, -1):
+    for back in range(later - 1, 1, -1):
         sums[1] = hop(1, back)
     for step in range(2, cols):
         held = seconds[-1]
         if step == last:
-            held = after(held, v_last[-1], ups_first[last], sums[0])
+            held = after(held, v_last[-1], ups_first[1])
         seconds.append(down(held, step))
+
     bits = [(0, 0, half), (0, half, unit), (1, unit, span_two)]
-    ends = [sums[q][:, lo - cuts[q][0] : hi - cuts[q][0]] for q, lo, hi in bits]
+    ends = []
+    if later > 1:
+        sums = [add(sums[q], own[1][q]) for q in range(2)]
+    for q, lo, hi in bits:
+        held = sums[q][:, lo - cuts[q][0] : hi - cuts[q][0]]
+        if later > 1:
+            held = after(held, ends[0] if ends else seconds[-2])
+            held = move(held, [(c, c - 1) for c in range(1, cols)])
+        ends.append(held)
+
+    def second_factor(met, sent, grad_near):
+        two = [grad_near[d] + (sent[d - 1] if d else met[0]) for d in range(cols)]
+        two = jnp.concatenate(two, axis=0)
+        two = jnp.pad(two, ((order_two - span_two, 0), (0, 0)))
+        two = lax.dynamic_slice(
+            two, (order_two - span_two - place * span_two, 0), (order_two, span_two)
+        )
+        return two.reshape(rows, order_two // rows, span_two)
+
+    met = [pairs(far_part, [ups_first[d], ups_last[d]], per) for d in range(cols)]
+    sent = [move(met[d], [(c, c - d) for c in range(d, cols)]) for d in range(1, cols)]
 
     w_near, grad_near = [], 0.0
     for g, chunk in enumerate((firsts, seconds)):
         held = [chunk[0]] + chunk[1:]
         if g:
-            held[0] = after(held[0], early, ups_last[min(2, last)])
+            held[0] = after(held[0], early, met[min(2, last)], ups_first[last])
         else:
-            held[0] = after(held[0], ups_last[1])
+            held[0] = after(held[0], met[0], met[1])
         *w, grad = gathered(held, [v_first[g], v_last[g]], mix_near, cuts, per)
         w_near.append(w)
         grad_near = grad_near + grad
-
-    two, met, sent = [], [], []
-    for d in range(cols):
-        grad = pairs(far_part, [ups_first[d], ups_last[d]], per)
-        met.append(grad)
-        if d:
-            grad = move(grad, [(c, c - d) for c in range(d, cols)])
-            sent.append(grad)
-        two.append(grad_near[d] + grad)
-    two = jnp.concatenate(two, axis=0)
-    two = jnp.pad(two, ((order_two - span_two, 0), (0, 0)))
-    two = lax.dynamic_slice(
-        two, (order_two - span_two - place * span_two, 0), (order_two, span_two)
-    )
-    two = two.reshape(rows, order_two // rows, span_two)
-
-    grad_latent, one, moved, written = None, None, [], []
+    one, moved = None, []
     for n, (q, lo, hi) in enumerate(bits):
         own_here = own[0][q][:, lo - cuts[q][0] : hi - cuts[q][0]]
         share = turn(add(ends[n], own_here))
-        if n == 1:
-            share = after(share, *met, sums[1], one)
-        elif n == 2:
-            share = after(share, *sent, one)
+        if n == 0:
+            share = after(share, ends[2])
+        else:
+            share = after(share, one, *sent[:2])
         parts = [turn(w[q][:, lo - cuts[q][0] : hi - cuts[q][0]]) for w in w_near] + [share]
         grad, w_y = finish(parts, left_t, fold)
         one = match(w_y, y_last if q else y_first, (lo - cuts[q][0]) // (2 * fold), one)
         grad = turn(grad).reshape(rows, tiles, hi - lo, LANES)
-        moved = [exchange(after(grad, *moved, *written[:-1]))]
-        where = (lo, hi, half if q == 0 else unit)
-        grad_latent = unpack(moved[0], swap, latent.shape, where, grad_latent)
-        written.append(grad_latent)
+        moved.append(exchange(after(grad, *moved[-1:])))
 
     one = dot(one.astype(BF16), pick_latent).astype(BF16)
-    one = jnp.transpose(one.reshape(order_one, cols, order_one // cols), (1, 0, 2))
-    total = lax.dynamic_index_in_dim(one, place, 0, keepdims=False).astype(F32)
+    one = one.reshape(fold, rows * tiles, order_one)
+    one = jnp.concatenate(
+        [
+            one[:, rows * lo : rows * hi].reshape(fold, rows, hi - lo, order_one)
+            for lo, hi in groups
+        ],
+        axis=2,
+    )
+    one = jnp.transpose(one, (1, 2, 0, 3)).reshape(rows, span_one, order_one)
+    where = [(lo, hi, half if q == 0 else unit) for q, lo, hi in bits]
+    grad_latent = unpack(moved[0], swap, latent.shape, where[0], None)
+    grad_latent = unpack(moved[1], swap, latent.shape, where[1], grad_latent)
+    one, grad_latent = lax.optimization_barrier((one, grad_latent))
+    one = exchange(after(one, moved[2], ups_last[last]))
+    grad_latent = unpack(moved[2], swap, latent.shape, where[2], grad_latent)
+    one = one.astype(F32).sum(0)
+    one = jnp.transpose(one.reshape(span_one, cols, order_one // cols), (1, 0, 2))
+    total = lax.dynamic_index_in_dim(one, place, 0, keepdims=False)
     for d in range(1, cols):
         ring = [(c, (c + d) % cols) for c in range(cols)]
         mine = lax.dynamic_index_in_dim(one, (place + d) % cols, 0, keepdims=False)
-        total = total + move(mine, ring).astype(F32)
-    total = total.reshape(fold, rows * tiles, order_one // cols)
-    total = jnp.concatenate(
-        [
-            total[:, rows * lo : rows * hi].reshape(fold, rows, hi - lo, order_one // cols)
-            for lo, hi in groups
-        ],
-        axis=2,
-    )
-    total = jnp.transpose(total, (1, 2, 0, 3)).reshape(rows, span_one, order_one // cols)
-    total = jnp.concatenate([total, two], axis=2)
-    total = exchange(after(total, *moved, written[-2])).sum(0)
-    grad_one = keep_lower(total[:, : order_one // cols], depth)
-    grad_two = keep_lower(total[:, order_one // cols :], depth)
+        total = total + move(mine, ring)
+    grad_one = keep_lower(total, depth)
+    sent[-1], grad_latent = lax.optimization_barrier((sent[-1], grad_latent))
+    two = second_factor(met, sent, grad_near)
+    two = exchange(after(two, one)).sum(0)
+    grad_two = keep_lower(two, depth)
     return (grad_latent, grad_one, grad_two)
 
 

time: 623 us -> 588 us (0.944)
  waiting for transfers between devices: 260 us -> 215 us
  starting transfers between devices: 93.6 us -> 101 us
  local copies, waits for them, and re-layouts: 58.3 us -> 65.4 us
    ppermute x27 -> x28, waiting for transfers between devices: 204 us -> 180 us  [move(): return lax.ppermute(value, 'col', pairs_of)]
    all_to_all x9 -> x10, waiting for transfers between devices: 55.2 us -> 34.8 us  [exchange(): return lax.all_to_all(value, 'row', split_axis=0, concat_axis=0, tiled=True)]
    all_to_all x9 -> x10, starting transfers between devices: 40.8 us -> 45.5 us  [exchange(): return lax.all_to_all(value, 'row', split_axis=0, concat_axis=0, tiled=True)]
    unnamed x112 -> x123, local copies, waits for them, and re-layouts: 15.9 us -> 20.4 us
    ppermute x27 -> x28, starting transfers between devices: 52.7 us -> 55.9 us  [move(): return lax.ppermute(value, 'col', pairs_of)]
  transfers between devices with their start and end apart: 36 -> 38, of which waited for: 14 -> 19; matrix products, arithmetic and copies ran while one was open for 12% -> 12% of each run, Pallas kernels for 24% -> 27%
where the time goes in v2:
time: 588 us; the launch traced here: 577 us
  waiting for transfers between devices  215 us (37%)
  Pallas kernels  164 us (28%)
  starting transfers between devices  101 us (17%)
  local copies, waits for them, and re-layouts  65.4 us (11%)
  other arithmetic  22.1 us (4%)
  matrix products  7.08 us (1%)
    ppermute x28, waiting for transfers between devices, move(): return lax.ppermute(value, 'col', pairs_of)  180 us
    ppermute x28, starting transfers between devices, move(): return lax.ppermute(value, 'col', pairs_of)  55.9 us
    all_to_all x10, starting transfers between devices, exchange(): return lax.all_to_all(value, 'row', split_axis=0, concat_axis=0, tiled=True)  45.5 us
    all_to_all x10, waiting for transfers between devices, exchange(): return lax.all_to_all(value, 'row', split_axis=0, concat_axis=0, tiled=True)  34.8 us
    pallas_call x4, Pallas kernels, pairs(): pl.pallas_call(kernel, grid=(tiles // per,), in_specs=[spec(span_two)] +...  26.9 us
    pallas_call x5, Pallas kernels, pack(): pl.pallas_call(kernel, grid=(count // per,), in_specs=[pl.BlockSpec((per...  25.3 us
    pallas_call x2, Pallas kernels, raise_field(): pl.pallas_call(kernel, grid=(count,), in_specs=[pl.BlockSpec((step,) + fi...  23.6 us
    pallas_call x3, Pallas kernels, unpack(): pl.pallas_call(kernel, grid=(tiles // per,), in_specs=[pl.BlockSpec((rows...  23.3 us
  transfers between devices with their start and end apart: 38, of which 19 were waited for; matrix products, arithmetic and copies ran while one was open for 12% of the time, Pallas kernels for 27%

profile of v2, /device:TPU:0, one launch (start us, length us, event | category | flops | bytes accessed | tf_op | source)
XLA Modules:
  0.0 576.9 jit_solution(9508077901153436417)
XLA Ops:
  1.7 3.7 pack.6
  5.4 5.3 all-to-all-start
  15.1 4.1 pack.5
  20.8 3.8 collective-permute-done.1
  24.7 12.3 %all-to-all-done = bf16[8,6,168,128]{3,2,1,0:T(8,128)(2,1)S(1)} async-done(((bf16[8,6,168,128]{3,2,1,0:T(8,128)(2,1)}), bf16[8,6,168,128]{3,2,1,0:T(8,128)(2,1)S(1)}, u32[]{:S(2)}, u32[]{:S(2)}) %all-to-all-start) | async-done | bytes 2064416 | tf_op jit(solution)/shard_map/all_to_all | solution.py:444
  37.0 4.5 all-to-all-start.1
  42.9 7.0 %pack.7 = bf16[8,21,96,128]{3,2,1,0:T(8,128)(2,1)S(1)} custom-call(bf16[84,168,256]{2,1,0:T(8,128)(2,1)} %x_ref.8, bf16[512,512]{1,0:T(8,128)(2,1)S(1)} %fusion.63.p_ref), custom_call_target="tpu_custom_call" | custom-call | flops 1 | bytes 1 | tf_op jit(solution)/shard_map/pack/pallas_call | solution.py:138
  52.3 4.9 pad_maximum_fusion
  57.2 33.6 %collective-permute-done.3.refs_1_ = bf16[48,168,128]{2,1,0:T(8,128)(2,1)} collective-permute-done((bf16[48,168,128]{2,1,0:T(8,128)(2,1)S(1)}, bf16[48,168,128]{2,1,0:T(8,128)(2,1)}, u32[]{:S(2)}, u32[]{:S(2)}) %collective-permute-start.3) | collective-permute-done | bytes 2064416 | tf_op jit(solution)/shard_map/ppermute | solution.py:453
  90.8 4.7 all-to-all-start.2
  97.1 9.3 %shares.1 = (f32[72,96,128]{2,1,0:T(8,128)}, f32[72,72,128]{2,1,0:T(8,128)}, bf16[72,96,128]{2,1,0:T(8,128)(2,1)S(1)}, bf16[72,72,128]{2,1,0:T(8,128)(2,1)S(1)},...) custom-call(bf16[72,168,128]{2,1,0:T(8,128)(2,1)} %bitcast.6.c_ref.r, ...), custom_call_target="tpu_custom_call" | custom-call | flops 1 | bytes 1 | tf_op jit(solution)/shard_map/shares/pallas_call | solution.py:406
  108.7 3.1 copy.121
  112.7 3.7 pack.9
  116.6 28.3 %collective-permute-done.7.refs_2_ = bf16[48,168,128]{2,1,0:T(8,128)(2,1)} collective-permute-done((bf16[48,168,128]{2,1,0:T(8,128)(2,1)}, bf16[48,168,128]{2,1,0:T(8,128)(2,1)}, u32[]{:S(2)}, u32[]{:S(2)}) %collective-permute-start.7) | collective-permute-done | bytes 2064416 | tf_op jit(solution)/shard_map/ppermute | solution.py:453
  150.0 4.4 all-to-all-done.2
  154.4 4.9 slice.103
  159.3 4.5 all-to-all-start.3
  166.9 3.7 fusion.52.clone.5
  173.4 5.7 copy.184
  179.1 13.2 %raise_field.2 = (bf16[12,672,256]{2,1,0:T(8,128)(2,1)}, bf16[96,48,128]{2,1,0:T(8,128)(2,1)S(1)}, bf16[96,48,128]{2,1,0:T(8,128)(2,1)S(1)}, bf16[96,72,128]{2,1,0:T(8,128)(2,1)S(1)}) custom-call(bf16[96,168,128]{2,1,0:T(8,128)(2,1)} %bitcast.130, bf16[672,672]{1,0:T(8,128)(2,1)S(1)} %copy.119.l_ref), custom_call_target="tpu_custom_call" | custom-call | flops 1 | bytes 1 | tf_op jit(solution)/shard_map/raise_field/pallas_call | solution.py:230
  197.3 6.9 %pack.8 = bf16[8,21,72,128]{3,2,1,0:T(8,128)(2,1)S(1)} custom-call(bf16[84,168,256]{2,1,0:T(8,128)(2,1)} %x_ref.8, bf16[512,512]{1,0:T(8,128)(2,1)S(1)} %fusion.63.p_ref), custom_call_target="tpu_custom_call" | custom-call | flops 1 | bytes 1 | tf_op jit(solution)/shard_map/pack/pallas_call | solution.py:138
  205.8 4.4 all-to-all-start.4
  210.3 5.8 %collective-permute-start.4 = (bf16[72,96,128]{2,1,0:T(8,128)(2,1)}, bf16[72,96,128]{2,1,0:T(8,128)(2,1)}, u32[]{:S(2)}, u32[]{:S(2)}) collective-permute-start(bf16[72,96,128]{2,1,0:T(8,128)(2,1)} %bitcast.118), channel_id=1, source_target_pairs={{0,1},{1,2},{2,3},{4,5},{5,6},{6,7},{8,9},{9,10},{10,11},{12,13},{... | collective-permute-start | bytes 5308424 | tf_op jit(solution)/shard_map/ppermute | solution.py:453
  219.3 26.2 %collective-permute-done.11.refs_1_ = bf16[48,168,128]{2,1,0:T(8,128)(2,1)} collective-permute-done((bf16[48,168,128]{2,1,0:T(8,128)(2,1)}, bf16[48,168,128]{2,1,0:T(8,128)(2,1)}, u32[]{:S(2)}, u32[]{:S(2)}) %collective-permute-start.11) | collective-permute-done | bytes 2064416 | tf_op jit(solution)/shard_map/ppermute | solution.py:453
  246.8 6.8 %collective-permute-done.4.refs_1_ = bf16[72,96,128]{2,1,0:T(8,128)(2,1)} collective-permute-done((bf16[72,96,128]{2,1,0:T(8,128)(2,1)}, bf16[72,96,128]{2,1,0:T(8,128)(2,1)}, u32[]{:S(2)}, u32[]{:S(2)}) %collective-permute-start.4) | collective-permute-done | bytes 1769504 | tf_op jit(solution)/shard_map/ppermute | solution.py:453
  255.4 3.9 copy.185
  259.3 10.3 %raise_field.3 = (bf16[9,672,256]{2,1,0:T(8,128)(2,1)}, bf16[72,48,128]{2,1,0:T(8,128)(2,1)S(1)}, bf16[72,48,128]{2,1,0:T(8,128)(2,1)S(1)}, bf16[72,72,128]{2,1,0:T(8,128)(2,1)S(1)}) custom-call(bf16[72,168,128]{2,1,0:T(8,128)(2,1)} %bitcast.133, bf16[672,672]{1,0:T(8,128)(2,1)S(1)} %copy.119.l_ref), custom_call_target="tpu_custom_call" | custom-call | flops 1 | bytes 1 | tf_op jit(solution)/shard_map/raise_field/pallas_call | solution.py:230
  269.8 15.9 %collective-permute-start.13 = (bf16[72,72,128]{2,1,0:T(8,128)(2,1)S(1)}, bf16[72,72,128]{2,1,0:T(8,128)(2,1)}, u32[]{:S(2)}, u32[]{:S(2)}) collective-permute-start(bf16[72,72,128]{2,1,0:T(8,128)(2,1)S(1)} %bitcast.120), channel_id=1, source_target_pairs={{0,1},{1,2},{2,3},{4,5},{5,6},{6,7},{8,9},{9,10},{10,11},{12,13},{... | collective-permute-start | bytes 3981320 | tf_op jit(solution)/shard_map/ppermute | solution.py:453
  288.1 2.2 add_convert_fusion
  290.5 9.9 %collective-permute-done.18.refs_2_ = bf16[48,168,128]{2,1,0:T(8,128)(2,1)} collective-permute-done((bf16[48,168,128]{2,1,0:T(8,128)(2,1)}, bf16[48,168,128]{2,1,0:T(8,128)(2,1)}, u32[]{:S(2)}, u32[]{:S(2)}) %collective-permute-start.18) | collective-permute-done | bytes 2064416 | tf_op jit(solution)/shard_map/ppermute | solution.py:453
  303.8 8.8 %collective-permute-done.13.refs_2_ = bf16[72,72,128]{2,1,0:T(8,128)(2,1)} collective-permute-done((bf16[72,72,128]{2,1,0:T(8,128)(2,1)S(1)}, bf16[72,72,128]{2,1,0:T(8,128)(2,1)}, u32[]{:S(2)}, u32[]{:S(2)}) %collective-permute-start.13) | collective-permute-done | bytes 1327136 | tf_op jit(solution)/shard_map/ppermute | solution.py:453
  313.3 15.4 %collective-permute-done.20 = bf16[72,48,128]{2,0,1:T(8,128)(2,1)S(1)} collective-permute-done((bf16[72,48,128]{2,0,1:T(8,128)(2,1)S(1)}, bf16[72,48,128]{2,0,1:T(8,128)(2,1)S(1)}, u32[]{:S(2)}, u32[]{:S(2)}) %collective-permute-start.20) | collective-permute-done | bytes 884768 | tf_op jit(solution)/shard_map/ppermute | solution.py:453
  332.9 3.9 copy.139
  338.5 6.3 %pairs.5 = f32[168,168]{1,0:T(8,128)S(1)} custom-call(bf16[72,168,128]{2,1,0:T(8,128)(2,1)} %bitcast.6.c_ref.refs_0_, bf16[72,96,128]{2,1,0:T(8,128)(2,1)S(1)} %bitcast.119, bf16[72,72,128]{2,1,0:T(8,128)(2,1)S(1)} %bitcast.121), custom_call_target="tpu_custom_call" | custom-call | flops 1 | bytes 1 | tf_op jit(solution)/shard_map/pairs/pallas_call | solution.py:372
  345.4 7.0 %pairs.6 = f32[168,168]{1,0:T(8,128)S(1)} custom-call(bf16[72,168,128]{2,1,0:T(8,128)(2,1)} %bitcast.6.c_ref.refs_0_, bf16[72,96,128]{2,1,0:T(8,128)(2,1)} %collective-permute-done.4.refs_1_, bf16[72,72,128]{2,1,0:T(8,128)(2,1)} %collective-permute-done.13.refs_2_), custom_call_target="tpu_custom_call" | custom-call | flops 1 | bytes 1 | tf_op jit(solution)/shard_map/pairs/pallas_call | solution.py:372
  352.4 7.9 %gathered.2 = (bf16[48,96,128]{2,1,0:T(8,128)(2,1)S(1)}, bf16[48,72,128]{2,1,0:T(8,128)(2,1)S(1)}, f32[4,168,168]{2,1,0:T(8,128)S(1)}) custom-call(bf16[48,168,128]{2,1,0:T(8,128)(2,1)} %bitcast.137, bf16[48,168,128]{2,1,0:T(8,128)(2,1)} %collective-permute-done.3.refs_1_, bf16[48,168,128]{2,1,0:T(8,128)(2,1)} %collective-permute-done.7.refs_2_, ...), custom_call_target="tpu_custom_call" | custom-call | flops 1 | bytes 1 | tf_op jit(solution)/shard_map/gathered/pallas_call | solution.py:342
  361.5 7.1 %pairs.7 = f32[168,168]{1,0:T(8,128)S(1)} custom-call(bf16[72,168,128]{2,1,0:T(8,128)(2,1)} %bitcast.6.c_ref.refs_0_, bf16[72,96,128]{2,1,0:T(8,128)(2,1)} %collective-permute-done.5.refs_1_, bf16[72,72,128]{2,1,0:T(8,128)(2,1)S(1)} %collective-permute-done.14.refs_2_), custom_call_target="tpu_custom_call" | custom-call | flops 1 | bytes 1 | tf_op jit(solution)/shard_map/pairs/pallas_call | solution.py:372
  368.7 23.3 %collective-permute-done.22 = bf16[72,48,128]{2,0,1:T(8,128)(2,1)} collective-permute-done((bf16[72,48,128]{2,0,1:T(8,128)(2,1)S(1)}, bf16[72,48,128]{2,0,1:T(8,128)(2,1)}, u32[]{:S(2)}, u32[]{:S(2)}) %collective-permute-start.22) | collective-permute-done | bytes 884768 | tf_op jit(solution)/shard_map/ppermute | solution.py:453
  392.0 2.6 fusion.104
  394.6 7.8 %gathered.3 = (bf16[48,96,128]{2,1,0:T(8,128)(2,1)S(1)}, bf16[48,72,128]{2,1,0:T(8,128)(2,1)S(1)}, f32[4,168,168]{2,1,0:T(8,128)S(1)}) custom-call(bf16[48,168,128]{2,1,0:T(8,128)(2,1)} %bitcast.12.refs_0_, bf16[48,168,128]{2,1,0:T(8,128)(2,1)} %collective-permute-done.11.refs_1_, bf16[48,168,128]{2,1,0:T(8,128)(2,1)} %collective-permute-done.18.refs_2_, ...), custom_call_target="tpu_custom_call" | custom-call | flops 1 | bytes 1 | tf_op jit(solution)/shard_map/gathered/pallas_call | solution.py:342
  403.8 15.4 %collective-permute-done.21 = bf16[72,72,128]{2,0,1:T(8,128)(2,1)S(1)} collective-permute-done((bf16[72,72,128]{2,0,1:T(8,128)(2,1)}, bf16[72,72,128]{2,0,1:T(8,128)(2,1)S(1)}, u32[]{:S(2)}, u32[]{:S(2)}) %collective-permute-start.21) | collective-permute-done | bytes 1327136 | tf_op jit(solution)/shard_map/ppermute | solution.py:453
  419.2 6.2 %finish.3 = (bf16[48,168,128]{2,1,0:T(8,128)(2,1)S(1)}, bf16[6,672,256]{2,1,0:T(8,128)(2,1)}) custom-call(bf16[48,48,128]{2,1,0:T(8,128)(2,1)S(1)} %get-tuple-element.111.refs_0_, bf16[48,48,128]{2,1,0:T(8,128)(2,1)S(1)} %get-tuple-element.109.refs_1_, bf16[48,72,128]{2,1,0:T(8,128)(2,1)S(1)} %get-tuple-element.85.refs_2_, bf16[672,672]{1,0:T(8,128)(2,1)S(1)} %bitcast.115), custom_call_target="tpu_custom_call" | custom-call | flops 1 | bytes 1 | tf_op jit(solution)/shard_map/finish/pallas_call | solution.py:260
  427.0 4.5 all-to-all-start.5
  435.7 5.1 match.3.rest_0_
  442.1 5.7 collective-permute-done.24
  447.8 6.2 %finish.4 = (bf16[48,168,128]{2,1,0:T(8,128)(2,1)S(1)}, bf16[6,672,256]{2,1,0:T(8,128)(2,1)}) custom-call(bf16[48,48,128]{2,1,0:T(8,128)(2,1)S(1)} %get-tuple-element.112.refs_0_, bf16[48,48,128]{2,1,0:T(8,128)(2,1)S(1)} %copy-done.8, bf16[48,72,128]{2,1,0:T(8,128)(2,1)S(1)} %get-tuple-element.88.refs_2_, bf16[672,672]{1,0:T(8,128)(2,1)S(1)} %bitcast.116), custom_call_target="tpu_custom_call" | custom-call | flops 1 | bytes 1 | tf_op jit(solution)/shard_map/finish/pallas_call | solution.py:260
  455.6 2.1 all-to-all-done.5.x_ref
  457.8 4.7 all-to-all-start.6
  465.9 5.2 match.4.rest_0_
  472.4 9.1 %finish.5 = (bf16[72,168,128]{2,1,0:T(8,128)(2,1)}, bf16[9,672,256]{2,1,0:T(8,128)(2,1)}) custom-call(bf16[72,48,128]{2,1,0:T(8,128)(2,1)S(1)} %bitcast.125, bf16[72,48,128]{2,1,0:T(8,128)(2,1)S(1)} %bitcast.126, bf16[72,72,128]{2,1,0:T(8,128)(2,1)S(1)} %fusion.53.refs_2_, bf16[672,672]{1,0:T(8,128)(2,1)S(1)} %bitcast.117), custom_call_target="tpu_custom_call" | custom-call | flops 1 | bytes 1 | tf_op jit(solution)/shard_map/finish/pallas_call | solution.py:260
  481.5 4.0 copy.143
  485.5 3.3 all-to-all-done.6.x_ref
  488.8 4.6 all-to-all-start.7
  494.2 8.0 %match.5 = f32[672,672]{1,0:T(8,128)S(1)} custom-call(bf16[9,672,256]{2,1,0:T(8,128)(2,1)} %get-tuple-element.96.w_ref, bf16[9,672,256]{2,1,0:T(8,128)(2,1)} %get-tuple-element.97.z_ref, f32[672,672]{1,0:T(8,128)S(1)} %copy-done.4), custom_call_target="tpu_custom_call" | custom-call | flops 1 | bytes 1 | tf_op jit(solution)/shard_map/match/pallas_call | solution.py:290
  505.1 7.6 %unpack.3.rest_0_ = bf16[84,168,256]{2,1,0:T(8,128)(2,1)} custom-call(bf16[8,21,48,128]{3,2,1,0:T(8,128)(2,1)} %all-to-all-done.5.x_ref, bf16[512,512]{1,0:T(8,128)(2,1)S(1)} %fusion.63.p_ref), custom_call_target="tpu_custom_call" | custom-call | flops 1 | bytes 1 | tf_op jit(solution)/shard_map/unpack/pallas_call | solution.py:174
  512.8 7.6 %unpack.4.rest_0_ = bf16[84,168,256]{2,1,0:T(8,128)(2,1)} custom-call(bf16[8,21,48,128]{3,2,1,0:T(8,128)(2,1)} %all-to-all-done.6.x_ref, bf16[512,512]{1,0:T(8,128)(2,1)S(1)} %fusion.63.p_ref, bf16[84,168,256]{2,1,0:T(8,128)(2,1)} %unpack.3.rest_0_), custom_call_target="tpu_custom_call", output_to_operand_aliasing={{}: (2, {})} | custom-call | flops 1 | bytes 1 | tf_op jit(solution)/shard_map/unpack/pallas_call | solution.py:174
  521.4 9.3 %all-to-all-done.7.x_ref = bf16[8,21,72,128]{3,2,1,0:T(8,128)(2,1)} async-done(((bf16[8,21,72,128]{3,2,1,0:T(8,128)(2,1)}), bf16[8,21,72,128]{3,2,1,0:T(8,128)(2,1)}, u32[]{:S(2)}, u32[]{:S(2)}) %all-to-all-start.7) | async-done | bytes 3096608 | tf_op jit(solution)/shard_map/all_to_all | solution.py:444
  531.9 4.2 all-to-all-start.8
  537.6 6.4 %pairs.4 = f32[168,168]{1,0:T(8,128)S(1)} custom-call(bf16[72,168,128]{2,1,0:T(8,128)(2,1)} %bitcast.6.c_ref.refs_0_, bf16[72,96,128]{2,1,0:T(8,128)(2,1)S(1)} %copy-done.12, bf16[72,72,128]{2,1,0:T(8,128)(2,1)S(1)} %copy-done.22), custom_call_target="tpu_custom_call" | custom-call | flops 1 | bytes 1 | tf_op jit(solution)/shard_map/pairs/pallas_call | solution.py:372
  546.5 8.1 %unpack.5 = bf16[84,168,256]{2,1,0:T(8,128)(2,1)} custom-call(bf16[8,21,72,128]{3,2,1,0:T(8,128)(2,1)} %all-to-all-done.7.x_ref, bf16[512,512]{1,0:T(8,128)(2,1)S(1)} %fusion.63.p_ref, bf16[84,168,256]{2,1,0:T(8,128)(2,1)} %unpack.4.rest_0_), custom_call_target="tpu_custom_call", output_to_operand_aliasing={{}: (2, {})} | custom-call | flops 1 | bytes 1 | tf_op jit(solution)/shard_map/unpack/pallas_call | solution.py:174
  557.2 4.1 all-to-all-start.9
  564.2 5.1 collective-permute-start.26
  569.5 3.4 all-to-all-done.9
  573.0 2.5 collective-permute-done.26
  (233 shorter events, 85.0 us)
Async XLA Ops:
  5.4 31.6 %all-to-all-start = ((bf16[8,6,168,128]{3,2,1,0:T(8,128)(2,1)}), bf16[8,6,168,128]{3,2,1,0:T(8,128)(2,1)S(1)}, u32[]{:S(2)}, u32[]{:S(2)}) async-start(bf16[8,6,168,128]{3,2,1,0:T(8,128)(2,1)} %pack.6), calls=%async_computation | async-start | bytes 4128768 | tf_op jit(solution)/shard_map/all_to_all | solution.py:444
  11.2 9.6 %collective-permute-start = (bf16[168,168]{1,0:T(8,128)(2,1)S(1)}, bf16[168,168]{1,0:T(8,128)(2,1)S(1)}, u32[]{:S(2)}, u32[]{:S(2)}) collective-permute-start(bf16[168,168]{1,0:T(8,128)(2,1)S(1)} %get-tuple-element.126), channel_id=1, source_target_pairs={{1,0},{2,1},{3,2},{5,4},{6,5},{7,6},{9,8},{10,9},{11,10},{13,12},{... | collective-permute-start | bytes 169352 | tf_op jit(solution)/shard_map/ppermute | solution.py:453
  12.5 12.1 %collective-permute-start.1 = (bf16[168,168]{1,0:T(8,128)(2,1)S(1)}, bf16[168,168]{1,0:T(8,128)(2,1)S(1)}, u32[]{:S(2)}, u32[]{:S(2)}) collective-permute-start(bf16[168,168]{1,0:T(8,128)(2,1)S(1)} %get-tuple-element.125), channel_id=1, source_target_pairs={{2,0},{3,1},{6,4},{7,5},{10,8},{11,9},{14,12},{15,13},{18,16},{19,... | collective-permute-start | bytes 169352 | tf_op jit(solution)/shard_map/ppermute | solution.py:453
  13.8 10.8 %collective-permute-start.2 = (bf16[168,168]{1,0:T(8,128)(2,1)S(1)}, bf16[168,168]{1,0:T(8,128)(2,1)S(1)}, u32[]{:S(2)}, u32[]{:S(2)}) collective-permute-start(bf16[168,168]{1,0:T(8,128)(2,1)S(1)} %get-tuple-element.124), channel_id=1, source_target_pairs={{3,0},{7,4},{11,8},{15,12},{19,16},{23,20},{27,24},{31,28}} | collective-permute-start | bytes 169352 | tf_op jit(solution)/shard_map/ppermute | solution.py:453
  37.0 53.8 %all-to-all-start.1 = ((bf16[8,9,168,128]{3,2,1,0:T(8,128)(2,1)}), bf16[8,9,168,128]{3,2,1,0:T(8,128)(2,1)}, u32[]{:S(2)}, u32[]{:S(2)}) async-start(bf16[8,9,168,128]{3,2,1,0:T(8,128)(2,1)} %copy-done.1), calls=%async_computation.1 | async-start | bytes 6193152 | tf_op jit(solution)/shard_map/all_to_all | solution.py:444
  41.5 10.4 %copy-start.50 = (bf16[84,672]{1,0:T(8,128)(2,1)S(1)}, bf16[84,672]{1,0:T(8,128)(2,1)}, u32[]{:S(2)}) copy-start(bf16[84,672]{1,0:T(8,128)(2,1)} %param.6) | copy-start | bytes 338692
  41.5 49.3 %collective-permute-start.3 = (bf16[48,168,128]{2,1,0:T(8,128)(2,1)S(1)}, bf16[48,168,128]{2,1,0:T(8,128)(2,1)}, u32[]{:S(2)}, u32[]{:S(2)}) collective-permute-start(bf16[48,168,128]{2,1,0:T(8,128)(2,1)S(1)} %bitcast.136), channel_id=1, source_target_pairs={{1,0},{2,1},{3,2},{5,4},{6,5},{7,6},{9,8},{10,9},{11,10},{13,12},{... | collective-permute-start | bytes 6193160 | tf_op jit(solution)/shard_map/ppermute | solution.py:453
  90.8 63.6 %all-to-all-start.2 = ((bf16[8,26,96,128]{3,2,1,0:T(8,128)(2,1)}), bf16[8,26,96,128]{3,2,1,0:T(8,128)(2,1)}, u32[]{:S(2)}, u32[]{:S(2)}) async-start(bf16[8,26,96,128]{3,2,1,0:T(8,128)(2,1)} %pad_maximum_fusion), calls=%async_computation.2 | async-start | bytes 10223616 | tf_op jit(solution)/shard_map/all_to_all | solution.py:444
  95.5 49.4 %collective-permute-start.7 = (bf16[48,168,128]{2,1,0:T(8,128)(2,1)}, bf16[48,168,128]{2,1,0:T(8,128)(2,1)}, u32[]{:S(2)}, u32[]{:S(2)}) collective-permute-start(bf16[48,168,128]{2,1,0:T(8,128)(2,1)} %collective-permute-done.3.refs_1_), channel_id=1, source_target_pairs={{1,0},{2,1},{5,4},{6,5},{9,8},{10,9},{13,12},{14,13},{17,16},{18,1... | collective-permute-start | bytes 6193160 | tf_op jit(solution)/shard_map/ppermute | solution.py:453
  108.7 7.8 %copy-start.15 = (bf16[72,72,128]{2,1,0:T(8,128)(2,1)}, bf16[72,72,128]{2,1,0:T(8,128)(2,1)S(1)}, u32[]{:S(2)}) copy-start(bf16[72,72,128]{2,1,0:T(8,128)(2,1)S(1)} %get-tuple-element.63) | copy-start | bytes 3981316
  108.7 7.8 %copy-start.19 = (bf16[72,72,128]{2,1,0:T(8,128)(2,1)}, bf16[72,72,128]{2,1,0:T(8,128)(2,1)S(1)}, u32[]{:S(2)}) copy-start(bf16[72,72,128]{2,1,0:T(8,128)(2,1)S(1)} %get-tuple-element.70) | copy-start | bytes 3981316
  111.8 34.3 %copy-start.40 = (bf16[72,96,128]{2,1,0:T(8,128)(2,1)S(1)}, bf16[72,96,128]{2,1,0:T(8,128)(2,1)}, u32[]{:S(2)}) copy-start(bf16[72,96,128]{2,1,0:T(8,128)(2,1)} %get-tuple-element.59) | copy-start | bytes 5308420
  111.8 34.3 %collective-permute-start.8 = (bf16[72,96,128]{2,0,1:T(8,128)(2,1)S(1)}, bf16[72,96,128]{2,0,1:T(8,128)(2,1)S(1)}, u32[]{:S(2)}, u32[]{:S(2)}) collective-permute-start(bf16[72,96,128]{2,0,1:T(8,128)(2,1)S(1)} %copy.121), channel_id=1, source_target_pairs={{3,2},{7,6},{11,10},{15,14},{19,18},{23,22},{27,26},{31,30}} | collective-permute-start | bytes 5308424 | tf_op jit(solution)/shard_map/ppermute | solution.py:453
  116.5 54.2 %copy-start.55 = (pred[672]{0:T(1024)(128)(4,1)}, pred[672]{0:T(1024)(128)(4,1)S(1)}, u32[]{:S(2)}) copy-start(pred[672]{0:T(1024)(128)(4,1)S(1)} %get-tuple-element.129) | copy-start | bytes 2020
  116.5 54.2 %copy-start.57 = (pred[672]{0:T(1024)(128)(4,1)}, pred[672]{0:T(1024)(128)(4,1)S(1)}, u32[]{:S(2)}) copy-start(pred[672]{0:T(1024)(128)(4,1)S(1)} %get-tuple-element.130) | copy-start | bytes 2020
  116.5 54.1 %copy-start.51 = (s32[672]{0:T(1024)}, s32[672]{0:T(1024)S(1)}, u32[]{:S(2)}) copy-start(s32[672]{0:T(1024)S(1)} %get-tuple-element.141) | copy-start | bytes 8068
  116.5 54.1 %copy-start.53 = (s32[672]{0:T(1024)}, s32[672]{0:T(1024)S(1)}, u32[]{:S(2)}) copy-start(s32[672]{0:T(1024)S(1)} %get-tuple-element.142) | copy-start | bytes 8068
  144.9 60.9 %collective-permute-start.9 = (bf16[48,168,128]{2,1,0:T(8,128)(2,1)}, bf16[48,168,128]{2,1,0:T(8,128)(2,1)}, u32[]{:S(2)}, u32[]{:S(2)}) collective-permute-start(bf16[48,168,128]{2,1,0:T(8,128)(2,1)} %collective-permute-done.7.refs_2_), channel_id=1, source_target_pairs={{1,0},{5,4},{9,8},{13,12},{17,16},{21,20},{25,24},{29,28}} | collective-permute-start | bytes 6193160 | tf_op jit(solution)/shard_map/ppermute | solution.py:453
  148.2 57.6 %collective-permute-start.10 = (bf16[72,96,128]{2,0,1:T(8,128)(2,1)}, bf16[72,96,128]{2,0,1:T(8,128)(2,1)}, u32[]{:S(2)}, u32[]{:S(2)}) collective-permute-start(bf16[72,96,128]{2,0,1:T(8,128)(2,1)} %add_convert_fusion.1), channel_id=1, source_target_pairs={{2,1},{3,2},{6,5},{7,6},{10,9},{11,10},{14,13},{15,14},{18,17},{19... | collective-permute-start | bytes 5308424 | tf_op jit(solution)/shard_map/ppermute | solution.py:453
  159.3 36.7 %all-to-all-start.3 = ((bf16[8,6,168,128]{3,2,1,0:T(8,128)(2,1)}), bf16[8,6,168,128]{3,2,1,0:T(8,128)(2,1)}, u32[]{:S(2)}, u32[]{:S(2)}) async-start(bf16[8,6,168,128]{3,2,1,0:T(8,128)(2,1)} %pack.9), calls=%async_computation.3 | async-start | bytes 4128768 | tf_op jit(solution)/shard_map/all_to_all | solution.py:444
  196.0 49.5 %collective-permute-start.11 = (bf16[48,168,128]{2,1,0:T(8,128)(2,1)}, bf16[48,168,128]{2,1,0:T(8,128)(2,1)}, u32[]{:S(2)}, u32[]{:S(2)}) collective-permute-start(bf16[48,168,128]{2,1,0:T(8,128)(2,1)} %bitcast.12.refs_0_), channel_id=1, source_target_pairs={{1,0},{2,1},{3,2},{5,4},{6,5},{7,6},{9,8},{10,9},{11,10},{13,12},{... | collective-permute-start | bytes 6193160 | tf_op jit(solution)/shard_map/ppermute | solution.py:453
  205.8 49.6 %all-to-all-start.4 = ((bf16[8,21,72,128]{3,2,1,0:T(8,128)(2,1)}), bf16[8,21,72,128]{3,2,1,0:T(8,128)(2,1)}, u32[]{:S(2)}, u32[]{:S(2)}) async-start(bf16[8,21,72,128]{3,2,1,0:T(8,128)(2,1)} %copy-done.2), calls=%async_computation.4 | async-start | bytes 6193152 | tf_op jit(solution)/shard_map/all_to_all | solution.py:444
  210.3 43.3 %collective-permute-start.4 = (bf16[72,96,128]{2,1,0:T(8,128)(2,1)}, bf16[72,96,128]{2,1,0:T(8,128)(2,1)}, u32[]{:S(2)}, u32[]{:S(2)}) collective-permute-start(bf16[72,96,128]{2,1,0:T(8,128)(2,1)} %bitcast.118), channel_id=1, source_target_pairs={{0,1},{1,2},{2,3},{4,5},{5,6},{6,7},{8,9},{9,10},{10,11},{12,13},{... | collective-permute-start | bytes 5308424 | tf_op jit(solution)/shard_map/ppermute | solution.py:453
  217.6 37.8 %collective-permute-start.12 = (bf16[72,72,128]{2,0,1:T(8,128)(2,1)S(1)}, bf16[72,72,128]{2,0,1:T(8,128)(2,1)}, u32[]{:S(2)}, u32[]{:S(2)}) collective-permute-start(bf16[72,72,128]{2,0,1:T(8,128)(2,1)S(1)} %copy.123), channel_id=1, source_target_pairs={{3,2},{7,6},{11,10},{15,14},{19,18},{23,22},{27,26},{31,30}} | collective-permute-start | bytes 3981320 | tf_op jit(solution)/shard_map/ppermute | solution.py:453
  245.5 54.9 %collective-permute-start.18 = (bf16[48,168,128]{2,1,0:T(8,128)(2,1)}, bf16[48,168,128]{2,1,0:T(8,128)(2,1)}, u32[]{:S(2)}, u32[]{:S(2)}) collective-permute-start(bf16[48,168,128]{2,1,0:T(8,128)(2,1)} %collective-permute-done.11.refs_1_), channel_id=1, source_target_pairs={{1,0},{2,1},{5,4},{6,5},{9,8},{10,9},{13,12},{14,13},{17,16},{18,1... | collective-permute-start | bytes 6193160 | tf_op jit(solution)/shard_map/ppermute | solution.py:453
  253.5 48.1 %collective-permute-start.5 = (bf16[72,96,128]{2,1,0:T(8,128)(2,1)}, bf16[72,96,128]{2,1,0:T(8,128)(2,1)}, u32[]{:S(2)}, u32[]{:S(2)}) collective-permute-start(bf16[72,96,128]{2,1,0:T(8,128)(2,1)} %collective-permute-done.4.refs_1_), channel_id=1, source_target_pairs={{1,2},{2,3},{5,6},{6,7},{9,10},{10,11},{13,14},{14,15},{17,18},{18... | collective-permute-start | bytes 5308424 | tf_op jit(solution)/shard_map/ppermute | solution.py:453
  269.6 16.1 %copy-start.20 = (bf16[72,72,128]{2,1,0:T(8,128)(2,1)S(1)}, bf16[72,72,128]{2,1,0:T(8,128)(2,1)}, u32[]{:S(2)}) copy-start(bf16[72,72,128]{2,1,0:T(8,128)(2,1)} %copy-done.19) | copy-start | bytes 3981316
  269.8 18.3 %copy-start.14 = (bf16[72,96,128]{2,1,0:T(8,128)(2,1)S(1)}, bf16[72,96,128]{2,1,0:T(8,128)(2,1)}, u32[]{:S(2)}) copy-start(bf16[72,96,128]{2,1,0:T(8,128)(2,1)} %copy-done.13) | copy-start | bytes 5308420
  269.8 42.7 %collective-permute-start.13 = (bf16[72,72,128]{2,1,0:T(8,128)(2,1)S(1)}, bf16[72,72,128]{2,1,0:T(8,128)(2,1)}, u32[]{:S(2)}, u32[]{:S(2)}) collective-permute-start(bf16[72,72,128]{2,1,0:T(8,128)(2,1)S(1)} %bitcast.120), channel_id=1, source_target_pairs={{0,1},{1,2},{2,3},{4,5},{5,6},{6,7},{8,9},{9,10},{10,11},{12,13},{... | collective-permute-start | bytes 3981320 | tf_op jit(solution)/shard_map/ppermute | solution.py:453
  287.3 42.7 %collective-permute-start.17 = (bf16[72,72,128]{2,0,1:T(8,128)(2,1)S(1)}, bf16[72,72,128]{2,0,1:T(8,128)(2,1)S(1)}, u32[]{:S(2)}, u32[]{:S(2)}) collective-permute-start(bf16[72,72,128]{2,0,1:T(8,128)(2,1)S(1)} %add_convert_fusion.3), channel_id=1, source_target_pairs={{2,1},{3,2},{6,5},{7,6},{10,9},{11,10},{14,13},{15,14},{18,17},{19... | collective-permute-start | bytes 3981320 | tf_op jit(solution)/shard_map/ppermute | solution.py:453
  290.3 39.7 %copy-start.18 = (bf16[72,72,128]{2,1,0:T(8,128)(2,1)S(1)}, bf16[72,72,128]{2,1,0:T(8,128)(2,1)}, u32[]{:S(2)}) copy-start(bf16[72,72,128]{2,1,0:T(8,128)(2,1)} %copy-done.17) | copy-start | bytes 3981316
  290.5 42.4 %copy-start.38 = (f32[72,96,128]{2,1,0:T(8,128)S(1)}, f32[72,96,128]{2,1,0:T(8,128)}, u32[]{:S(2)}) copy-start(f32[72,96,128]{2,1,0:T(8,128)} %get-tuple-element.84) | copy-start | bytes 10616836
  300.4 28.3 %collective-permute-start.20 = (bf16[72,48,128]{2,0,1:T(8,128)(2,1)S(1)}, bf16[72,48,128]{2,0,1:T(8,128)(2,1)S(1)}, u32[]{:S(2)}, u32[]{:S(2)}) collective-permute-start(bf16[72,48,128]{2,0,1:T(8,128)(2,1)S(1)} %get-tuple-element.78), channel_id=1, source_target_pairs={{1,0},{2,1},{3,2},{5,4},{6,5},{7,6},{9,8},{10,9},{11,10},{13,12},{... | collective-permute-start | bytes 2654216 | tf_op jit(solution)/shard_map/ppermute | solution.py:453
  301.7 67.0 %collective-permute-start.6 = (bf16[72,96,128]{2,1,0:T(8,128)(2,1)}, bf16[72,96,128]{2,1,0:T(8,128)(2,1)S(1)}, u32[]{:S(2)}, u32[]{:S(2)}) collective-permute-start(bf16[72,96,128]{2,1,0:T(8,128)(2,1)} %collective-permute-done.5.refs_1_), channel_id=1, source_target_pairs={{2,3},{6,7},{10,11},{14,15},{18,19},{22,23},{26,27},{30,31}} | collective-permute-start | bytes 5308424 | tf_op jit(solution)/shard_map/ppermute | solution.py:453
  302.5 92.1 %collective-permute-start.19 = (bf16[48,168,128]{2,1,0:T(8,128)(2,1)}, bf16[48,168,128]{2,1,0:T(8,128)(2,1)}, u32[]{:S(2)}, u32[]{:S(2)}) collective-permute-start(bf16[48,168,128]{2,1,0:T(8,128)(2,1)} %collective-permute-done.18.refs_2_), channel_id=1, source_target_pairs={{1,0},{5,4},{9,8},{13,12},{17,16},{21,20},{25,24},{29,28}} | collective-permute-start | bytes 6193160 | tf_op jit(solution)/shard_map/ppermute | solution.py:453
  312.5 49.0 %collective-permute-start.14 = (bf16[72,72,128]{2,1,0:T(8,128)(2,1)}, bf16[72,72,128]{2,1,0:T(8,128)(2,1)S(1)}, u32[]{:S(2)}, u32[]{:S(2)}) collective-permute-start(bf16[72,72,128]{2,1,0:T(8,128)(2,1)} %collective-permute-done.13.refs_2_), channel_id=1, source_target_pairs={{1,2},{2,3},{5,6},{6,7},{9,10},{10,11},{13,14},{14,15},{17,18},{18... | collective-permute-start | bytes 3981320 | tf_op jit(solution)/shard_map/ppermute | solution.py:453
  328.7 63.3 %collective-permute-start.22 = (bf16[72,48,128]{2,0,1:T(8,128)(2,1)S(1)}, bf16[72,48,128]{2,0,1:T(8,128)(2,1)}, u32[]{:S(2)}, u32[]{:S(2)}) collective-permute-start(bf16[72,48,128]{2,0,1:T(8,128)(2,1)S(1)} %get-tuple-element.83), channel_id=1, source_target_pairs={{1,0},{2,1},{3,2},{5,4},{6,5},{7,6},{9,8},{10,9},{11,10},{13,12},{... | collective-permute-start | bytes 2654216 | tf_op jit(solution)/shard_map/ppermute | solution.py:453
  331.3 87.9 %collective-permute-start.21 = (bf16[72,72,128]{2,0,1:T(8,128)(2,1)}, bf16[72,72,128]{2,0,1:T(8,128)(2,1)S(1)}, u32[]{:S(2)}, u32[]{:S(2)}) collective-permute-start(bf16[72,72,128]{2,0,1:T(8,128)(2,1)} %add_convert_fusion.2), channel_id=1, source_target_pairs={{1,0},{2,1},{3,2},{5,4},{6,5},{7,6},{9,8},{10,9},{11,10},{13,12},{... | collective-permute-start | bytes 3981320 | tf_op jit(solution)/shard_map/ppermute | solution.py:453
  352.4 7.9 %copy-start.33 = (f32[168,168]{1,0:T(8,128)}, f32[168,168]{1,0:T(8,128)S(1)}, u32[]{:S(2)}) copy-start(f32[168,168]{1,0:T(8,128)S(1)} %pairs.6) | copy-start | bytes 338692
  361.5 30.5 %copy-start.44 = (bf16[72,48,128]{2,0,1:T(8,128)(2,1)S(1)}, bf16[72,48,128]{2,0,1:T(8,128)(2,1)}, u32[]{:S(2)}) copy-start(bf16[72,48,128]{2,0,1:T(8,128)(2,1)} %copy-done.43) | copy-start | bytes 2654212
  368.6 25.9 %copy-start.35 = (f32[168,168]{1,0:T(8,128)}, f32[168,168]{1,0:T(8,128)S(1)}, u32[]{:S(2)}) copy-start(f32[168,168]{1,0:T(8,128)S(1)} %pairs.7) | copy-start | bytes 338692
  368.7 25.9 %copy-start.11 = (bf16[72,96,128]{2,1,0:T(8,128)(2,1)}, bf16[72,96,128]{2,1,0:T(8,128)(2,1)S(1)}, u32[]{:S(2)}) copy-start(bf16[72,96,128]{2,1,0:T(8,128)(2,1)S(1)} %collective-permute-done.6.refs_1_) | copy-start | bytes 5308420
  419.2 7.8 %copy-start.41 = (bf16[72,72,128]{2,0,1:T(8,128)(2,1)}, bf16[72,72,128]{2,0,1:T(8,128)(2,1)S(1)}, u32[]{:S(2)}) copy-start(bf16[72,72,128]{2,0,1:T(8,128)(2,1)S(1)} %collective-permute-done.21) | copy-start | bytes 3981316
  427.0 30.8 %all-to-all-start.5 = ((bf16[8,21,48,128]{3,2,1,0:T(8,128)(2,1)}), bf16[8,21,48,128]{3,2,1,0:T(8,128)(2,1)}, u32[]{:S(2)}, u32[]{:S(2)}) async-start(bf16[8,21,48,128]{3,2,1,0:T(8,128)(2,1)} %bitcast.134), calls=%async_computation.5 | async-start | bytes 4128768 | tf_op jit(solution)/shard_map/all_to_all | solution.py:444
  431.5 10.6 %collective-permute-start.23 = (f32[168,168]{1,0:T(8,128)S(1)}, f32[168,168]{1,0:T(8,128)S(1)}, u32[]{:S(2)}, u32[]{:S(2)}) collective-permute-start(f32[168,168]{1,0:T(8,128)S(1)} %copy-done.34), channel_id=1, source_target_pairs={{1,0},{2,1},{3,2},{5,4},{6,5},{7,6},{9,8},{10,9},{11,10},{13,12},{... | collective-permute-start | bytes 338696 | tf_op jit(solution)/shard_map/ppermute | solution.py:453
  432.8 15.0 %collective-permute-start.24 = (f32[168,168]{1,0:T(8,128)S(1)}, f32[168,168]{1,0:T(8,128)S(1)}, u32[]{:S(2)}, u32[]{:S(2)}) collective-permute-start(f32[168,168]{1,0:T(8,128)S(1)} %copy-done.36), channel_id=1, source_target_pairs={{2,0},{3,1},{6,4},{7,5},{10,8},{11,9},{14,12},{15,13},{18,16},{19,... | collective-permute-start | bytes 338696 | tf_op jit(solution)/shard_map/ppermute | solution.py:453
  435.7 12.1 %copy-start.8 = (bf16[48,48,128]{2,1,0:T(8,128)(2,1)S(1)}, bf16[48,48,128]{2,1,0:T(8,128)(2,1)}, u32[]{:S(2)}) copy-start(bf16[48,48,128]{2,1,0:T(8,128)(2,1)} %get-tuple-element.110.refs_1_) | copy-start | bytes 1769476
  442.1 11.9 %copy-start.46 = (f32[168,168]{1,0:T(8,128)}, f32[168,168]{1,0:T(8,128)S(1)}, u32[]{:S(2)}) copy-start(f32[168,168]{1,0:T(8,128)S(1)} %collective-permute-done.23) | copy-start | bytes 338692
  457.8 31.0 %all-to-all-start.6 = ((bf16[8,21,48,128]{3,2,1,0:T(8,128)(2,1)}), bf16[8,21,48,128]{3,2,1,0:T(8,128)(2,1)}, u32[]{:S(2)}, u32[]{:S(2)}) async-start(bf16[8,21,48,128]{3,2,1,0:T(8,128)(2,1)} %bitcast.135), calls=%async_computation.6 | async-start | bytes 4128768 | tf_op jit(solution)/shard_map/all_to_all | solution.py:444
  488.8 42.0 %all-to-all-start.7 = ((bf16[8,21,72,128]{3,2,1,0:T(8,128)(2,1)}), bf16[8,21,72,128]{3,2,1,0:T(8,128)(2,1)}, u32[]{:S(2)}, u32[]{:S(2)}) async-start(bf16[8,21,72,128]{3,2,1,0:T(8,128)(2,1)} %bitcast.132), calls=%async_computation.7 | async-start | bytes 6193152 | tf_op jit(solution)/shard_map/all_to_all | solution.py:444
  493.4 27.0 %collective-permute-start.15 = (bf16[72,72,128]{2,1,0:T(8,128)(2,1)}, bf16[72,72,128]{2,1,0:T(8,128)(2,1)S(1)}, u32[]{:S(2)}, u32[]{:S(2)}) collective-permute-start(bf16[72,72,128]{2,1,0:T(8,128)(2,1)} %copy-done.16), channel_id=1, source_target_pairs={{2,3},{6,7},{10,11},{14,15},{18,19},{22,23},{26,27},{30,31}} | collective-permute-start | bytes 3981320 | tf_op jit(solution)/shard_map/ppermute | solution.py:453
  494.2 8.1 %copy-start.52 = (s32[672]{0:T(1024)S(1)}, s32[672]{0:T(1024)}, u32[]{:S(2)}) copy-start(s32[672]{0:T(1024)} %copy-done.51) | copy-start | bytes 8068
  494.2 8.1 %copy-start.54 = (s32[672]{0:T(1024)S(1)}, s32[672]{0:T(1024)}, u32[]{:S(2)}) copy-start(s32[672]{0:T(1024)} %copy-done.53) | copy-start | bytes 8068
  494.2 8.1 %copy-start.56 = (pred[672]{0:T(1024)(128)(4,1)S(1)}, pred[672]{0:T(1024)(128)(4,1)}, u32[]{:S(2)}) copy-start(pred[672]{0:T(1024)(128)(4,1)} %copy-done.55) | copy-start | bytes 2020
  494.2 8.1 %copy-start.58 = (pred[672]{0:T(1024)(128)(4,1)S(1)}, pred[672]{0:T(1024)(128)(4,1)}, u32[]{:S(2)}) copy-start(pred[672]{0:T(1024)(128)(4,1)} %copy-done.57) | copy-start | bytes 2020
  520.4 15.8 %copy-start.12 = (bf16[72,96,128]{2,1,0:T(8,128)(2,1)S(1)}, bf16[72,96,128]{2,1,0:T(8,128)(2,1)}, u32[]{:S(2)}) copy-start(bf16[72,96,128]{2,1,0:T(8,128)(2,1)} %copy-done.11) | copy-start | bytes 5308420
  531.9 25.3 %all-to-all-start.8 = ((bf16[8,84,672]{2,1,0:T(8,128)(2,1)}), bf16[8,84,672]{2,1,0:T(8,128)(2,1)}, u32[]{:S(2)}, u32[]{:S(2)}) async-start(bf16[8,84,672]{2,1,0:T(8,128)(2,1)} %copy.150), calls=%async_computation.8 | async-start | bytes 2162688 | tf_op jit(solution)/shard_map/all_to_all | solution.py:444
  544.0 10.6 %collective-permute-start.16 = (f32[168,168]{1,0:T(8,128)S(1)}, f32[168,168]{1,0:T(8,128)S(1)}, u32[]{:S(2)}, u32[]{:S(2)}) collective-permute-start(f32[168,168]{1,0:T(8,128)S(1)} %pairs.4), channel_id=1, source_target_pairs={{3,0},{7,4},{11,8},{15,12},{19,16},{23,20},{27,24},{31,28}} | collective-permute-start | bytes 338696 | tf_op jit(solution)/shard_map/ppermute | solution.py:453
  546.5 8.1 %copy-start.47 = (f32[168,168]{1,0:T(8,128)S(1)}, f32[168,168]{1,0:T(8,128)}, u32[]{:S(2)}) copy-start(f32[168,168]{1,0:T(8,128)} %copy-done.46) | copy-start | bytes 338692
  546.5 8.1 %copy-start.49 = (f32[168,168]{1,0:T(8,128)S(1)}, f32[168,168]{1,0:T(8,128)}, u32[]{:S(2)}) copy-start(f32[168,168]{1,0:T(8,128)} %copy-done.48) | copy-start | bytes 338692
  557.2 15.6 %all-to-all-start.9 = ((f32[8,84,168]{1,2,0:T(8,128)}), f32[8,84,168]{1,2,0:T(8,128)S(1)}, u32[]{:S(2)}, u32[]{:S(2)}) async-start(f32[8,84,168]{1,2,0:T(8,128)} %copy.157), calls=%async_computation.9 | async-start | bytes 1376256 | tf_op jit(solution)/shard_map/all_to_all | solution.py:444
  564.0 8.9 %collective-permute-start.25 = (f32[84,168]{0,1:T(8,128)S(1)}, f32[84,168]{0,1:T(8,128)S(1)}, u32[]{:S(2)}, u32[]{:S(2)}) collective-permute-start(f32[84,168]{0,1:T(8,128)S(1)} %bitcast.149), channel_id=1, source_target_pairs={{0,1},{1,2},{2,3},{3,0},{4,5},{5,6},{6,7},{7,4},{8,9},{9,10},{10,1... | collective-permute-start | bytes 169352 | tf_op jit(solution)/shard_map/ppermute | solution.py:453
  564.2 11.3 %collective-permute-start.26 = (f32[84,168]{0,1:T(8,128)S(1)}, f32[84,168]{0,1:T(8,128)S(1)}, u32[]{:S(2)}, u32[]{:S(2)}) collective-permute-start(f32[84,168]{0,1:T(8,128)S(1)} %bitcast.150), channel_id=1, source_target_pairs={{0,2},{1,3},{2,0},{3,1},{4,6},{5,7},{6,4},{7,5},{8,10},{9,11},{10,... | collective-permute-start | bytes 169352 | tf_op jit(solution)/shard_map/ppermute | solution.py:453
  569.4 6.3 %collective-permute-start.27 = (f32[84,168]{0,1:T(8,128)S(1)}, f32[84,168]{0,1:T(8,128)S(1)}, u32[]{:S(2)}, u32[]{:S(2)}) collective-permute-start(f32[84,168]{0,1:T(8,128)S(1)} %bitcast.151), channel_id=1, source_target_pairs={{0,3},{1,0},{2,1},{3,2},{4,7},{5,4},{6,5},{7,6},{8,11},{9,8},{10,9... | collective-permute-start | bytes 169352 | tf_op jit(solution)/shard_map/ppermute | solution.py:453
  (33 other events, 97.2 us)

commit v3 on v2

--- a/solution.py
+++ b/solution.py
@@ -587,36 +587,37 @@
         grad, w_y = finish(parts, left_t, fold)
         one = match(w_y, y_last if q else y_first, (lo - cuts[q][0]) // (2 * fold), one)
         grad = turn(grad).reshape(rows, tiles, hi - lo, LANES)
+        if n == 2:
+            grad = after(grad, ups_last[last])
         moved.append(exchange(after(grad, *moved[-1:])))
 
+    where = [(lo, hi, half if q == 0 else unit) for q, lo, hi in bits]
+    span_col = order_one // cols
     one = dot(one.astype(BF16), pick_latent).astype(BF16)
-    one = one.reshape(fold, rows * tiles, order_one)
-    one = jnp.concatenate(
+    one = jnp.transpose(one.reshape(order_one, cols, span_col), (1, 0, 2))
+    total = lax.dynamic_index_in_dim(one, place, 0, keepdims=False).astype(F32)
+    grad_latent = unpack(moved[0], swap, latent.shape, where[0], None)
+    for d in range(1, cols):
+        ring = [(c, (c + d) % cols) for c in range(cols)]
+        mine = move(lax.dynamic_index_in_dim(one, (place + d) % cols, 0, keepdims=False), ring)
+        if d == 1:
+            mine, grad_latent = lax.optimization_barrier((mine, grad_latent))
+        total = total + mine.astype(F32)
+    total = total.reshape(fold, rows * tiles, span_col)
+    total = jnp.concatenate(
         [
-            one[:, rows * lo : rows * hi].reshape(fold, rows, hi - lo, order_one)
+            total[:, rows * lo : rows * hi].reshape(fold, rows, hi - lo, span_col)
             for lo, hi in groups
         ],
         axis=2,
     )
-    one = jnp.transpose(one, (1, 2, 0, 3)).reshape(rows, span_one, order_one)
-    where = [(lo, hi, half if q == 0 else unit) for q, lo, hi in bits]
-    grad_latent = unpack(moved[0], swap, latent.shape, where[0], None)
-    grad_latent = unpack(moved[1], swap, latent.shape, where[1], grad_latent)
-    one, grad_latent = lax.optimization_barrier((one, grad_latent))
-    one = exchange(after(one, moved[2], ups_last[last]))
-    grad_latent = unpack(moved[2], swap, latent.shape, where[2], grad_latent)
-    one = one.astype(F32).sum(0)
-    one = jnp.transpose(one.reshape(span_one, cols, order_one // cols), (1, 0, 2))
-    total = lax.dynamic_index_in_dim(one, place, 0, keepdims=False)
-    for d in range(1, cols):
-        ring = [(c, (c + d) % cols) for c in range(cols)]
-        mine = lax.dynamic_index_in_dim(one, (place + d) % cols, 0, keepdims=False)
-        total = total + move(mine, ring)
-    grad_one = keep_lower(total, depth)
-    sent[-1], grad_latent = lax.optimization_barrier((sent[-1], grad_latent))
-    two = second_factor(met, sent, grad_near)
-    two = exchange(after(two, one)).sum(0)
-    grad_two = keep_lower(two, depth)
+    total = jnp.transpose(total, (1, 2, 0, 3)).reshape(rows, span_one, span_col)
+    total = jnp.concatenate([total, second_factor(met, sent, grad_near)], axis=2)
+    total = exchange(after(total, moved[2])).sum(0)
+    grad_one = keep_lower(total[:, :span_col], depth)
+    grad_two = keep_lower(total[:, span_col:], depth)
+    for n in (1, 2):
+        grad_latent = unpack(moved[n], swap, latent.shape, where[n], grad_latent)
     return (grad_latent, grad_one, grad_two)
 
 

time: 588 us -> 588 us (level)
  starting transfers between devices: 101 us -> 107 us
    all_to_all x10 -> x9, waiting for transfers between devices: 34.8 us -> 21 us  [exchange(): return lax.all_to_all(value, 'row', split_axis=0, concat_axis=0, tiled=True)]
    ppermute x28, waiting for transfers between devices: 180 us -> 190 us  [move(): return lax.ppermute(value, 'col', pairs_of)]
    ppermute x28, starting transfers between devices: 55.9 us -> 63.8 us  [move(): return lax.ppermute(value, 'col', pairs_of)]
    all_to_all x10 -> x9, starting transfers between devices: 45.5 us -> 43.4 us  [exchange(): return lax.all_to_all(value, 'row', split_axis=0, concat_axis=0, tiled=True)]
    unnamed x123 -> x124, local copies, waits for them, and re-layouts: 20.4 us -> 20.7 us
  transfers between devices with their start and end apart: 38 -> 37, of which waited for: 19 -> 19; matrix products, arithmetic and copies ran while one was open for 12% -> 12% of each run, Pallas kernels for 27% -> 27%
where the time goes in v3:
time: 588 us; the launch traced here: 577 us
  waiting for transfers between devices  211 us (36%)
  Pallas kernels  164 us (28%)
  starting transfers between devices  107 us (18%)
  local copies, waits for them, and re-layouts  62.7 us (11%)
  other arithmetic  22.8 us (4%)
  matrix products  7.21 us (1%)
    ppermute x28, waiting for transfers between devices, move(): return lax.ppermute(value, 'col', pairs_of)  190 us
    ppermute x28, starting transfers between devices, move(): return lax.ppermute(value, 'col', pairs_of)  63.8 us
    all_to_all x9, starting transfers between devices, exchange(): return lax.all_to_all(value, 'row', split_axis=0, concat_axis=0, tiled=True)  43.4 us
    pallas_call x4, Pallas kernels, pairs(): pl.pallas_call(kernel, grid=(tiles // per,), in_specs=[spec(span_two)] +...  26.9 us
    pallas_call x5, Pallas kernels, pack(): pl.pallas_call(kernel, grid=(count // per,), in_specs=[pl.BlockSpec((per...  25.4 us
    pallas_call x2, Pallas kernels, raise_field(): pl.pallas_call(kernel, grid=(count,), in_specs=[pl.BlockSpec((step,) + fi...  23.6 us
    pallas_call x3, Pallas kernels, unpack(): pl.pallas_call(kernel, grid=(tiles // per,), in_specs=[pl.BlockSpec((rows...  23.2 us
    pallas_call x3, Pallas kernels, finish(): pl.pallas_call(kernel, grid=(count,), in_specs=[pl.BlockSpec((step,) + p....  21.5 us
  transfers between devices with their start and end apart: 37, of which 19 were waited for; matrix products, arithmetic and copies ran while one was open for 12% of the time, Pallas kernels for 27%

profile of v3, /device:TPU:0, one launch (start us, length us, event | category | flops | bytes accessed | tf_op | source)
XLA Modules:
  0.0 577.3 jit_solution(394912153136230151)
XLA Ops:
  1.7 3.7 pack.5
  5.4 5.3 all-to-all-start
  15.1 4.1 pack.6
  20.8 2.8 collective-permute-done.1
  23.6 13.3 %all-to-all-done = bf16[8,6,168,128]{3,2,1,0:T(8,128)(2,1)S(1)} async-done(((bf16[8,6,168,128]{3,2,1,0:T(8,128)(2,1)}), bf16[8,6,168,128]{3,2,1,0:T(8,128)(2,1)S(1)}, u32[]{:S(2)}, u32[]{:S(2)}) %all-to-all-start) | async-done | bytes 2064416 | tf_op jit(solution)/shard_map/all_to_all | solution.py:444
  37.0 4.5 all-to-all-start.1
  42.9 7.0 %pack.7 = bf16[8,21,96,128]{3,2,1,0:T(8,128)(2,1)S(1)} custom-call(bf16[84,168,256]{2,1,0:T(8,128)(2,1)} %x_ref.8, bf16[512,512]{1,0:T(8,128)(2,1)S(1)} %fusion.63.p_ref), custom_call_target="tpu_custom_call" | custom-call | flops 1 | bytes 1 | tf_op jit(solution)/shard_map/pack/pallas_call | solution.py:138
  49.9 2.0 copy-done
  52.3 4.9 pad_maximum_fusion
  57.2 33.6 %collective-permute-done.3.refs_1_ = bf16[48,168,128]{2,1,0:T(8,128)(2,1)} collective-permute-done((bf16[48,168,128]{2,1,0:T(8,128)(2,1)S(1)}, bf16[48,168,128]{2,1,0:T(8,128)(2,1)}, u32[]{:S(2)}, u32[]{:S(2)}) %collective-permute-start.3) | collective-permute-done | bytes 2064416 | tf_op jit(solution)/shard_map/ppermute | solution.py:453
  90.8 4.6 all-to-all-start.2
  97.0 9.3 %shares.1 = (f32[72,96,128]{2,1,0:T(8,128)}, f32[72,72,128]{2,1,0:T(8,128)}, bf16[72,96,128]{2,1,0:T(8,128)(2,1)S(1)}, bf16[72,72,128]{2,1,0:T(8,128)(2,1)S(1)},...) custom-call(bf16[72,168,128]{2,1,0:T(8,128)(2,1)} %bitcast.6.c_ref.r, ...), custom_call_target="tpu_custom_call" | custom-call | flops 1 | bytes 1 | tf_op jit(solution)/shard_map/shares/pallas_call | solution.py:406
  108.6 3.1 copy.116
  112.7 3.7 pack.9
  116.5 28.3 %collective-permute-done.4.refs_2_ = bf16[48,168,128]{2,1,0:T(8,128)(2,1)} collective-permute-done((bf16[48,168,128]{2,1,0:T(8,128)(2,1)}, bf16[48,168,128]{2,1,0:T(8,128)(2,1)}, u32[]{:S(2)}, u32[]{:S(2)}) %collective-permute-start.4) | collective-permute-done | bytes 2064416 | tf_op jit(solution)/shard_map/ppermute | solution.py:453
  148.1 2.0 collective-permute-start.7
  150.1 4.2 all-to-all-done.2
  154.4 2.9 slice.111
  157.2 3.6 copy.178
  164.0 4.4 all-to-all-start.3
  168.3 3.7 fusion.52.clone.5
  174.8 13.3 %raise_field.2 = (bf16[12,672,256]{2,1,0:T(8,128)(2,1)}, bf16[96,48,128]{2,1,0:T(8,128)(2,1)S(1)}, bf16[96,48,128]{2,1,0:T(8,128)(2,1)S(1)}, bf16[96,72,128]{2,1,0:T(8,128)(2,1)S(1)}) custom-call(bf16[96,168,128]{2,1,0:T(8,128)(2,1)} %bitcast.126, bf16[672,672]{1,0:T(8,128)(2,1)S(1)} %copy.114.l_ref), custom_call_target="tpu_custom_call" | custom-call | flops 1 | bytes 1 | tf_op jit(solution)/shard_map/raise_field/pallas_call | solution.py:230
  191.7 2.9 all-to-all-done.3
  195.9 6.9 %pack.8 = bf16[8,21,72,128]{3,2,1,0:T(8,128)(2,1)S(1)} custom-call(bf16[84,168,256]{2,1,0:T(8,128)(2,1)} %x_ref.8, bf16[512,512]{1,0:T(8,128)(2,1)S(1)} %fusion.63.p_ref), custom_call_target="tpu_custom_call" | custom-call | flops 1 | bytes 1 | tf_op jit(solution)/shard_map/pack/pallas_call | solution.py:138
  204.5 4.4 all-to-all-start.4
  208.9 5.8 collective-permute-start.10
  217.9 23.2 %collective-permute-done.8.refs_1_ = bf16[48,168,128]{2,1,0:T(8,128)(2,1)} collective-permute-done((bf16[48,168,128]{2,1,0:T(8,128)(2,1)}, bf16[48,168,128]{2,1,0:T(8,128)(2,1)}, u32[]{:S(2)}, u32[]{:S(2)}) %collective-permute-start.8) | collective-permute-done | bytes 2064416 | tf_op jit(solution)/shard_map/ppermute | solution.py:453
  242.4 9.8 %collective-permute-done.10.refs_1_ = bf16[72,96,128]{2,1,0:T(8,128)(2,1)} collective-permute-done((bf16[72,96,128]{2,1,0:T(8,128)(2,1)}, bf16[72,96,128]{2,1,0:T(8,128)(2,1)}, u32[]{:S(2)}, u32[]{:S(2)}) %collective-permute-start.10) | collective-permute-done | bytes 1769504 | tf_op jit(solution)/shard_map/ppermute | solution.py:453
  254.1 3.9 copy.179
  258.0 10.3 %raise_field.3 = (bf16[9,672,256]{2,1,0:T(8,128)(2,1)}, bf16[72,48,128]{2,1,0:T(8,128)(2,1)S(1)}, bf16[72,48,128]{2,1,0:T(8,128)(2,1)S(1)}, bf16[72,72,128]{2,1,0:T(8,128)(2,1)S(1)}) custom-call(bf16[72,168,128]{2,1,0:T(8,128)(2,1)} %bitcast.129, bf16[672,672]{1,0:T(8,128)(2,1)S(1)} %copy.114.l_ref), custom_call_target="tpu_custom_call" | custom-call | flops 1 | bytes 1 | tf_op jit(solution)/shard_map/raise_field/pallas_call | solution.py:230
  269.5 14.8 %collective-permute-start.11 = (bf16[72,72,128]{2,1,0:T(8,128)(2,1)S(1)}, bf16[72,72,128]{2,1,0:T(8,128)(2,1)S(1)}, u32[]{:S(2)}, u32[]{:S(2)}) collective-permute-start(bf16[72,72,128]{2,1,0:T(8,128)(2,1)S(1)} %bitcast.116), channel_id=1, source_target_pairs={{0,1},{1,2},{2,3},{4,5},{5,6},{6,7},{8,9},{9,10},{10,11},{12,13},{... | collective-permute-start | bytes 3981320 | tf_op jit(solution)/shard_map/ppermute | solution.py:453
  286.7 2.2 add_convert_fusion
  289.0 4.0 collective-permute-done.16.refs_2_
  296.6 15.4 %collective-permute-done.11.refs_2_ = bf16[72,72,128]{2,1,0:T(8,128)(2,1)S(1)} collective-permute-done((bf16[72,72,128]{2,1,0:T(8,128)(2,1)S(1)}, bf16[72,72,128]{2,1,0:T(8,128)(2,1)S(1)}, u32[]{:S(2)}, u32[]{:S(2)}) %collective-permute-start.11) | collective-permute-done | bytes 1327136 | tf_op jit(solution)/shard_map/ppermute | solution.py:453
  312.8 12.7 %collective-permute-done.18 = bf16[72,48,128]{2,0,1:T(8,128)(2,1)S(1)} collective-permute-done((bf16[72,48,128]{2,0,1:T(8,128)(2,1)S(1)}, bf16[72,48,128]{2,0,1:T(8,128)(2,1)S(1)}, u32[]{:S(2)}, u32[]{:S(2)}) %collective-permute-start.18) | collective-permute-done | bytes 884768 | tf_op jit(solution)/shard_map/ppermute | solution.py:453
  329.4 3.8 copy.134
  335.1 6.4 %pairs.4 = f32[168,168]{1,0:T(8,128)S(1)} custom-call(bf16[72,168,128]{2,1,0:T(8,128)(2,1)} %bitcast.6.c_ref.refs_0_, bf16[72,96,128]{2,1,0:T(8,128)(2,1)S(1)} %bitcast.115, bf16[72,72,128]{2,1,0:T(8,128)(2,1)S(1)} %bitcast.117), custom_call_target="tpu_custom_call" | custom-call | flops 1 | bytes 1 | tf_op jit(solution)/shard_map/pairs/pallas_call | solution.py:372
  342.0 6.6 %pairs.5 = f32[168,168]{1,0:T(8,128)S(1)} custom-call(bf16[72,168,128]{2,1,0:T(8,128)(2,1)} %bitcast.6.c_ref.refs_0_, bf16[72,96,128]{2,1,0:T(8,128)(2,1)} %collective-permute-done.10.refs_1_, bf16[72,72,128]{2,1,0:T(8,128)(2,1)S(1)} %collective-permute-done.11.refs_2_), custom_call_target="tpu_custom_call" | custom-call | flops 1 | bytes 1 | tf_op jit(solution)/shard_map/pairs/pallas_call | solution.py:372
  348.7 7.9 %gathered.2 = (bf16[48,96,128]{2,1,0:T(8,128)(2,1)S(1)}, bf16[48,72,128]{2,1,0:T(8,128)(2,1)S(1)}, f32[4,168,168]{2,1,0:T(8,128)S(1)}) custom-call(bf16[48,168,128]{2,1,0:T(8,128)(2,1)} %bitcast.133, bf16[48,168,128]{2,1,0:T(8,128)(2,1)} %collective-permute-done.3.refs_1_, bf16[48,168,128]{2,1,0:T(8,128)(2,1)} %collective-permute-done.4.refs_2_, ...), custom_call_target="tpu_custom_call" | custom-call | flops 1 | bytes 1 | tf_op jit(solution)/shard_map/gathered/pallas_call | solution.py:342
  357.8 7.1 %pairs.6 = f32[168,168]{1,0:T(8,128)S(1)} custom-call(bf16[72,168,128]{2,1,0:T(8,128)(2,1)} %bitcast.6.c_ref.refs_0_, bf16[72,96,128]{2,1,0:T(8,128)(2,1)} %collective-permute-done.13.refs_1_, bf16[72,72,128]{2,1,0:T(8,128)(2,1)S(1)} %collective-permute-done.14.refs_2_), custom_call_target="tpu_custom_call" | custom-call | flops 1 | bytes 1 | tf_op jit(solution)/shard_map/pairs/pallas_call | solution.py:372
  365.0 23.8 %collective-permute-done.20 = bf16[72,48,128]{2,0,1:T(8,128)(2,1)} collective-permute-done((bf16[72,48,128]{2,0,1:T(8,128)(2,1)S(1)}, bf16[72,48,128]{2,0,1:T(8,128)(2,1)}, u32[]{:S(2)}, u32[]{:S(2)}) %collective-permute-start.20) | collective-permute-done | bytes 884768 | tf_op jit(solution)/shard_map/ppermute | solution.py:453
  388.8 2.6 fusion.104
  391.4 7.8 %gathered.3 = (bf16[48,96,128]{2,1,0:T(8,128)(2,1)S(1)}, bf16[48,72,128]{2,1,0:T(8,128)(2,1)S(1)}, f32[4,168,168]{2,1,0:T(8,128)S(1)}) custom-call(bf16[48,168,128]{2,1,0:T(8,128)(2,1)} %bitcast.12.refs_0_, bf16[48,168,128]{2,1,0:T(8,128)(2,1)} %collective-permute-done.8.refs_1_, bf16[48,168,128]{2,1,0:T(8,128)(2,1)} %collective-permute-done.16.refs_2_, ...), custom_call_target="tpu_custom_call" | custom-call | flops 1 | bytes 1 | tf_op jit(solution)/shard_map/gathered/pallas_call | solution.py:342
  400.6 12.3 %collective-permute-done.19 = bf16[72,72,128]{2,0,1:T(8,128)(2,1)} collective-permute-done((bf16[72,72,128]{2,0,1:T(8,128)(2,1)}, bf16[72,72,128]{2,0,1:T(8,128)(2,1)}, u32[]{:S(2)}, u32[]{:S(2)}) %collective-permute-start.19) | collective-permute-done | bytes 1327136 | tf_op jit(solution)/shard_map/ppermute | solution.py:453
  413.0 6.2 %finish.3 = (bf16[48,168,128]{2,1,0:T(8,128)(2,1)S(1)}, bf16[6,672,256]{2,1,0:T(8,128)(2,1)}) custom-call(bf16[48,48,128]{2,1,0:T(8,128)(2,1)S(1)} %get-tuple-element.112.refs_0_, bf16[48,48,128]{2,1,0:T(8,128)(2,1)S(1)} %get-tuple-element.110.refs_1_, bf16[48,72,128]{2,1,0:T(8,128)(2,1)S(1)} %get-tuple-element.84.refs_2_, bf16[672,672]{1,0:T(8,128)(2,1)S(1)} %bitcast.111), custom_call_target="tpu_custom_call" | custom-call | flops 1 | bytes 1 | tf_op jit(solution)/shard_map/finish/pallas_call | solution.py:260
  420.7 7.3 %all-to-all-start.5 = ((bf16[8,21,48,128]{3,2,1,0:T(8,128)(2,1)}), bf16[8,21,48,128]{3,2,1,0:T(8,128)(2,1)}, u32[]{:S(2)}, u32[]{:S(2)}) async-start(bf16[8,21,48,128]{3,2,1,0:T(8,128)(2,1)} %bitcast.131), calls=%async_computation.5 | async-start | bytes 4128768 | tf_op jit(solution)/shard_map/all_to_all | solution.py:444
  432.2 5.1 match.3.rest_0_
  438.6 7.5 %collective-permute-done.22 = f32[168,168]{1,0:T(8,128)S(1)} collective-permute-done((f32[168,168]{1,0:T(8,128)S(1)}, f32[168,168]{1,0:T(8,128)S(1)}, u32[]{:S(2)}, u32[]{:S(2)}) %collective-permute-start.22) | collective-permute-done | bytes 112928 | tf_op jit(solution)/shard_map/ppermute | solution.py:453
  446.2 6.2 %finish.4 = (bf16[48,168,128]{2,1,0:T(8,128)(2,1)S(1)}, bf16[6,672,256]{2,1,0:T(8,128)(2,1)}) custom-call(bf16[48,48,128]{2,1,0:T(8,128)(2,1)S(1)} %get-tuple-element.113.refs_0_, bf16[48,48,128]{2,1,0:T(8,128)(2,1)S(1)} %copy-done.8, bf16[48,72,128]{2,1,0:T(8,128)(2,1)S(1)} %get-tuple-element.87.refs_2_, bf16[672,672]{1,0:T(8,128)(2,1)S(1)} %bitcast.112), custom_call_target="tpu_custom_call" | custom-call | flops 1 | bytes 1 | tf_op jit(solution)/shard_map/finish/pallas_call | solution.py:260
  454.4 4.5 all-to-all-start.6
  464.2 5.2 match.4.rest_0_
  469.5 2.6 fusion.53.refs_2_
  472.1 9.1 %finish.5 = (bf16[72,168,128]{2,1,0:T(8,128)(2,1)}, bf16[9,672,256]{2,1,0:T(8,128)(2,1)}) custom-call(bf16[72,48,128]{2,1,0:T(8,128)(2,1)S(1)} %bitcast.121, bf16[72,48,128]{2,1,0:T(8,128)(2,1)S(1)} %bitcast.122, bf16[72,72,128]{2,1,0:T(8,128)(2,1)S(1)} %fusion.53.refs_2_, bf16[672,672]{1,0:T(8,128)(2,1)S(1)} %bitcast.113), custom_call_target="tpu_custom_call" | custom-call | flops 1 | bytes 1 | tf_op jit(solution)/shard_map/finish/pallas_call | solution.py:260
  481.2 3.9 copy.138
  486.2 4.6 all-to-all-start.7
  492.6 8.0 %match.5 = f32[672,672]{1,0:T(8,128)S(1)} custom-call(bf16[9,672,256]{2,1,0:T(8,128)(2,1)} %get-tuple-element.96.w_ref, bf16[9,672,256]{2,1,0:T(8,128)(2,1)} %get-tuple-element.97.z_ref, f32[672,672]{1,0:T(8,128)S(1)} %copy-done.4), custom_call_target="tpu_custom_call" | custom-call | flops 1 | bytes 1 | tf_op jit(solution)/shard_map/match/pallas_call | solution.py:290
  502.5 6.7 %pairs.7 = f32[168,168]{1,0:T(8,128)S(1)} custom-call(bf16[72,168,128]{2,1,0:T(8,128)(2,1)} %bitcast.6.c_ref.refs_0_, bf16[72,96,128]{2,1,0:T(8,128)(2,1)S(1)} %copy-done.12, bf16[72,72,128]{2,1,0:T(8,128)(2,1)S(1)} %copy-done.21), custom_call_target="tpu_custom_call" | custom-call | flops 1 | bytes 1 | tf_op jit(solution)/shard_map/pairs/pallas_call | solution.py:372
  511.2 13.0 %collective-permute-start.26 = (bf16[672,168]{0,1:T(8,128)(2,1)S(1)}, bf16[672,168]{0,1:T(8,128)(2,1)}, u32[]{:S(2)}, u32[]{:S(2)}) collective-permute-start(bf16[672,168]{0,1:T(8,128)(2,1)S(1)} %get-tuple-element.115), channel_id=1, source_target_pairs={{0,3},{1,0},{2,1},{3,2},{4,7},{5,4},{6,5},{7,6},{8,11},{9,8},{10,9... | collective-permute-start | bytes 677384 | tf_op jit(solution)/shard_map/ppermute | solution.py:453
  524.8 4.0 collective-permute-done.27
  530.2 7.6 %unpack.3.rest_0_ = bf16[84,168,256]{2,1,0:T(8,128)(2,1)} custom-call(bf16[8,21,48,128]{3,2,1,0:T(8,128)(2,1)} %all-to-all-done.5.x_ref, bf16[512,512]{1,0:T(8,128)(2,1)S(1)} %fusion.63.p_ref), custom_call_target="tpu_custom_call" | custom-call | flops 1 | bytes 1 | tf_op jit(solution)/shard_map/unpack/pallas_call | solution.py:174
  538.1 12.5 %collective-permute-done.25 = bf16[672,168]{0,1:T(8,128)(2,1)} collective-permute-done((bf16[672,168]{0,1:T(8,128)(2,1)S(1)}, bf16[672,168]{0,1:T(8,128)(2,1)}, u32[]{:S(2)}, u32[]{:S(2)}) %collective-permute-start.25) | collective-permute-done | bytes 225824 | tf_op jit(solution)/shard_map/ppermute | solution.py:453
  555.5 3.9 all-to-all-start.8
  559.4 7.6 %unpack.4.rest_0_ = bf16[84,168,256]{2,1,0:T(8,128)(2,1)} custom-call(bf16[8,21,48,128]{3,2,1,0:T(8,128)(2,1)} %all-to-all-done.6.x_ref, bf16[512,512]{1,0:T(8,128)(2,1)S(1)} %fusion.63.p_ref, bf16[84,168,256]{2,1,0:T(8,128)(2,1)} %unpack.3.rest_0_), custom_call_target="tpu_custom_call", output_to_operand_aliasing={{}: (2, {})} | custom-call | flops 1 | bytes 1 | tf_op jit(solution)/shard_map/unpack/pallas_call | solution.py:174
  567.0 8.0 %unpack.5 = bf16[84,168,256]{2,1,0:T(8,128)(2,1)} custom-call(bf16[8,21,72,128]{3,2,1,0:T(8,128)(2,1)} %all-to-all-done.7.x_ref, bf16[512,512]{1,0:T(8,128)(2,1)S(1)} %fusion.63.p_ref, bf16[84,168,256]{2,1,0:T(8,128)(2,1)} %unpack.4.rest_0_), custom_call_target="tpu_custom_call", output_to_operand_aliasing={{}: (2, {})} | custom-call | flops 1 | bytes 1 | tf_op jit(solution)/shard_map/unpack/pallas_call | solution.py:174
  (231 shorter events, 82.4 us)
Async XLA Ops:
  5.4 31.6 %all-to-all-start = ((bf16[8,6,168,128]{3,2,1,0:T(8,128)(2,1)}), bf16[8,6,168,128]{3,2,1,0:T(8,128)(2,1)S(1)}, u32[]{:S(2)}, u32[]{:S(2)}) async-start(bf16[8,6,168,128]{3,2,1,0:T(8,128)(2,1)} %pack.5), calls=%async_computation | async-start | bytes 4128768 | tf_op jit(solution)/shard_map/all_to_all | solution.py:444
  11.2 9.6 %collective-permute-start.2 = (bf16[168,168]{1,0:T(8,128)(2,1)S(1)}, bf16[168,168]{1,0:T(8,128)(2,1)S(1)}, u32[]{:S(2)}, u32[]{:S(2)}) collective-permute-start(bf16[168,168]{1,0:T(8,128)(2,1)S(1)} %get-tuple-element.124), channel_id=1, source_target_pairs={{3,0},{7,4},{11,8},{15,12},{19,16},{23,20},{27,24},{31,28}} | collective-permute-start | bytes 169352 | tf_op jit(solution)/shard_map/ppermute | solution.py:453
  12.5 11.1 %collective-permute-start.1 = (bf16[168,168]{1,0:T(8,128)(2,1)S(1)}, bf16[168,168]{1,0:T(8,128)(2,1)S(1)}, u32[]{:S(2)}, u32[]{:S(2)}) collective-permute-start(bf16[168,168]{1,0:T(8,128)(2,1)S(1)} %get-tuple-element.125), channel_id=1, source_target_pairs={{2,0},{3,1},{6,4},{7,5},{10,8},{11,9},{14,12},{15,13},{18,16},{19,... | collective-permute-start | bytes 169352 | tf_op jit(solution)/shard_map/ppermute | solution.py:453
  13.8 9.8 %collective-permute-start = (bf16[168,168]{1,0:T(8,128)(2,1)S(1)}, bf16[168,168]{1,0:T(8,128)(2,1)S(1)}, u32[]{:S(2)}, u32[]{:S(2)}) collective-permute-start(bf16[168,168]{1,0:T(8,128)(2,1)S(1)} %get-tuple-element.126), channel_id=1, source_target_pairs={{1,0},{2,1},{3,2},{5,4},{6,5},{7,6},{9,8},{10,9},{11,10},{13,12},{... | collective-permute-start | bytes 169352 | tf_op jit(solution)/shard_map/ppermute | solution.py:453
  37.0 53.8 %all-to-all-start.1 = ((bf16[8,9,168,128]{3,2,1,0:T(8,128)(2,1)}), bf16[8,9,168,128]{3,2,1,0:T(8,128)(2,1)}, u32[]{:S(2)}, u32[]{:S(2)}) async-start(bf16[8,9,168,128]{3,2,1,0:T(8,128)(2,1)} %copy-done.1), calls=%async_computation.1 | async-start | bytes 6193152 | tf_op jit(solution)/shard_map/all_to_all | solution.py:444
  41.4 10.4 %copy-start.51 = (bf16[84,672]{1,0:T(8,128)(2,1)S(1)}, bf16[84,672]{1,0:T(8,128)(2,1)}, u32[]{:S(2)}) copy-start(bf16[84,672]{1,0:T(8,128)(2,1)} %param.6) | copy-start | bytes 338692
  41.4 49.3 %collective-permute-start.3 = (bf16[48,168,128]{2,1,0:T(8,128)(2,1)S(1)}, bf16[48,168,128]{2,1,0:T(8,128)(2,1)}, u32[]{:S(2)}, u32[]{:S(2)}) collective-permute-start(bf16[48,168,128]{2,1,0:T(8,128)(2,1)S(1)} %bitcast.132), channel_id=1, source_target_pairs={{1,0},{2,1},{3,2},{5,4},{6,5},{7,6},{9,8},{10,9},{11,10},{13,12},{... | collective-permute-start | bytes 6193160 | tf_op jit(solution)/shard_map/ppermute | solution.py:453
  90.8 63.6 %all-to-all-start.2 = ((bf16[8,26,96,128]{3,2,1,0:T(8,128)(2,1)}), bf16[8,26,96,128]{3,2,1,0:T(8,128)(2,1)}, u32[]{:S(2)}, u32[]{:S(2)}) async-start(bf16[8,26,96,128]{3,2,1,0:T(8,128)(2,1)} %pad_maximum_fusion), calls=%async_computation.2 | async-start | bytes 10223616 | tf_op jit(solution)/shard_map/all_to_all | solution.py:444
  95.4 49.4 %collective-permute-start.4 = (bf16[48,168,128]{2,1,0:T(8,128)(2,1)}, bf16[48,168,128]{2,1,0:T(8,128)(2,1)}, u32[]{:S(2)}, u32[]{:S(2)}) collective-permute-start(bf16[48,168,128]{2,1,0:T(8,128)(2,1)} %collective-permute-done.3.refs_1_), channel_id=1, source_target_pairs={{1,0},{2,1},{5,4},{6,5},{9,8},{10,9},{13,12},{14,13},{17,16},{18,1... | collective-permute-start | bytes 6193160 | tf_op jit(solution)/shard_map/ppermute | solution.py:453
  108.6 7.8 %copy-start.15 = (bf16[72,72,128]{2,1,0:T(8,128)(2,1)}, bf16[72,72,128]{2,1,0:T(8,128)(2,1)S(1)}, u32[]{:S(2)}) copy-start(bf16[72,72,128]{2,1,0:T(8,128)(2,1)S(1)} %get-tuple-element.62) | copy-start | bytes 3981316
  108.6 7.8 %copy-start.22 = (bf16[72,72,128]{2,1,0:T(8,128)(2,1)}, bf16[72,72,128]{2,1,0:T(8,128)(2,1)S(1)}, u32[]{:S(2)}) copy-start(bf16[72,72,128]{2,1,0:T(8,128)(2,1)S(1)} %get-tuple-element.69) | copy-start | bytes 3981316
  111.8 34.4 %copy-start.42 = (bf16[72,96,128]{2,1,0:T(8,128)(2,1)S(1)}, bf16[72,96,128]{2,1,0:T(8,128)(2,1)}, u32[]{:S(2)}) copy-start(bf16[72,96,128]{2,1,0:T(8,128)(2,1)} %get-tuple-element.58) | copy-start | bytes 5308420
  111.8 34.3 %collective-permute-start.5 = (bf16[72,96,128]{2,0,1:T(8,128)(2,1)S(1)}, bf16[72,96,128]{2,0,1:T(8,128)(2,1)S(1)}, u32[]{:S(2)}, u32[]{:S(2)}) collective-permute-start(bf16[72,96,128]{2,0,1:T(8,128)(2,1)S(1)} %copy.116), channel_id=1, source_target_pairs={{3,2},{7,6},{11,10},{15,14},{19,18},{23,22},{27,26},{31,30}} | collective-permute-start | bytes 5308424 | tf_op jit(solution)/shard_map/ppermute | solution.py:453
  116.4 55.6 %copy-start.56 = (pred[672]{0:T(1024)(128)(4,1)}, pred[672]{0:T(1024)(128)(4,1)S(1)}, u32[]{:S(2)}) copy-start(pred[672]{0:T(1024)(128)(4,1)S(1)} %get-tuple-element.129) | copy-start | bytes 2020
  116.5 55.6 %copy-start.58 = (pred[672]{0:T(1024)(128)(4,1)}, pred[672]{0:T(1024)(128)(4,1)S(1)}, u32[]{:S(2)}) copy-start(pred[672]{0:T(1024)(128)(4,1)S(1)} %get-tuple-element.130) | copy-start | bytes 2020
  116.5 55.6 %copy-start.52 = (s32[672]{0:T(1024)}, s32[672]{0:T(1024)S(1)}, u32[]{:S(2)}) copy-start(s32[672]{0:T(1024)S(1)} %get-tuple-element.141) | copy-start | bytes 8068
  116.5 55.6 %copy-start.54 = (s32[672]{0:T(1024)}, s32[672]{0:T(1024)S(1)}, u32[]{:S(2)}) copy-start(s32[672]{0:T(1024)S(1)} %get-tuple-element.142) | copy-start | bytes 8068
  144.8 59.6 %collective-permute-start.6 = (bf16[48,168,128]{2,1,0:T(8,128)(2,1)}, bf16[48,168,128]{2,1,0:T(8,128)(2,1)}, u32[]{:S(2)}, u32[]{:S(2)}) collective-permute-start(bf16[48,168,128]{2,1,0:T(8,128)(2,1)} %collective-permute-done.4.refs_2_), channel_id=1, source_target_pairs={{1,0},{5,4},{9,8},{13,12},{17,16},{21,20},{25,24},{29,28}} | collective-permute-start | bytes 6193160 | tf_op jit(solution)/shard_map/ppermute | solution.py:453
  148.1 56.4 %collective-permute-start.7 = (bf16[72,96,128]{2,0,1:T(8,128)(2,1)}, bf16[72,96,128]{2,0,1:T(8,128)(2,1)}, u32[]{:S(2)}, u32[]{:S(2)}) collective-permute-start(bf16[72,96,128]{2,0,1:T(8,128)(2,1)} %add_convert_fusion.1), channel_id=1, source_target_pairs={{2,1},{3,2},{6,5},{7,6},{10,9},{11,10},{14,13},{15,14},{18,17},{19... | collective-permute-start | bytes 5308424 | tf_op jit(solution)/shard_map/ppermute | solution.py:453
  164.0 30.7 %all-to-all-start.3 = ((bf16[8,6,168,128]{3,2,1,0:T(8,128)(2,1)}), bf16[8,6,168,128]{3,2,1,0:T(8,128)(2,1)}, u32[]{:S(2)}, u32[]{:S(2)}) async-start(bf16[8,6,168,128]{3,2,1,0:T(8,128)(2,1)} %pack.9), calls=%async_computation.3 | async-start | bytes 4128768 | tf_op jit(solution)/shard_map/all_to_all | solution.py:444
  194.6 46.5 %collective-permute-start.8 = (bf16[48,168,128]{2,1,0:T(8,128)(2,1)}, bf16[48,168,128]{2,1,0:T(8,128)(2,1)}, u32[]{:S(2)}, u32[]{:S(2)}) collective-permute-start(bf16[48,168,128]{2,1,0:T(8,128)(2,1)} %bitcast.12.refs_0_), channel_id=1, source_target_pairs={{1,0},{2,1},{3,2},{5,4},{6,5},{7,6},{9,8},{10,9},{11,10},{13,12},{... | collective-permute-start | bytes 6193160 | tf_op jit(solution)/shard_map/ppermute | solution.py:453
  204.5 49.6 %all-to-all-start.4 = ((bf16[8,21,72,128]{3,2,1,0:T(8,128)(2,1)}), bf16[8,21,72,128]{3,2,1,0:T(8,128)(2,1)}, u32[]{:S(2)}, u32[]{:S(2)}) async-start(bf16[8,21,72,128]{3,2,1,0:T(8,128)(2,1)} %copy-done.2), calls=%async_computation.4 | async-start | bytes 6193152 | tf_op jit(solution)/shard_map/all_to_all | solution.py:444
  208.9 43.3 %collective-permute-start.10 = (bf16[72,96,128]{2,1,0:T(8,128)(2,1)}, bf16[72,96,128]{2,1,0:T(8,128)(2,1)}, u32[]{:S(2)}, u32[]{:S(2)}) collective-permute-start(bf16[72,96,128]{2,1,0:T(8,128)(2,1)} %bitcast.114), channel_id=1, source_target_pairs={{0,1},{1,2},{2,3},{4,5},{5,6},{6,7},{8,9},{9,10},{10,11},{12,13},{... | collective-permute-start | bytes 5308424 | tf_op jit(solution)/shard_map/ppermute | solution.py:453
  216.2 37.9 %collective-permute-start.9 = (bf16[72,72,128]{2,0,1:T(8,128)(2,1)S(1)}, bf16[72,72,128]{2,0,1:T(8,128)(2,1)}, u32[]{:S(2)}, u32[]{:S(2)}) collective-permute-start(bf16[72,72,128]{2,0,1:T(8,128)(2,1)S(1)} %copy.118), channel_id=1, source_target_pairs={{3,2},{7,6},{11,10},{15,14},{19,18},{23,22},{27,26},{31,30}} | collective-permute-start | bytes 3981320 | tf_op jit(solution)/shard_map/ppermute | solution.py:453
  241.1 51.9 %collective-permute-start.16 = (bf16[48,168,128]{2,1,0:T(8,128)(2,1)}, bf16[48,168,128]{2,1,0:T(8,128)(2,1)}, u32[]{:S(2)}, u32[]{:S(2)}) collective-permute-start(bf16[48,168,128]{2,1,0:T(8,128)(2,1)} %collective-permute-done.8.refs_1_), channel_id=1, source_target_pairs={{1,0},{2,1},{5,4},{6,5},{9,8},{10,9},{13,12},{14,13},{17,16},{18,1... | collective-permute-start | bytes 6193160 | tf_op jit(solution)/shard_map/ppermute | solution.py:453
  252.2 42.2 %collective-permute-start.13 = (bf16[72,96,128]{2,1,0:T(8,128)(2,1)}, bf16[72,96,128]{2,1,0:T(8,128)(2,1)}, u32[]{:S(2)}, u32[]{:S(2)}) collective-permute-start(bf16[72,96,128]{2,1,0:T(8,128)(2,1)} %collective-permute-done.10.refs_1_), channel_id=1, source_target_pairs={{1,2},{2,3},{5,6},{6,7},{9,10},{10,11},{13,14},{14,15},{17,18},{18... | collective-permute-start | bytes 5308424 | tf_op jit(solution)/shard_map/ppermute | solution.py:453
  269.3 15.0 %copy-start.23 = (bf16[72,72,128]{2,1,0:T(8,128)(2,1)S(1)}, bf16[72,72,128]{2,1,0:T(8,128)(2,1)}, u32[]{:S(2)}) copy-start(bf16[72,72,128]{2,1,0:T(8,128)(2,1)} %copy-done.22) | copy-start | bytes 3981316
  269.5 17.2 %copy-start.14 = (bf16[72,96,128]{2,1,0:T(8,128)(2,1)S(1)}, bf16[72,96,128]{2,1,0:T(8,128)(2,1)}, u32[]{:S(2)}) copy-start(bf16[72,96,128]{2,1,0:T(8,128)(2,1)} %copy-done.13) | copy-start | bytes 5308420
  269.5 42.5 %collective-permute-start.11 = (bf16[72,72,128]{2,1,0:T(8,128)(2,1)S(1)}, bf16[72,72,128]{2,1,0:T(8,128)(2,1)S(1)}, u32[]{:S(2)}, u32[]{:S(2)}) collective-permute-start(bf16[72,72,128]{2,1,0:T(8,128)(2,1)S(1)} %bitcast.116), channel_id=1, source_target_pairs={{0,1},{1,2},{2,3},{4,5},{5,6},{6,7},{8,9},{9,10},{10,11},{12,13},{... | collective-permute-start | bytes 3981320 | tf_op jit(solution)/shard_map/ppermute | solution.py:453
  285.9 40.9 %collective-permute-start.12 = (bf16[72,72,128]{2,0,1:T(8,128)(2,1)S(1)}, bf16[72,72,128]{2,0,1:T(8,128)(2,1)S(1)}, u32[]{:S(2)}, u32[]{:S(2)}) collective-permute-start(bf16[72,72,128]{2,0,1:T(8,128)(2,1)S(1)} %add_convert_fusion.3), channel_id=1, source_target_pairs={{2,1},{3,2},{6,5},{7,6},{10,9},{11,10},{14,13},{15,14},{18,17},{19... | collective-permute-start | bytes 3981320 | tf_op jit(solution)/shard_map/ppermute | solution.py:453
  288.9 37.9 %copy-start.17 = (bf16[72,72,128]{2,1,0:T(8,128)(2,1)S(1)}, bf16[72,72,128]{2,1,0:T(8,128)(2,1)}, u32[]{:S(2)}) copy-start(bf16[72,72,128]{2,1,0:T(8,128)(2,1)} %copy-done.16) | copy-start | bytes 3981316
  289.0 40.4 %copy-start.40 = (f32[72,96,128]{2,1,0:T(8,128)S(1)}, f32[72,96,128]{2,1,0:T(8,128)}, u32[]{:S(2)}) copy-start(f32[72,96,128]{2,1,0:T(8,128)} %get-tuple-element.83) | copy-start | bytes 10616836
  293.0 32.4 %collective-permute-start.18 = (bf16[72,48,128]{2,0,1:T(8,128)(2,1)S(1)}, bf16[72,48,128]{2,0,1:T(8,128)(2,1)S(1)}, u32[]{:S(2)}, u32[]{:S(2)}) collective-permute-start(bf16[72,48,128]{2,0,1:T(8,128)(2,1)S(1)} %get-tuple-element.77), channel_id=1, source_target_pairs={{1,0},{2,1},{3,2},{5,4},{6,5},{7,6},{9,8},{10,9},{11,10},{13,12},{... | collective-permute-start | bytes 2654216 | tf_op jit(solution)/shard_map/ppermute | solution.py:453
  294.3 70.6 %collective-permute-start.15 = (bf16[72,96,128]{2,1,0:T(8,128)(2,1)}, bf16[72,96,128]{2,1,0:T(8,128)(2,1)S(1)}, u32[]{:S(2)}, u32[]{:S(2)}) collective-permute-start(bf16[72,96,128]{2,1,0:T(8,128)(2,1)} %collective-permute-done.13.refs_1_), channel_id=1, source_target_pairs={{2,3},{6,7},{10,11},{14,15},{18,19},{22,23},{26,27},{30,31}} | collective-permute-start | bytes 5308424 | tf_op jit(solution)/shard_map/ppermute | solution.py:453
  295.3 96.0 %collective-permute-start.17 = (bf16[48,168,128]{2,1,0:T(8,128)(2,1)}, bf16[48,168,128]{2,1,0:T(8,128)(2,1)}, u32[]{:S(2)}, u32[]{:S(2)}) collective-permute-start(bf16[48,168,128]{2,1,0:T(8,128)(2,1)} %collective-permute-done.16.refs_2_), channel_id=1, source_target_pairs={{1,0},{5,4},{9,8},{13,12},{17,16},{21,20},{25,24},{29,28}} | collective-permute-start | bytes 6193160 | tf_op jit(solution)/shard_map/ppermute | solution.py:453
  312.0 45.8 %collective-permute-start.14 = (bf16[72,72,128]{2,1,0:T(8,128)(2,1)S(1)}, bf16[72,72,128]{2,1,0:T(8,128)(2,1)S(1)}, u32[]{:S(2)}, u32[]{:S(2)}) collective-permute-start(bf16[72,72,128]{2,1,0:T(8,128)(2,1)S(1)} %collective-permute-done.11.refs_2_), channel_id=1, source_target_pairs={{1,2},{2,3},{5,6},{6,7},{9,10},{10,11},{13,14},{14,15},{17,18},{18... | collective-permute-start | bytes 3981320 | tf_op jit(solution)/shard_map/ppermute | solution.py:453
  325.5 63.3 %collective-permute-start.20 = (bf16[72,48,128]{2,0,1:T(8,128)(2,1)S(1)}, bf16[72,48,128]{2,0,1:T(8,128)(2,1)}, u32[]{:S(2)}, u32[]{:S(2)}) collective-permute-start(bf16[72,48,128]{2,0,1:T(8,128)(2,1)S(1)} %get-tuple-element.82), channel_id=1, source_target_pairs={{1,0},{2,1},{3,2},{5,4},{6,5},{7,6},{9,8},{10,9},{11,10},{13,12},{... | collective-permute-start | bytes 2654216 | tf_op jit(solution)/shard_map/ppermute | solution.py:453
  328.1 84.8 %collective-permute-start.19 = (bf16[72,72,128]{2,0,1:T(8,128)(2,1)}, bf16[72,72,128]{2,0,1:T(8,128)(2,1)}, u32[]{:S(2)}, u32[]{:S(2)}) collective-permute-start(bf16[72,72,128]{2,0,1:T(8,128)(2,1)} %add_convert_fusion.2), channel_id=1, source_target_pairs={{1,0},{2,1},{3,2},{5,4},{6,5},{7,6},{9,8},{10,9},{11,10},{13,12},{... | collective-permute-start | bytes 3981320 | tf_op jit(solution)/shard_map/ppermute | solution.py:453
  348.7 7.9 %copy-start.35 = (f32[168,168]{1,0:T(8,128)}, f32[168,168]{1,0:T(8,128)S(1)}, u32[]{:S(2)}) copy-start(f32[168,168]{1,0:T(8,128)S(1)} %pairs.5) | copy-start | bytes 338692
  357.8 31.0 %copy-start.45 = (bf16[72,48,128]{2,0,1:T(8,128)(2,1)S(1)}, bf16[72,48,128]{2,0,1:T(8,128)(2,1)}, u32[]{:S(2)}) copy-start(bf16[72,48,128]{2,0,1:T(8,128)(2,1)} %copy-done.44) | copy-start | bytes 2654212
  364.9 26.4 %copy-start.37 = (f32[168,168]{1,0:T(8,128)}, f32[168,168]{1,0:T(8,128)S(1)}, u32[]{:S(2)}) copy-start(f32[168,168]{1,0:T(8,128)S(1)} %pairs.6) | copy-start | bytes 338692
  365.0 26.4 %copy-start.11 = (bf16[72,96,128]{2,1,0:T(8,128)(2,1)}, bf16[72,96,128]{2,1,0:T(8,128)(2,1)S(1)}, u32[]{:S(2)}) copy-start(bf16[72,96,128]{2,1,0:T(8,128)(2,1)S(1)} %collective-permute-done.15.refs_1_) | copy-start | bytes 5308420
  420.7 7.3 %copy-start.36 = (f32[168,168]{1,0:T(8,128)S(1)}, f32[168,168]{1,0:T(8,128)}, u32[]{:S(2)}) copy-start(f32[168,168]{1,0:T(8,128)} %copy-done.35) | copy-start | bytes 338692
  420.7 8.6 %copy-start.38 = (f32[168,168]{1,0:T(8,128)S(1)}, f32[168,168]{1,0:T(8,128)}, u32[]{:S(2)}) copy-start(f32[168,168]{1,0:T(8,128)} %copy-done.37) | copy-start | bytes 338692
  420.7 33.7 %all-to-all-start.5 = ((bf16[8,21,48,128]{3,2,1,0:T(8,128)(2,1)}), bf16[8,21,48,128]{3,2,1,0:T(8,128)(2,1)}, u32[]{:S(2)}, u32[]{:S(2)}) async-start(bf16[8,21,48,128]{3,2,1,0:T(8,128)(2,1)} %bitcast.131), calls=%async_computation.5 | async-start | bytes 4128768 | tf_op jit(solution)/shard_map/all_to_all | solution.py:444
  428.0 10.6 %collective-permute-start.21 = (f32[168,168]{1,0:T(8,128)S(1)}, f32[168,168]{1,0:T(8,128)S(1)}, u32[]{:S(2)}, u32[]{:S(2)}) collective-permute-start(f32[168,168]{1,0:T(8,128)S(1)} %copy-done.36), channel_id=1, source_target_pairs={{1,0},{2,1},{3,2},{5,4},{6,5},{7,6},{9,8},{10,9},{11,10},{13,12},{... | collective-permute-start | bytes 338696 | tf_op jit(solution)/shard_map/ppermute | solution.py:453
  429.3 16.8 %collective-permute-start.22 = (f32[168,168]{1,0:T(8,128)S(1)}, f32[168,168]{1,0:T(8,128)S(1)}, u32[]{:S(2)}, u32[]{:S(2)}) collective-permute-start(f32[168,168]{1,0:T(8,128)S(1)} %copy-done.38), channel_id=1, source_target_pairs={{2,0},{3,1},{6,4},{7,5},{10,8},{11,9},{14,12},{15,13},{18,16},{19,... | collective-permute-start | bytes 338696 | tf_op jit(solution)/shard_map/ppermute | solution.py:453
  432.2 13.9 %copy-start.8 = (bf16[48,48,128]{2,1,0:T(8,128)(2,1)S(1)}, bf16[48,48,128]{2,1,0:T(8,128)(2,1)}, u32[]{:S(2)}) copy-start(bf16[48,48,128]{2,1,0:T(8,128)(2,1)} %get-tuple-element.111.refs_1_) | copy-start | bytes 1769476
  438.6 13.7 %copy-start.47 = (f32[168,168]{1,0:T(8,128)}, f32[168,168]{1,0:T(8,128)S(1)}, u32[]{:S(2)}) copy-start(f32[168,168]{1,0:T(8,128)S(1)} %collective-permute-done.21) | copy-start | bytes 338692
  454.4 31.8 %all-to-all-start.6 = ((bf16[8,21,48,128]{3,2,1,0:T(8,128)(2,1)}), bf16[8,21,48,128]{3,2,1,0:T(8,128)(2,1)}, u32[]{:S(2)}, u32[]{:S(2)}) async-start(bf16[8,21,48,128]{3,2,1,0:T(8,128)(2,1)} %bitcast.130), calls=%async_computation.6 | async-start | bytes 4128768 | tf_op jit(solution)/shard_map/all_to_all | solution.py:444
  458.9 26.2 %collective-permute-start.23 = (bf16[72,72,128]{2,1,0:T(8,128)(2,1)S(1)}, bf16[72,72,128]{2,1,0:T(8,128)(2,1)S(1)}, u32[]{:S(2)}, u32[]{:S(2)}) collective-permute-start(bf16[72,72,128]{2,1,0:T(8,128)(2,1)S(1)} %copy-done.19), channel_id=1, source_target_pairs={{2,3},{6,7},{10,11},{14,15},{18,19},{22,23},{26,27},{30,31}} | collective-permute-start | bytes 3981320 | tf_op jit(solution)/shard_map/ppermute | solution.py:453
  486.2 68.1 %all-to-all-start.7 = ((bf16[8,21,72,128]{3,2,1,0:T(8,128)(2,1)}), bf16[8,21,72,128]{3,2,1,0:T(8,128)(2,1)}, u32[]{:S(2)}, u32[]{:S(2)}) async-start(bf16[8,21,72,128]{3,2,1,0:T(8,128)(2,1)} %bitcast.128), calls=%async_computation.7 | async-start | bytes 6193152 | tf_op jit(solution)/shard_map/all_to_all | solution.py:444
  492.6 8.0 %copy-start.53 = (s32[672]{0:T(1024)S(1)}, s32[672]{0:T(1024)}, u32[]{:S(2)}) copy-start(s32[672]{0:T(1024)} %copy-done.52) | copy-start | bytes 8068
  492.6 8.0 %copy-start.55 = (s32[672]{0:T(1024)S(1)}, s32[672]{0:T(1024)}, u32[]{:S(2)}) copy-start(s32[672]{0:T(1024)} %copy-done.54) | copy-start | bytes 8068
  492.6 8.0 %copy-start.57 = (pred[672]{0:T(1024)(128)(4,1)S(1)}, pred[672]{0:T(1024)(128)(4,1)}, u32[]{:S(2)}) copy-start(pred[672]{0:T(1024)(128)(4,1)} %copy-done.56) | copy-start | bytes 2020
  492.6 8.0 %copy-start.59 = (pred[672]{0:T(1024)(128)(4,1)S(1)}, pred[672]{0:T(1024)(128)(4,1)}, u32[]{:S(2)}) copy-start(pred[672]{0:T(1024)(128)(4,1)} %copy-done.58) | copy-start | bytes 2020
  502.5 8.0 %copy-start.43 = (bf16[672,672]{0,1:T(8,128)(2,1)}, bf16[672,672]{0,1:T(8,128)(2,1)S(1)}, u32[]{:S(2)}) copy-start(bf16[672,672]{0,1:T(8,128)(2,1)S(1)} %convolution_convert_fusion) | copy-start | bytes 2709508
  502.5 26.4 %copy-start.48 = (f32[168,168]{1,0:T(8,128)S(1)}, f32[168,168]{1,0:T(8,128)}, u32[]{:S(2)}) copy-start(f32[168,168]{1,0:T(8,128)} %copy-done.47) | copy-start | bytes 338692
  502.5 26.4 %copy-start.50 = (f32[168,168]{1,0:T(8,128)S(1)}, f32[168,168]{1,0:T(8,128)}, u32[]{:S(2)}) copy-start(f32[168,168]{1,0:T(8,128)} %copy-done.49) | copy-start | bytes 338692
  509.1 19.7 %collective-permute-start.27 = (f32[168,168]{1,0:T(8,128)S(1)}, f32[168,168]{1,0:T(8,128)S(1)}, u32[]{:S(2)}, u32[]{:S(2)}) collective-permute-start(f32[168,168]{1,0:T(8,128)S(1)} %pairs.7), channel_id=1, source_target_pairs={{3,0},{7,4},{11,8},{15,12},{19,16},{23,20},{27,24},{31,28}} | collective-permute-start | bytes 338696 | tf_op jit(solution)/shard_map/ppermute | solution.py:453
  511.2 26.5 %collective-permute-start.24 = (bf16[672,168]{0,1:T(8,128)(2,1)}, bf16[672,168]{0,1:T(8,128)(2,1)}, u32[]{:S(2)}, u32[]{:S(2)}) collective-permute-start(bf16[672,168]{0,1:T(8,128)(2,1)} %get-tuple-element.116), channel_id=1, source_target_pairs={{0,1},{1,2},{2,3},{3,0},{4,5},{5,6},{6,7},{7,4},{8,9},{9,10},{10,1... | collective-permute-start | bytes 677384 | tf_op jit(solution)/shard_map/ppermute | solution.py:453
  511.2 26.9 %collective-permute-start.26 = (bf16[672,168]{0,1:T(8,128)(2,1)S(1)}, bf16[672,168]{0,1:T(8,128)(2,1)}, u32[]{:S(2)}, u32[]{:S(2)}) collective-permute-start(bf16[672,168]{0,1:T(8,128)(2,1)S(1)} %get-tuple-element.115), channel_id=1, source_target_pairs={{0,3},{1,0},{2,1},{3,2},{4,7},{5,4},{6,5},{7,6},{8,11},{9,8},{10,9... | collective-permute-start | bytes 677384 | tf_op jit(solution)/shard_map/ppermute | solution.py:453
  524.3 26.3 %collective-permute-start.25 = (bf16[672,168]{0,1:T(8,128)(2,1)S(1)}, bf16[672,168]{0,1:T(8,128)(2,1)}, u32[]{:S(2)}, u32[]{:S(2)}) collective-permute-start(bf16[672,168]{0,1:T(8,128)(2,1)S(1)} %get-tuple-element.114), channel_id=1, source_target_pairs={{0,2},{1,3},{2,0},{3,1},{4,6},{5,7},{6,4},{7,5},{8,10},{9,11},{10,... | collective-permute-start | bytes 677384 | tf_op jit(solution)/shard_map/ppermute | solution.py:453
  555.5 19.7 %all-to-all-start.8 = ((f32[8,84,336]{2,1,0:T(8,128)}), f32[8,84,336]{2,1,0:T(8,128)S(1)}, u32[]{:S(2)}, u32[]{:S(2)}) async-start(f32[8,84,336]{2,1,0:T(8,128)} %copy.147), calls=%async_computation.8 | async-start | bytes 2162688 | tf_op jit(solution)/shard_map/all_to_all | solution.py:444
  (33 other events, 84.8 us)
